TPU v7x, 128 devices: a whole 4x4x4 slice. The times are simulated.
128 devices in a mesh: cluster: 8 (over z_hi, y), cone: 16 (over z_lo, x, core).
Axes of the slice: x: 4, y: 4, z: 4 (z_hi: 2, z_lo: 2; z = z_hi * 2 + z_lo), core: 2. Of those that a mesh axis runs over, the one named last changes fastest.
Arguments:
- upper_coef: bfloat16 [256, 32, 128, 128], P('cluster', 'cone'), may hold values from -6 to 6
- phase: float32 [256, 32, 8], P('cluster', 'cone'), may hold values from -3.140625 to 3.140625
- cone_used: int32 [256, 32], P('cluster', 'cone'), may hold values 0 or 1
- transfer: bfloat16 [32, 8, 128, 128], P('cone'), may hold values from -0.5 to 0.5
- leaf_basis: bfloat16 [2048, 2, 256, 128], P(('cluster', 'cone')), may hold values from -0.09375 to 0.09375
- charges: bfloat16 [2048, 256, 256], P(('cluster', 'cone')), may hold values from -6 to 6
- neighbours: int32 [2048, 4], P(('cluster', 'cone')), may hold values from 0 to 2047, as said below
- near_real: bfloat16 [2048, 4, 256, 256], P(('cluster', 'cone')), may hold values from -0.1875 to 0.1875
- near_imag: bfloat16 [2048, 4, 256, 256], P(('cluster', 'cone')), may hold values from -0.1875 to 0.1875
Outputs:
- potential: bfloat16 [2048, 256, 256], P(('cluster', 'cone'))
Inputs may be any that keep to these rules, and one draw needn't show every extreme that they name: `neighbours`: entry 0 of row l is l; every entry lies within 16 of l; for l > 0 a multiple of 16, entry 1 is l - 16.
All inputs are finite; a program needn't handle non-finite values. No bound on the sum of `cone_used` on one device may be relied on, other than what follows from the above.
Results may differ from a plain program's by a relative error of at most 0.015.
Values may be sent and summed in bfloat16 or wider, within the bound.
No kernel may reach another device: no remote copies, remote signals or barrier semaphores. Data moves between devices by JAX's collectives and lax.ppermute only.
A program may use at most 256 MiB of HBM per device.

v0:
```python
import jax
import jax.numpy as jnp
from jax import lax
from jax.sharding import PartitionSpec as P


def padded_2(cells, sides, width):
    for axis, dim in sides:
        count = lax.axis_size(axis)
        ends = count - 1
        head = lax.slice_in_dim(cells, 0, width, axis=dim)
        tail = lax.slice_in_dim(cells, cells.shape[dim] - width, cells.shape[dim], axis=dim)
        cells = jnp.concatenate(
            [
                lax.ppermute(tail, axis, [(i, (i + 1) % count) for i in range(ends)]),
                cells,
                lax.ppermute(head, axis, [((i + 1) % count, i) for i in range(ends)]),
            ],
            axis=dim,
        )
    return cells


def rotate(coef, phase, cone_used):
    half = coef.shape[-2] // 2
    coef_wide = coef.astype(jnp.float32)[..., None, :, :]
    real_rows = coef_wide[..., :half, :]
    imag_rows = coef_wide[..., half:, :]
    cosines = jnp.cos(phase)[..., None, None]
    sine_part = jnp.sin(phase)[..., None, None]
    weight = cone_used.astype(jnp.float32)[..., None, None, None]
    turned = jnp.concatenate(
        [cosines * real_rows - sine_part * imag_rows, sine_part * real_rows + cosines * imag_rows],
        axis=-2,
    )
    return (turned * weight).astype(jnp.bfloat16)


def per_device(
    upper_coef, phase, cone_used, transfer, leaf_basis, charges, neighbours, near_real, near_imag
):
    leaf_count = charges.shape[0]
    width = upper_coef.shape[2]
    columns = upper_coef.shape[3]
    turned = rotate(upper_coef, phase, cone_used)
    terms = jnp.einsum("coij,pcojr->poir", transfer, turned, preferred_element_type=jnp.float32)
    leaf_coef = lax.psum_scatter(
        terms.reshape(lax.axis_size("cone") * leaf_count, width, columns).astype(jnp.bfloat16),
        "cone",
        scatter_dimension=0,
        tiled=True,
    )
    far = jnp.einsum("lspk,lkr->lpsr", leaf_basis, leaf_coef, preferred_element_type=jnp.float32)
    far = far.reshape(leaf_count, far.shape[1], 2 * columns)
    padded = padded_2(charges, ((("cluster", "cone"), 0),), leaf_count)
    first_leaf = lax.axis_index(("cluster", "cone")) * leaf_count
    local_ids = neighbours - first_leaf + leaf_count
    sources = padded[local_ids]
    first = jnp.einsum("lnij,lnjr->lir", near_real, sources, preferred_element_type=jnp.float32)
    second = jnp.einsum("lnij,lnjr->lir", near_imag, sources, preferred_element_type=jnp.float32)
    near = jnp.concatenate(
        [
            first[..., :columns] - second[..., columns:],
            first[..., columns:] + second[..., :columns],
        ],
        axis=-1,
    )
    return (far + near).astype(jnp.bfloat16)


def solution(mesh):
    in_specs = (
        P("cluster", "cone", None, None),
        P("cluster", "cone", None),
        P("cluster", "cone"),
        P("cone", None, None, None),
        P(("cluster", "cone"), None, None, None),
        P(("cluster", "cone"), None, None),
        P(("cluster", "cone"), None),
        P(("cluster", "cone"), None, None, None),
        P(("cluster", "cone"), None, None, None),
    )
    out_specs = P(("cluster", "cone"), None, None)
    return jax.shard_map(
        per_device, mesh=mesh, in_specs=in_specs, out_specs=out_specs, check_vma=False
    )
```

profile of v0, /device:TPU:63, one launch (start us, length us, event | category | flops | bytes accessed | tf_op | source)
XLA Modules:
  0.0 197.0 jit_solution(7513017592023164458)
XLA Ops:
  6.5 0.0 copy-start
  6.5 0.0 reduce-scatter.2.cloned.1.call-start
  6.5 2.3 %bitcast_convert_fusion.1 = f32[32,2,1,128,128]{4,3,1,0,2:T(8,128)S(1)} fusion(bf16[32,2,128,128]{3,2,1,0:T(8,128)(2,1)} %param.9), kind=kLoop, calls=%fused_computation.18 | loop fusion | flops 1048576 | bytes 6291456 | tf_op jit(solution)/shard_map/broadcast_in_dim | solution.py:26
  8.8 2.3 %slice_bitcast_fusion.1 = (f32[32,2,64,128]{3,2,1,0:T(8,128)}, f32[32,2,64,128]{3,2,1,0:T(8,128)}) fusion(f32[32,2,1,128,128]{4,3,1,0,2:T(8,128)S(1)} %bitcast_convert_fusion.1), kind=kLoop, calls=%fused_computation.17 | loop fusion | bytes 8388608 | tf_op jit(solution)/shard_map/mul | solution.py:33
  11.1 0.0 copy-start.4
  11.1 0.0 copy-start.6
  11.1 3.8 %copy.21 = f32[32,2,64,128]{2,3,1,0:T(8,128)} copy(f32[32,2,64,128]{3,2,1,0:T(8,128)} %get-tuple-element.9) | data formatting | bytes 4194304 | tf_op jit(solution)/shard_map/mul | solution.py:33
  15.0 3.8 %copy.23 = f32[32,2,64,128]{2,3,1,0:T(8,128)} copy(f32[32,2,64,128]{3,2,1,0:T(8,128)} %get-tuple-element.10) | data formatting | bytes 4194304 | tf_op jit(solution)/shard_map/mul | solution.py:33
  18.8 0.0 copy-done.4
  18.8 0.1 copy.20
  19.0 0.1 copy.22
  19.1 0.0 copy-done.6
  19.1 0.1 copy.24
  19.2 0.0 copy-start.3
  19.2 25.2 %multiply_subtract_fusion = (f32[32,2,8,64,128]{3,4,1,0,2:T(8,128)}, f32[32,2,8,64,128]{3,4,1,0,2:T(8,128)}) fusion(f32[32,2,64,128]{2,3,1,0:T(8,128)} %copy.23, f32[32,2,8]{1,0,2:T(8,128)S(1)} %copy.22, f32[32,2,64,128]{2,3,1,0:T(8,128)} %copy.21, f32[32,2,8]{1,0,2:T(8,128)S(1)} %copy.20), kind=kLoop, calls=%fused_computation.4 | loop fusion | flops 25165824 | bytes 37752832 | tf_op jit(solution)/shard_map/sub | solution.py:33
  44.4 0.0 copy-done.3
  44.4 26.1 %fusion.4 = bf16[32,8,128,128]{2,3,0,1:T(8,128)(2,1)} fusion(f32[32,2,8,64,128]{3,4,1,0,2:T(8,128)} %get-tuple-element.6, f32[32,2,8,64,128]{3,4,1,0,2:T(8,128)} %get-tuple-element.5, f32[32,2]{1,0:T(8,128)S(1)} %copy.24, bf16[2,8,128,128]{3,2,1,0:T(8,128)(2,1)S(1)} %copy-done.3), kind=kOutput, calls=%fused_computation.8 | convolution fusion | flops 2176843776 | bytes 42467584 | tf_op jit(solution)/shard_map/coij,pcojr->poir/dot_general | solution.py:46
  70.5 12.0 %copy.26 = bf16[32,8,128,128]{3,2,1,0:T(8,128)(2,1)} copy(bf16[32,8,128,128]{2,3,0,1:T(8,128)(2,1)} %fusion.4) | data formatting | bytes 16777216 | tf_op jit(solution)/shard_map/convert_element_type | solution.py:48
  82.5 0.0 copy-start.5
  82.5 0.0 reduce-scatter.2.cloned.1.call-update
  82.6 3.7 %collective-permute-start = (bf16[16,256,256]{2,1,0:T(8,128)(2,1)}, bf16[16,256,256]{2,1,0:T(8,128)(2,1)}, u32[]{:S(2)}, u32[]{:S(2)}) collective-permute-start(bf16[16,256,256]{2,1,0:T(8,128)(2,1)} %param.14), channel_id=1, source_target_pairs={{0,1},{1,2},{2,3},{3,4},{4,5},{5,6},{6,7},{7,8},{8,9},{9,10},{10,1... | collective-permute-start | bytes 6291464 | tf_op jit(solution)/shard_map/ppermute | solution.py:15
  86.3 2.1 %collective-permute-start.1 = (bf16[16,256,256]{2,1,0:T(8,128)(2,1)}, bf16[16,256,256]{2,1,0:T(8,128)(2,1)}, u32[]{:S(2)}, u32[]{:S(2)}) collective-permute-start(bf16[16,256,256]{2,1,0:T(8,128)(2,1)} %param.14), channel_id=1, source_target_pairs={{1,0},{2,1},{3,2},{4,3},{5,4},{6,5},{7,6},{8,7},{9,8},{10,9},{11,1... | collective-permute-start | bytes 6291464 | tf_op jit(solution)/shard_map/ppermute | solution.py:17
  88.4 0.0 copy-done.5
  88.4 0.1 copy.28
  88.5 0.1 reshape.12
  88.6 37.1 %collective-permute-done = bf16[16,256,256]{2,1,0:T(8,128)(2,1)} collective-permute-done((bf16[16,256,256]{2,1,0:T(8,128)(2,1)}, bf16[16,256,256]{2,1,0:T(8,128)(2,1)}, u32[]{:S(2)}, u32[]{:S(2)}) %collective-permute-start) | collective-permute-done | bytes 2097184 | tf_op jit(solution)/shard_map/ppermute | solution.py:15
  125.7 14.0 %collective-permute-done.1 = bf16[16,256,256]{2,1,0:T(8,128)(2,1)} collective-permute-done((bf16[16,256,256]{2,1,0:T(8,128)(2,1)}, bf16[16,256,256]{2,1,0:T(8,128)(2,1)}, u32[]{:S(2)}, u32[]{:S(2)}) %collective-permute-start.1) | collective-permute-done | bytes 2097184 | tf_op jit(solution)/shard_map/ppermute | solution.py:17
  139.6 6.5 %pad_maximum_fusion = bf16[48,256,256]{2,1,0:T(8,128)(2,1)} fusion(bf16[16,256,256]{2,1,0:T(8,128)(2,1)} %collective-permute-done.1, bf16[16,256,256]{2,1,0:T(8,128)(2,1)} %param.14, bf16[16,256,256]{2,1,0:T(8,128)(2,1)} %collective-permute-done), kind=kLoop, calls=%fused_computation.9 | loop fusion | flops 6291456 | bytes 12582912 | tf_op jit(solution)/shard_map/concatenate | solution.py:13
  146.1 8.5 %gather_fusion = bf16[64,256,256]{2,1,0:T(8,128)(2,1)} fusion(bf16[48,256,256]{2,1,0:T(8,128)(2,1)} %pad_maximum_fusion, s32[1024]{0:T(1024)S(1)} %pad_clamp_fusion), kind=kCustom, calls=%fused_computation | custom fusion | bytes 16777472 | tf_op jit(solution)/shard_map/gather | solution.py:58
  154.7 10.4 %convolution_bitcast_fusion = f32[16,256,256]{1,2,0:T(8,128)} fusion(bf16[16,4,256,256]{3,2,1,0:T(8,128)(2,1)} %bitcast.44, bf16[16,4,256,256]{3,2,1,0:T(8,128)(2,1)} %param.17), kind=kOutput, calls=%fused_computation.12 | convolution fusion | flops 2147483648 | bytes 20971520 | tf_op jit(solution)/shard_map/lnij,lnjr->lir/dot_general | solution.py:60
  165.1 10.4 %convolution_bitcast_fusion.1 = f32[16,256,256]{1,2,0:T(8,128)} fusion(bf16[16,4,256,256]{3,2,1,0:T(8,128)(2,1)} %bitcast.45, bf16[16,4,256,256]{3,2,1,0:T(8,128)(2,1)} %param.16), kind=kOutput, calls=%fused_computation.13 | convolution fusion | flops 2147483648 | bytes 20971520 | tf_op jit(solution)/shard_map/lnij,lnjr->lir/dot_general | solution.py:59
  175.5 6.3 %slice_subtract_fusion = (f32[16,256,128]{1,2,0:T(8,128)}, f32[16,256,128]{1,2,0:T(8,128)}) fusion(f32[16,256,256]{1,2,0:T(8,128)} %convolution_bitcast_fusion, f32[16,256,256]{1,2,0:T(8,128)} %convolution_bitcast_fusion.1), kind=kLoop, calls=%fused_computation.15 | loop fusion | flops 1048576 | bytes 12582912 | tf_op jit(solution)/shard_map/sub | solution.py:63
  181.7 0.0 reduce-scatter.2.cloned.1.call-done
  181.7 0.0 copy-done
  181.7 0.0 copy-start.1
  181.7 0.0 copy-start.2
  181.7 1.9 fusion.8
  183.7 0.0 copy-done.1
  183.7 0.4 copy-done.2
  184.1 2.2 %fusion.7 = bf16[16,256,256]{1,2,0:T(8,128)(2,1)} fusion(f32[16,256,128]{1,2,0:T(8,128)S(1)} %copy-done.2, f32[16,256,128]{1,2,0:T(8,128)S(1)} %copy-done.1, f32[16,128,2,256]{3,1,2,0:T(8,128)S(1)} %fusion.8), kind=kLoop, calls=%fused_computation.11 | loop fusion | flops 3145728 | bytes 10485760 | tf_op jit(solution)/shard_map/convert_element_type | solution.py:68
  186.3 3.9 %copy.31 = bf16[16,256,256]{2,1,0:T(8,128)(2,1)} copy(bf16[16,256,256]{1,2,0:T(8,128)(2,1)} %fusion.7) | data formatting | bytes 4194304 | tf_op jit(solution)/shard_map/convert_element_type | solution.py:68
  (4 shorter events, 0.1 us)
Async XLA Ops:
  6.5 175.2 %copy-start = (bf16[16,2,256,128]{3,2,1,0:T(8,128)(2,1)S(1)}, bf16[16,2,256,128]{3,2,1,0:T(8,128)(2,1)}, u32[]{:S(2)}) copy-start(bf16[16,2,256,128]{3,2,1,0:T(8,128)(2,1)} %param.13) | copy-start | bytes 6291460
  6.5 175.2 %reduce-scatter.2.cloned.1.call-start = ((), (), s32[]{:S(2)}) async-start(), calls=%async_computation.1 | async-start | bytes 8912896 | tf_op jit(solution)/shard_map/reduce_scatter | solution.py:47
  11.1 7.7 %copy-start.4 = (f32[32,2,8]{0,2,1:T(8,128)S(1)}, f32[32,2,8]{0,2,1:T(8,128)}, u32[]{:S(2)}) copy-start(f32[32,2,8]{0,2,1:T(8,128)} %param.10) | copy-start | bytes 6148
  11.1 8.0 %copy-start.6 = (s32[32,2]{0,1:T(2,128)S(1)}, s32[32,2]{0,1:T(2,128)}, u32[]{:S(2)}) copy-start(s32[32,2]{0,1:T(2,128)} %param.11) | copy-start | bytes 772
  19.2 25.2 %copy-start.3 = (bf16[2,8,128,128]{3,2,1,0:T(8,128)(2,1)S(1)}, bf16[2,8,128,128]{3,2,1,0:T(8,128)(2,1)}, u32[]{:S(2)}) copy-start(bf16[2,8,128,128]{3,2,1,0:T(8,128)(2,1)} %param.12) | copy-start | bytes 1572868
  82.5 5.8 %copy-start.5 = (s32[16,4]{0,1:T(4,128)S(1)}, s32[16,4]{0,1:T(4,128)}, u32[]{:S(2)}) copy-start(s32[16,4]{0,1:T(4,128)} %param.15) | copy-start | bytes 772
  82.6 43.1 %collective-permute-start = (bf16[16,256,256]{2,1,0:T(8,128)(2,1)}, bf16[16,256,256]{2,1,0:T(8,128)(2,1)}, u32[]{:S(2)}, u32[]{:S(2)}) collective-permute-start(bf16[16,256,256]{2,1,0:T(8,128)(2,1)} %param.14), channel_id=1, source_target_pairs={{0,1},{1,2},{2,3},{3,4},{4,5},{5,6},{6,7},{7,8},{8,9},{9,10},{10,1... | collective-permute-start | bytes 6291464 | tf_op jit(solution)/shard_map/ppermute | solution.py:15
  86.3 53.4 %collective-permute-start.1 = (bf16[16,256,256]{2,1,0:T(8,128)(2,1)}, bf16[16,256,256]{2,1,0:T(8,128)(2,1)}, u32[]{:S(2)}, u32[]{:S(2)}) collective-permute-start(bf16[16,256,256]{2,1,0:T(8,128)(2,1)} %param.14), channel_id=1, source_target_pairs={{1,0},{2,1},{3,2},{4,3},{5,4},{6,5},{7,6},{8,7},{9,8},{10,9},{11,1... | collective-permute-start | bytes 6291464 | tf_op jit(solution)/shard_map/ppermute | solution.py:17
  181.7 2.0 copy-start.1
  181.7 2.4 %copy-start.2 = (f32[16,256,128]{1,2,0:T(8,128)S(1)}, f32[16,256,128]{1,2,0:T(8,128)}, u32[]{:S(2)}) copy-start(f32[16,256,128]{1,2,0:T(8,128)} %get-tuple-element.8) | copy-start | bytes 6291460
Sparse Core Ops, SparseCore 0:
  82.7 85.8 reduce-scatter.1
where the time goes:
time: 198 us; the launch traced here: 197 us
  waiting for transfers between devices  51.1 us (26%)
  matrix products  48.9 us (25%)
  other arithmetic  42.4 us (21%)
  local copies, waits for them, and re-layouts  35.4 us (18%)
  between operations  13.5 us (7%)
  starting transfers between devices  5.79 us (3%)
    ppermute x1, waiting for transfers between devices, padded_2(): lax.ppermute(tail, axis, [(i, (i + 1) % count) for i in range(ends)])  37.1 us
    dot_general x1, matrix products, per_device(): jnp.einsum('coij,pcojr->poir', transfer, turned, preferred_element_type=j...  26.1 us
    sub x1, other arithmetic, rotate(): cosines * real_rows - sine_part * imag_rows  25.2 us
    ppermute x1, waiting for transfers between devices, padded_2(): lax.ppermute(head, axis, [((i + 1) % count, i) for i in range(ends)])  14 us
    convert_element_type x1, local copies, waits for them, and re-layouts, per_device(): terms.reshape(lax.axis_size('cone') * leaf_count, width, columns)  12 us
    dot_general x1, matrix products, per_device(): jnp.einsum('lnij,lnjr->lir', near_imag, sources, preferred_element_type=j...  10.4 us
    dot_general x1, matrix products, per_device(): jnp.einsum('lnij,lnjr->lir', near_real, sources, preferred_element_type=j...  10.4 us
    gather x1, local copies, waits for them, and re-layouts, per_device(): sources = padded[local_ids]  8.53 us
  transfers between devices with their start and end apart: 3, of which 2 were waited for; matrix products, arithmetic and copies ran while one was open for 21% of the time, Pallas kernels for 0%

commit v1 on v0

v1 whole, which is shorter than its diff:
```python
import functools

import jax
import jax.numpy as jnp
from jax import lax
from jax.experimental import pallas as pl
from jax.experimental.pallas import tpu as pltpu
from jax.sharding import PartitionSpec as P

AXES = ("cluster", "cone")
DEVICES = 128
ROW = 8
F32 = jnp.float32
BF16 = jnp.bfloat16


def moved(dx):
    return [(d, (d & ~6) | ((((d >> 1) & 3) + dx) % 4) << 1) for d in range(DEVICES)]


FLIP_CORE = [(d, d ^ 1) for d in range(DEVICES)]
FLIP_Z = [(d, d ^ 8) for d in range(DEVICES)]
FLIP_BOTH = [(d, d ^ 9) for d in range(DEVICES)]
FLIP_OUTER = [(d, d ^ 72) for d in range(DEVICES)]
X_UP = moved(1)
X_DOWN = moved(-1)
UP = [(d, d + 1) for d in range(DEVICES) if d % ROW != ROW - 1]
DOWN = [(d, d - 1) for d in range(DEVICES) if d % ROW != 0]
WRAP = [(d, d ^ 7) for d in range(DEVICES) if d % ROW in (0, ROW - 1)]
NEXT_ROW = [(d, d + ROW) for d in range(0, DEVICES - ROW, ROW)] + [
    (d, d - ROW) for d in range(2 * ROW - 1, DEVICES, ROW)
]


def permute(array, pairs):
    return lax.ppermute(array, AXES, pairs)


def split_kernel(place, coef, to_core, to_z, to_both, sems):
    zl, core = place[0], place[1]
    copies = [
        pltpu.make_async_copy(coef.at[1 - zl, :, core], to_z, sems.at[0]),
        pltpu.make_async_copy(coef.at[1 - zl, :, 1 - core], to_both, sems.at[1]),
        pltpu.make_async_copy(coef.at[zl, :, 1 - core], to_core, sems.at[2]),
    ]
    for copy in copies:
        copy.start()
    for copy in copies:
        copy.wait()


def split_coef(place, coef):
    part = jax.ShapeDtypeStruct(coef.shape[1:2] + coef.shape[3:], coef.dtype)
    return pl.pallas_call(
        split_kernel,
        out_shape=(part, part, part),
        in_specs=[pl.BlockSpec(memory_space=pltpu.SMEM), pl.BlockSpec(memory_space=pl.ANY)],
        out_specs=(pl.BlockSpec(memory_space=pl.ANY),) * 3,
        scratch_shapes=[pltpu.SemaphoreType.DMA((3,))],
        name="split_coef",
    )(place, coef)


def transfer_kernel(octants, place, targets, cosines, sines, own, c1, c2, c3, t0, t1, t2, t3, out):
    target = targets[pl.program_id(0)]
    first = pl.program_id(1) * octants
    coefs = (own.at[0, 0, 0], c1.at[0], c2.at[0], c3.at[0])
    moves = (t0, t1, t2, t3)
    half = out.shape[-2] // 2
    for o in range(octants):
        total = None
        for source in range(4):
            columns = []
            for j in range(2):
                rows = []
                for cone in range(2):
                    at = ((target * 2 + j) * 8 + source * 2 + cone) * 8 + first + o
                    cosine, sine = cosines[at], sines[at]
                    real = coefs[source][j, cone, :half, :].astype(F32)
                    imag = coefs[source][j, cone, half:, :].astype(F32)
                    rows.append((cosine * real - sine * imag).astype(BF16))
                    rows.append((sine * real + cosine * imag).astype(BF16))
                columns.append(jnp.concatenate(rows, axis=0))
            turned = jnp.concatenate(columns, axis=1)
            matrix = jnp.concatenate([moves[source][0, o], moves[source][1, o]], axis=1)
            term = jnp.dot(matrix, turned, preferred_element_type=F32)
            total = term if total is None else total + term
        width = out.shape[-1]
        out[0, 0, o] = total[:, :width].astype(BF16)
        out[0, 1, o] = total[:, width:].astype(BF16)


def transfer_terms(place, targets, cosines, sines, coefs, moves):
    count = targets.shape[0]
    octants = 4
    part = (1,) + coefs[1].shape[1:]
    matrices = (2, octants) + moves[0].shape[2:]
    own_spec = pl.BlockSpec(
        (1, 1, 1) + part[1:], lambda t, o, place, targets, *_: (place[0], targets[t], place[1], 0, 0, 0, 0)
    )
    coef_spec = pl.BlockSpec(part, lambda t, o, place, targets, *_: (targets[t], 0, 0, 0, 0))
    move_spec = pl.BlockSpec(matrices, lambda t, o, *_: (0, o, 0, 0))
    shape = (count, 2, 8) + coefs[1].shape[-2:]
    return pl.pallas_call(
        functools.partial(transfer_kernel, octants),
        out_shape=jax.ShapeDtypeStruct(shape, BF16),
        grid_spec=pltpu.PrefetchScalarGridSpec(
            num_scalar_prefetch=4,
            grid=(count, 8 // octants),
            in_specs=[own_spec] + [coef_spec] * 3 + [move_spec] * 4,
            out_specs=pl.BlockSpec((1, 2, octants) + shape[3:], lambda t, o, *_: (t, 0, o, 0, 0)),
        ),
        compiler_params=pltpu.CompilerParams(vmem_limit_bytes=32 << 20),
        cost_estimate=pl.CostEstimate(
            flops=count * 2 * 8 * 2 * 1024 * 128 * 128, bytes_accessed=(count + 3) << 20, transcendentals=0
        ),
        name="transfer_terms",
    )(place, targets, cosines, sines, *coefs, *moves)


def apply_kernel(ids, edge, near_real, near_imag, basis, leaf0, leaf1, leaf2, below, own, above, wrapped, out, sources, sems):
    leaf = pl.program_id(0)
    count = own.shape[0]
    columns = leaf0.shape[-1]
    low, middle, high = (sources.at[pl.ds(i * count, count)] for i in range(3))

    @pl.when(leaf == 0)
    def _():
        copy_own = pltpu.make_async_copy(own, middle, sems.at[0])
        copy_own.start()

        @pl.when(edge[0] == 1)
        def _():
            pltpu.make_async_copy(wrapped, low, sems.at[1]).start()

        @pl.when(edge[0] == 0)
        def _():
            pltpu.make_async_copy(below, low, sems.at[1]).start()

        @pl.when(edge[1] == 1)
        def _():
            pltpu.make_async_copy(wrapped, high, sems.at[2]).start()

        @pl.when(edge[1] == 0)
        def _():
            pltpu.make_async_copy(above, high, sems.at[2]).start()

        copy_own.wait()
        pltpu.make_async_copy(below, low, sems.at[1]).wait()
        pltpu.make_async_copy(above, high, sems.at[2]).wait()

    coef = (leaf0[0].astype(F32) + leaf1[0].astype(F32) + leaf2[0].astype(F32)).astype(BF16)
    total = jnp.concatenate(
        [jnp.dot(basis[0, s], coef, preferred_element_type=F32) for s in range(2)], axis=1
    )
    for n in range(4):
        charge = sources[ids[leaf * 4 + n]]
        crossed = jnp.concatenate([-charge[:, columns:], charge[:, :columns]], axis=1)
        total += jnp.dot(near_real[0, n], charge, preferred_element_type=F32)
        total += jnp.dot(near_imag[0, n], crossed, preferred_element_type=F32)
    out[0] = total.astype(BF16)


def apply_leaves(ids, edge, near_real, near_imag, basis, leaf_terms, below, own, above, wrapped):
    count, points, wide = own.shape
    matrices = pl.BlockSpec((1,) + near_real.shape[1:], lambda l, *_: (l, 0, 0, 0))
    leaf_spec = pl.BlockSpec((1,) + leaf_terms[0].shape[1:], lambda l, *_: (l, 0, 0))
    anywhere = pl.BlockSpec(memory_space=pl.ANY)
    return pl.pallas_call(
        apply_kernel,
        out_shape=jax.ShapeDtypeStruct(own.shape, BF16),
        grid_spec=pltpu.PrefetchScalarGridSpec(
            num_scalar_prefetch=2,
            grid=(count,),
            in_specs=[matrices, matrices, pl.BlockSpec((1,) + basis.shape[1:], lambda l, *_: (l, 0, 0, 0))]
            + [leaf_spec] * 3
            + [anywhere] * 4,
            out_specs=pl.BlockSpec((1, points, wide), lambda l, *_: (l, 0, 0)),
            scratch_shapes=[pltpu.VMEM((3 * count, points, wide), BF16), pltpu.SemaphoreType.DMA((3,))],
        ),
        compiler_params=pltpu.CompilerParams(vmem_limit_bytes=32 << 20),
        cost_estimate=pl.CostEstimate(flops=4_600_000_000, bytes_accessed=28 << 20, transcendentals=0),
        name="apply_leaves",
    )(ids, edge, near_real, near_imag, basis, *leaf_terms, below, own, above, wrapped)


def per_device(
    upper_coef, phase, cone_used, transfer, leaf_basis, charges, neighbours, near_real, near_imag
):
    leaf_count = charges.shape[0]
    cluster, cone = lax.axis_index("cluster"), lax.axis_index("cone")
    zl, x, core = cone // 8, (cone // 2) % 4, cone % 2
    place = jnp.stack([zl, core]).astype(jnp.int32)

    coef = upper_coef.reshape((2, 4, 2, 2) + upper_coef.shape[1:])
    to_core, to_z, to_both = split_coef(place, coef)
    from_z = permute(to_z, FLIP_Z)
    from_both = permute(to_both, FLIP_BOTH)
    from_core = permute(to_core, FLIP_CORE)

    below = permute(charges, UP)
    above = permute(charges, DOWN)
    wrapped = permute(permute(charges, WRAP), NEXT_ROW)

    weight = cone_used.astype(F32)[..., None]
    turn = jnp.stack([jnp.cos(phase) * weight, jnp.sin(phase) * weight])
    turn = turn.reshape((2, 2, 4, 2, 2) + turn.shape[2:])

    def turn_of(z, c):
        return turn[:, z, :, c]

    turns = [
        turn_of(zl, core),
        permute(turn_of(zl, 1 - core), FLIP_CORE),
        permute(turn_of(1 - zl, core), FLIP_Z),
        permute(turn_of(1 - zl, 1 - core), FLIP_BOTH),
    ]
    turns = jnp.stack(turns, axis=3)
    cosines, sines = turns[0].reshape(-1), turns[1].reshape(-1)

    transfer_outer = permute(transfer, FLIP_OUTER)
    moves = [transfer, permute(transfer, FLIP_CORE), transfer_outer, permute(transfer_outer, FLIP_CORE)]
    coefs = [coef, from_core, from_z, from_both]

    def terms(offsets):
        targets = jnp.stack([(x + offset) % 4 for offset in offsets]).astype(jnp.int32)
        return transfer_terms(place, targets, cosines, sines, coefs, moves)

    far_terms = terms([2])
    up = permute(far_terms[0, 0], X_UP)
    down = permute(far_terms[0, 1], X_DOWN)
    rest = terms([1, 3, 0])

    def added(a, b):
        return (a.astype(F32) + b.astype(F32)).astype(BF16)

    from_below = permute(jnp.stack([added(rest[0, 0], up), rest[0, 1]]), X_UP)
    from_above = permute(jnp.stack([rest[1, 0], added(rest[1, 1], down)]), X_DOWN)
    leaf_terms = [
        part.reshape((leaf_count,) + part.shape[-2:]) for part in (rest[2], from_below, from_above)
    ]

    first_leaf = (cluster * 16 + cone) * leaf_count
    ids = (neighbours - first_leaf + leaf_count).reshape(-1)
    edge = jnp.stack([cone % ROW == 0, cone % ROW == ROW - 1]).astype(jnp.int32)
    return apply_leaves(
        ids, edge, near_real, near_imag, leaf_basis, leaf_terms, below, charges, above, wrapped
    )


def solution(mesh):
    in_specs = (
        P("cluster", "cone", None, None),
        P("cluster", "cone", None),
        P("cluster", "cone"),
        P("cone", None, None, None),
        P(("cluster", "cone"), None, None, None),
        P(("cluster", "cone"), None, None),
        P(("cluster", "cone"), None),
        P(("cluster", "cone"), None, None, None),
        P(("cluster", "cone"), None, None, None),
    )
    out_specs = P(("cluster", "cone"), None, None)
    return jax.shard_map(
        per_device, mesh=mesh, in_specs=in_specs, out_specs=out_specs, check_vma=False
    )
```

time: 198 us -> 164 us (0.83)
  the two profiles are of different devices: /device:TPU:63 before, /device:TPU:24 now
where the time goes in v1:
time: 164 us; the launch traced here: 163 us
  Pallas kernels  78.2 us (48%)
  waiting for transfers between devices  50.3 us (31%)
  starting transfers between devices  23.2 us (14%)
  local copies, waits for them, and re-layouts  7.38 us (4%)
  other arithmetic  3.58 us (2%)
    ppermute x17, waiting for transfers between devices, permute(): return lax.ppermute(array, AXES, pairs)  50.3 us
    pallas_call x1, Pallas kernels, split_coef(): pl.pallas_call(split_kernel, out_shape=(part, part, part), in_specs=[pl.B...  49.6 us
    ppermute x17, starting transfers between devices, permute(): return lax.ppermute(array, AXES, pairs)  23.2 us
    pallas_call x1, Pallas kernels, apply_leaves(): pl.pallas_call(apply_kernel, out_shape=jax.ShapeDtypeStruct(own.shape, BF...  17.1 us
    pallas_call x2, Pallas kernels, transfer_terms(): pl.pallas_call(functools.partial(transfer_kernel, octants), out_shape=jax...  11.6 us
    unnamed x17, local copies, waits for them, and re-layouts  5.77 us
  transfers between devices with their start and end apart: 17, of which 9 were waited for; matrix products, arithmetic and copies ran while one was open for 4% of the time, Pallas kernels for 38%

profile of v1, /device:TPU:24, one launch (start us, length us, event | category | flops | bytes accessed | tf_op | source)
XLA Modules:
  0.0 162.9 jit_solution(10508344781850845204)
XLA Ops:
  0.0 4.4 %collective-permute-start.15 = (bf16[16,256,256]{2,1,0:T(8,128)(2,1)}, bf16[16,256,256]{2,1,0:T(8,128)(2,1)}, u32[]{:S(2)}, u32[]{:S(2)}) collective-permute-start(bf16[16,256,256]{2,1,0:T(8,128)(2,1)} %own.1), channel_id=1, source_target_pairs={{0,7},{7,0},{8,15},{15,8},{16,23},{23,16},{24,31},{31,24},{32,39},... | collective-permute-start | bytes 6291464 | tf_op jit(solution)/shard_map/ppermute | solution.py:36
  4.4 0.6 pad_add_fusion.place
  5.0 49.6 %split_coef.1 = (bf16[4,2,2,128,128]{4,3,2,1,0:T(8,128)(2,1)}, bf16[4,2,2,128,128]{4,3,2,1,0:T(8,128)(2,1)}, bf16[4,2,2,128,128]{4,3,2,1,0:T(8,128)(2,1)}) custom-call(s32[2]{0:T(128)} %pad_add_fusion.place, bf16[2,4,2,2,2,128,128]{6,5,4,3,2,1,0:T(8,128)(2,1)} %bitcast.51), custom_call_target="tpu_custom_call" | custom-call | tf_op jit(solution)/shard_map/split_coef/pallas_call | solution.py:54
  54.6 0.1 collective-permute-start.3
  54.7 4.1 %collective-permute-start.7 = (bf16[2,8,128,128]{3,2,1,0:T(8,128)(2,1)}, bf16[2,8,128,128]{3,2,1,0:T(8,128)(2,1)}, u32[]{:S(2)}, u32[]{:S(2)}) collective-permute-start(bf16[2,8,128,128]{3,2,1,0:T(8,128)(2,1)} %t0.3), channel_id=1, source_target_pairs={{0,72},{1,73},{2,74},{3,75},{4,76},{5,77},{6,78},{7,79},{8,64},{9,... | collective-permute-start | bytes 1572872 | tf_op jit(solution)/shard_map/ppermute | solution.py:36
  58.8 0.8 copy.15
  59.6 0.7 convert_element_type.31
  60.3 0.1 sine_multiply_fusion
  60.5 0.2 collective-permute-start
  60.7 0.1 collective-permute-start.1
  60.8 0.9 collective-permute-done
  61.7 0.9 collective-permute-start.2
  62.6 1.9 %collective-permute-done.1 = f32[2,4,2,2,8]{4,3,2,1,0:T(2,128)S(1)} collective-permute-done((f32[2,4,2,2,8]{4,3,2,1,0:T(2,128)S(1)}, f32[2,4,2,2,8]{4,3,2,1,0:T(2,128)S(1)}, u32[]{:S(2)}, u32[]{:S(2)}) %collective-permute-start.1) | collective-permute-done | bytes 1056 | tf_op jit(solution)/shard_map/ppermute | solution.py:36
  64.6 0.3 collective-permute-done.2
  64.9 1.3 collective-permute-start.5
  66.2 0.0 collective-permute-done.3.c1
  66.2 0.5 collective-permute-start.6
  66.7 4.9 %collective-permute-done.7.t2 = bf16[2,8,128,128]{3,2,1,0:T(8,128)(2,1)} collective-permute-done((bf16[2,8,128,128]{3,2,1,0:T(8,128)(2,1)}, bf16[2,8,128,128]{3,2,1,0:T(8,128)(2,1)}, u32[]{:S(2)}, u32[]{:S(2)}) %collective-permute-start.7) | collective-permute-done | bytes 524320 | tf_op jit(solution)/shard_map/ppermute | solution.py:36
  71.6 8.1 %collective-permute-done.4.c2 = bf16[4,2,2,128,128]{4,3,2,1,0:T(8,128)(2,1)} collective-permute-done((bf16[4,2,2,128,128]{4,3,2,1,0:T(8,128)(2,1)}, bf16[4,2,2,128,128]{4,3,2,1,0:T(8,128)(2,1)}, u32[]{:S(2)}, u32[]{:S(2)}) %collective-permute-start.4) | collective-permute-done | bytes 524320 | tf_op jit(solution)/shard_map/ppermute | solution.py:36
  79.7 2.6 %collective-permute-start.13 = (bf16[16,256,256]{2,1,0:T(8,128)(2,1)}, bf16[16,256,256]{2,1,0:T(8,128)(2,1)}, u32[]{:S(2)}, u32[]{:S(2)}) collective-permute-start(bf16[16,256,256]{2,1,0:T(8,128)(2,1)} %own.1), channel_id=1, source_target_pairs={{0,1},{1,2},{2,3},{3,4},{4,5},{5,6},{6,7},{8,9},{9,10},{10,11},{11... | collective-permute-start | bytes 6291464 | tf_op jit(solution)/shard_map/ppermute | solution.py:36
  82.3 5.8 %collective-permute-done.5.c3 = bf16[4,2,2,128,128]{4,3,2,1,0:T(8,128)(2,1)} collective-permute-done((bf16[4,2,2,128,128]{4,3,2,1,0:T(8,128)(2,1)}, bf16[4,2,2,128,128]{4,3,2,1,0:T(8,128)(2,1)}, u32[]{:S(2)}, u32[]{:S(2)}) %collective-permute-start.5) | collective-permute-done | bytes 524320 | tf_op jit(solution)/shard_map/ppermute | solution.py:36
  88.1 1.3 collective-permute-start.14
  89.4 2.9 %collective-permute-start.16 = (bf16[16,256,256]{2,1,0:T(8,128)(2,1)}, bf16[16,256,256]{2,1,0:T(8,128)(2,1)}, u32[]{:S(2)}, u32[]{:S(2)}) collective-permute-start(bf16[16,256,256]{2,1,0:T(8,128)(2,1)} %collective-permute-done.15), channel_id=1, source_target_pairs={{0,8},{8,16},{16,24},{24,32},{32,40},{40,48},{48,56},{56,64},{64,7... | collective-permute-start | bytes 6291464 | tf_op jit(solution)/shard_map/ppermute | solution.py:36
  92.3 0.1 pad_add_fusion.1.targets
  92.5 0.1 reshape_squeeze.10.sines
  92.6 0.1 reshape_squeeze.9.cosines
  92.7 3.6 %transfer_terms.3 = bf16[1,2,8,128,128]{4,3,2,1,0:T(8,128)(2,1)S(1)} custom-call(s32[2]{0:T(128)S(1)} %copy-done.6, s32[1]{0:T(128)} %bitcast.19.targets, f32[512]{0:T(512)S(1)} %reshape_squeeze.9.cosines, f32[512]{0:T(512)S(1)} %reshape_squeeze.10.sines, bf16[2,4,2,2,2,128,128]{6,5,4,3,2,1,0:T(8,128)(2,1)S(1)} %bitcast.52, ...), custom_call_target="tpu_custom_call" | custom-call | flops 536870912 | bytes 4194304 | tf_op jit(solution)/shard_map/transfer_terms/pallas_call | solution.py:104
  96.4 2.3 %collective-permute-start.11 = (bf16[8,128,128]{2,1,0:T(8,128)(2,1)S(1)}, bf16[8,128,128]{2,1,0:T(8,128)(2,1)S(1)}, u32[]{:S(2)}, u32[]{:S(2)}) collective-permute-start(bf16[8,128,128]{2,1,0:T(8,128)(2,1)S(1)} %get-tuple-element.15), channel_id=1, source_target_pairs={{0,6},{1,7},{2,0},{3,1},{4,2},{5,3},{6,4},{7,5},{8,14},{9,15},{10,... | collective-permute-start | bytes 786440 | tf_op jit(solution)/shard_map/ppermute | solution.py:36
  98.8 0.5 collective-permute-start.9
  99.2 8.0 %transfer_terms.2 = bf16[3,2,8,128,128]{4,3,2,1,0:T(8,128)(2,1)S(1)} custom-call(s32[2]{0:T(128)S(1)} %copy-done.6, s32[3]{0:T(128)S(1)} %pad_add_fusion.1.targets, f32[512]{0:T(512)S(1)} %reshape_squeeze.9.cosines, f32[512]{0:T(512)S(1)} %reshape_squeeze.10.sines, bf16[2,4,2,2,2,128,128]{6,5,4,3,2,1,0:T(8,128)(2,1)S(1)} %bitcast.53, ...), custom_call_target="tpu_custom_call" | custom-call | flops 1610612736 | bytes 6291456 | tf_op jit(solution)/shard_map/transfer_terms/pallas_call | solution.py:104
  107.2 0.0 copy-start.2
  107.3 0.0 copy-start.7
  107.3 0.0 copy-start.3
  107.3 21.0 %collective-permute-done.11 = bf16[8,128,128]{2,1,0:T(8,128)(2,1)S(1)} collective-permute-done((bf16[8,128,128]{2,1,0:T(8,128)(2,1)S(1)}, bf16[8,128,128]{2,1,0:T(8,128)(2,1)S(1)}, u32[]{:S(2)}, u32[]{:S(2)}) %collective-permute-start.11) | collective-permute-done | bytes 262176 | tf_op jit(solution)/shard_map/ppermute | solution.py:36
  128.3 0.1 fusion.3
  128.5 0.8 pad_maximum_fusion.1
  129.3 0.9 pad_maximum_fusion
  130.2 2.0 %collective-permute-start.10 = (bf16[2,8,128,128]{3,2,1,0:T(8,128)(2,1)}, bf16[2,8,128,128]{3,2,1,0:T(8,128)(2,1)S(1)}, u32[]{:S(2)}, u32[]{:S(2)}) collective-permute-start(bf16[2,8,128,128]{3,2,1,0:T(8,128)(2,1)} %pad_maximum_fusion), channel_id=1, source_target_pairs={{0,2},{1,3},{2,4},{3,5},{4,6},{5,7},{6,0},{7,1},{8,10},{9,11},{10,... | collective-permute-start | bytes 1572872 | tf_op jit(solution)/shard_map/ppermute | solution.py:36
  132.3 0.1 copy.14
  132.4 0.1 reshape.22.ids
  132.4 0.1 add_convert_fusion.edge
  132.5 1.1 slice.38
  133.6 5.1 %collective-permute-done.12 = bf16[2,8,128,128]{3,2,1,0:T(8,128)(2,1)S(1)} collective-permute-done((bf16[2,8,128,128]{3,2,1,0:T(8,128)(2,1)}, bf16[2,8,128,128]{3,2,1,0:T(8,128)(2,1)S(1)}, u32[]{:S(2)}, u32[]{:S(2)}) %collective-permute-start.12) | collective-permute-done | bytes 524320 | tf_op jit(solution)/shard_map/ppermute | solution.py:36
  138.7 2.1 %collective-permute-done.10 = bf16[2,8,128,128]{3,2,1,0:T(8,128)(2,1)S(1)} collective-permute-done((bf16[2,8,128,128]{3,2,1,0:T(8,128)(2,1)}, bf16[2,8,128,128]{3,2,1,0:T(8,128)(2,1)S(1)}, u32[]{:S(2)}, u32[]{:S(2)}) %collective-permute-start.10) | collective-permute-done | bytes 524320 | tf_op jit(solution)/shard_map/ppermute | solution.py:36
  140.9 0.0 copy-start.1
  140.9 3.4 %copy-done.1 = bf16[16,4,256,256]{3,2,1,0:T(8,128)(2,1)S(1)} copy-done((bf16[16,4,256,256]{3,2,1,0:T(8,128)(2,1)S(1)}, bf16[16,4,256,256]{3,2,1,0:T(8,128)(2,1)}, u32[]{:S(2)}) %copy-start.1) | copy-done | bytes 8388632
  144.2 1.6 copy-done.4
  145.8 17.1 %apply_leaves.1 = bf16[16,256,256]{2,1,0:T(8,128)(2,1)} custom-call(s32[64]{0:T(128)S(1)} %reshape.22.ids, s32[2]{0:T(128)S(1)} %add_convert_fusion.edge, bf16[16,4,256,256]{3,2,1,0:T(8,128)(2,1)S(1)} %copy-done.1, bf16[16,4,256,256]{3,2,1,0:T(8,128)(2,1)} %near_imag.1, bf16[16,2,256,128]{3,2,1,0:T(8,128)(2,1)S(1)} %copy-done.3, ...), custom_call_target="tpu_custom_call" | custom-call | flops 4600000000 | bytes 29360128 | tf_op jit(solution)/shard_map/apply_leaves/pallas_call | solution.py:169
  (32 shorter events, 0.3 us)
Async XLA Ops:
  0.0 92.7 %copy-start = (bf16[32,2,128,128]{3,2,1,0:T(8,128)(2,1)S(1)}, bf16[32,2,128,128]{3,2,1,0:T(8,128)(2,1)}, u32[]{:S(2)}) copy-start(bf16[32,2,128,128]{3,2,1,0:T(8,128)(2,1)} %param.9) | copy-start | bytes 6291460
  0.0 92.7 %copy-start.5 = (bf16[2,8,128,128]{3,2,1,0:T(8,128)(2,1)S(1)}, bf16[2,8,128,128]{3,2,1,0:T(8,128)(2,1)}, u32[]{:S(2)}) copy-start(bf16[2,8,128,128]{3,2,1,0:T(8,128)(2,1)} %t0.3) | copy-start | bytes 1572868
  0.0 89.4 %collective-permute-start.15 = (bf16[16,256,256]{2,1,0:T(8,128)(2,1)}, bf16[16,256,256]{2,1,0:T(8,128)(2,1)}, u32[]{:S(2)}, u32[]{:S(2)}) collective-permute-start(bf16[16,256,256]{2,1,0:T(8,128)(2,1)} %own.1), channel_id=1, source_target_pairs={{0,7},{7,0},{8,15},{15,8},{16,23},{23,16},{24,31},{31,24},{32,39},... | collective-permute-start | bytes 6291464 | tf_op jit(solution)/shard_map/ppermute | solution.py:36
  5.0 87.7 %copy-start.6 = (s32[2]{0:T(128)S(1)}, s32[2]{0:T(128)}, u32[]{:S(2)}) copy-start(s32[2]{0:T(128)} %pad_add_fusion.place) | copy-start | bytes 28
  54.6 11.6 %collective-permute-start.3 = (bf16[4,2,2,128,128]{4,3,2,1,0:T(8,128)(2,1)}, bf16[4,2,2,128,128]{4,3,2,1,0:T(8,128)(2,1)S(1)}, u32[]{:S(2)}, u32[]{:S(2)}) collective-permute-start(bf16[4,2,2,128,128]{4,3,2,1,0:T(8,128)(2,1)} %get-tuple-element.8), channel_id=1, source_target_pairs={{0,1},{1,0},{2,3},{3,2},{4,5},{5,4},{6,7},{7,6},{8,9},{9,8},{10,11... | collective-permute-start | bytes 1572872 | tf_op jit(solution)/shard_map/ppermute | solution.py:36
  54.7 16.9 %collective-permute-start.7 = (bf16[2,8,128,128]{3,2,1,0:T(8,128)(2,1)}, bf16[2,8,128,128]{3,2,1,0:T(8,128)(2,1)}, u32[]{:S(2)}, u32[]{:S(2)}) collective-permute-start(bf16[2,8,128,128]{3,2,1,0:T(8,128)(2,1)} %t0.3), channel_id=1, source_target_pairs={{0,72},{1,73},{2,74},{3,75},{4,76},{5,77},{6,78},{7,79},{8,64},{9,... | collective-permute-start | bytes 1572872 | tf_op jit(solution)/shard_map/ppermute | solution.py:36
  60.5 1.3 collective-permute-start
  60.7 3.8 %collective-permute-start.1 = (f32[2,4,2,2,8]{4,3,2,1,0:T(2,128)S(1)}, f32[2,4,2,2,8]{4,3,2,1,0:T(2,128)S(1)}, u32[]{:S(2)}, u32[]{:S(2)}) collective-permute-start(f32[2,4,2,2,8]{4,3,2,1,0:T(2,128)S(1)} %bitcast.61), channel_id=1, source_target_pairs={{0,8},{1,9},{2,10},{3,11},{4,12},{5,13},{6,14},{7,15},{8,0},{9,1},... | collective-permute-start | bytes 3080 | tf_op jit(solution)/shard_map/ppermute | solution.py:36
  61.7 3.2 %collective-permute-start.2 = (f32[2,4,2,2,8]{4,3,2,1,0:T(2,128)S(1)}, f32[2,4,2,2,8]{4,3,2,1,0:T(2,128)S(1)}, u32[]{:S(2)}, u32[]{:S(2)}) collective-permute-start(f32[2,4,2,2,8]{4,3,2,1,0:T(2,128)S(1)} %bitcast.60), channel_id=1, source_target_pairs={{0,9},{1,8},{2,11},{3,10},{4,13},{5,12},{6,15},{7,14},{8,1},{9,0},... | collective-permute-start | bytes 3080 | tf_op jit(solution)/shard_map/ppermute | solution.py:36
  64.6 15.2 %collective-permute-start.4 = (bf16[4,2,2,128,128]{4,3,2,1,0:T(8,128)(2,1)}, bf16[4,2,2,128,128]{4,3,2,1,0:T(8,128)(2,1)}, u32[]{:S(2)}, u32[]{:S(2)}) collective-permute-start(bf16[4,2,2,128,128]{4,3,2,1,0:T(8,128)(2,1)} %get-tuple-element.9), channel_id=1, source_target_pairs={{0,8},{1,9},{2,10},{3,11},{4,12},{5,13},{6,14},{7,15},{8,0},{9,1},... | collective-permute-start | bytes 1572872 | tf_op jit(solution)/shard_map/ppermute | solution.py:36
  64.9 23.2 %collective-permute-start.5 = (bf16[4,2,2,128,128]{4,3,2,1,0:T(8,128)(2,1)}, bf16[4,2,2,128,128]{4,3,2,1,0:T(8,128)(2,1)}, u32[]{:S(2)}, u32[]{:S(2)}) collective-permute-start(bf16[4,2,2,128,128]{4,3,2,1,0:T(8,128)(2,1)} %get-tuple-element.10), channel_id=1, source_target_pairs={{0,9},{1,8},{2,11},{3,10},{4,13},{5,12},{6,15},{7,14},{8,1},{9,0},... | collective-permute-start | bytes 1572872 | tf_op jit(solution)/shard_map/ppermute | solution.py:36
  66.2 26.5 %collective-permute-start.6 = (bf16[2,8,128,128]{3,2,1,0:T(8,128)(2,1)}, bf16[2,8,128,128]{3,2,1,0:T(8,128)(2,1)}, u32[]{:S(2)}, u32[]{:S(2)}) collective-permute-start(bf16[2,8,128,128]{3,2,1,0:T(8,128)(2,1)} %t0.3), channel_id=1, source_target_pairs={{0,1},{1,0},{2,3},{3,2},{4,5},{5,4},{6,7},{7,6},{8,9},{9,8},{10,11... | collective-permute-start | bytes 1572872 | tf_op jit(solution)/shard_map/ppermute | solution.py:36
  71.6 21.1 %collective-permute-start.8 = (bf16[2,8,128,128]{3,2,1,0:T(8,128)(2,1)}, bf16[2,8,128,128]{3,2,1,0:T(8,128)(2,1)}, u32[]{:S(2)}, u32[]{:S(2)}) collective-permute-start(bf16[2,8,128,128]{3,2,1,0:T(8,128)(2,1)} %collective-permute-done.7.t2), channel_id=1, source_target_pairs={{0,1},{1,0},{2,3},{3,2},{4,5},{5,4},{6,7},{7,6},{8,9},{9,8},{10,11... | collective-permute-start | bytes 1572872 | tf_op jit(solution)/shard_map/ppermute | solution.py:36
  79.7 61.1 %collective-permute-start.13 = (bf16[16,256,256]{2,1,0:T(8,128)(2,1)}, bf16[16,256,256]{2,1,0:T(8,128)(2,1)}, u32[]{:S(2)}, u32[]{:S(2)}) collective-permute-start(bf16[16,256,256]{2,1,0:T(8,128)(2,1)} %own.1), channel_id=1, source_target_pairs={{0,1},{1,2},{2,3},{3,4},{4,5},{5,6},{6,7},{8,9},{9,10},{10,11},{11... | collective-permute-start | bytes 6291464 | tf_op jit(solution)/shard_map/ppermute | solution.py:36
  88.1 52.7 %collective-permute-start.14 = (bf16[16,256,256]{2,1,0:T(8,128)(2,1)}, bf16[16,256,256]{2,1,0:T(8,128)(2,1)}, u32[]{:S(2)}, u32[]{:S(2)}) collective-permute-start(bf16[16,256,256]{2,1,0:T(8,128)(2,1)} %own.1), channel_id=1, source_target_pairs={{1,0},{2,1},{3,2},{4,3},{5,4},{6,5},{7,6},{9,8},{10,9},{11,10},{12... | collective-permute-start | bytes 6291464 | tf_op jit(solution)/shard_map/ppermute | solution.py:36
  89.4 51.4 %collective-permute-start.16 = (bf16[16,256,256]{2,1,0:T(8,128)(2,1)}, bf16[16,256,256]{2,1,0:T(8,128)(2,1)}, u32[]{:S(2)}, u32[]{:S(2)}) collective-permute-start(bf16[16,256,256]{2,1,0:T(8,128)(2,1)} %collective-permute-done.15), channel_id=1, source_target_pairs={{0,8},{8,16},{16,24},{24,32},{32,40},{40,48},{48,56},{56,64},{64,7... | collective-permute-start | bytes 6291464 | tf_op jit(solution)/shard_map/ppermute | solution.py:36
  96.4 31.9 %collective-permute-start.11 = (bf16[8,128,128]{2,1,0:T(8,128)(2,1)S(1)}, bf16[8,128,128]{2,1,0:T(8,128)(2,1)S(1)}, u32[]{:S(2)}, u32[]{:S(2)}) collective-permute-start(bf16[8,128,128]{2,1,0:T(8,128)(2,1)S(1)} %get-tuple-element.15), channel_id=1, source_target_pairs={{0,6},{1,7},{2,0},{3,1},{4,2},{5,3},{6,4},{7,5},{8,14},{9,15},{10,... | collective-permute-start | bytes 786440 | tf_op jit(solution)/shard_map/ppermute | solution.py:36
  98.8 29.6 %collective-permute-start.9 = (bf16[8,128,128]{2,1,0:T(8,128)(2,1)S(1)}, bf16[8,128,128]{2,1,0:T(8,128)(2,1)S(1)}, u32[]{:S(2)}, u32[]{:S(2)}) collective-permute-start(bf16[8,128,128]{2,1,0:T(8,128)(2,1)S(1)} %get-tuple-element.16), channel_id=1, source_target_pairs={{0,2},{1,3},{2,4},{3,5},{4,6},{5,7},{6,0},{7,1},{8,10},{9,11},{10,... | collective-permute-start | bytes 786440 | tf_op jit(solution)/shard_map/ppermute | solution.py:36
  107.2 23.0 %copy-start.2 = (bf16[3,2,8,128,128]{4,3,2,1,0:T(8,128)(2,1)}, bf16[3,2,8,128,128]{4,3,2,1,0:T(8,128)(2,1)S(1)}, u32[]{:S(2)}) copy-start(bf16[3,2,8,128,128]{4,3,2,1,0:T(8,128)(2,1)S(1)} %transfer_terms.2) | copy-start | bytes 4718596
  107.3 25.0 %copy-start.7 = (s32[16,4]{0,1:T(4,128)S(1)}, s32[16,4]{0,1:T(4,128)}, u32[]{:S(2)}) copy-start(s32[16,4]{0,1:T(4,128)} %param.15) | copy-start | bytes 772
  107.3 33.6 %copy-start.3 = (bf16[16,2,256,128]{3,2,1,0:T(8,128)(2,1)S(1)}, bf16[16,2,256,128]{3,2,1,0:T(8,128)(2,1)}, u32[]{:S(2)}) copy-start(bf16[16,2,256,128]{3,2,1,0:T(8,128)(2,1)} %basis.1) | copy-start | bytes 6291460
  129.3 9.4 %collective-permute-start.12 = (bf16[2,8,128,128]{3,2,1,0:T(8,128)(2,1)}, bf16[2,8,128,128]{3,2,1,0:T(8,128)(2,1)S(1)}, u32[]{:S(2)}, u32[]{:S(2)}) collective-permute-start(bf16[2,8,128,128]{3,2,1,0:T(8,128)(2,1)} %pad_maximum_fusion.1), channel_id=1, source_target_pairs={{0,6},{1,7},{2,0},{3,1},{4,2},{5,3},{6,4},{7,5},{8,14},{9,15},{10,... | collective-permute-start | bytes 1572872 | tf_op jit(solution)/shard_map/ppermute | solution.py:36
  130.2 10.6 %collective-permute-start.10 = (bf16[2,8,128,128]{3,2,1,0:T(8,128)(2,1)}, bf16[2,8,128,128]{3,2,1,0:T(8,128)(2,1)S(1)}, u32[]{:S(2)}, u32[]{:S(2)}) collective-permute-start(bf16[2,8,128,128]{3,2,1,0:T(8,128)(2,1)} %pad_maximum_fusion), channel_id=1, source_target_pairs={{0,2},{1,3},{2,4},{3,5},{4,6},{5,7},{6,0},{7,1},{8,10},{9,11},{10,... | collective-permute-start | bytes 1572872 | tf_op jit(solution)/shard_map/ppermute | solution.py:36
  140.9 3.4 %copy-start.1 = (bf16[16,4,256,256]{3,2,1,0:T(8,128)(2,1)S(1)}, bf16[16,4,256,256]{3,2,1,0:T(8,128)(2,1)}, u32[]{:S(2)}) copy-start(bf16[16,4,256,256]{3,2,1,0:T(8,128)(2,1)} %near_real.1) | copy-start | bytes 25165828
  144.2 1.6 copy-start.4

commit v2 on v0

v2 whole, which is shorter than its diff:
```python
import jax
import jax.numpy as jnp
from jax import lax
from jax.experimental import pallas as pl
from jax.experimental.pallas import tpu as pltpu
from jax.sharding import PartitionSpec as P

AXES = ("cluster", "cone")
DEVICES = 128
ROW = 8
F32 = jnp.float32
BF16 = jnp.bfloat16
SMALL = pl.CostEstimate(flops=0, bytes_accessed=1024, transcendentals=0)


def moved(dx):
    return [(d, (d & ~6) | ((((d >> 1) & 3) + dx) % 4) << 1) for d in range(DEVICES)]


FLIP_CORE = [(d, d ^ 1) for d in range(DEVICES)]
FLIP_Z = [(d, d ^ 8) for d in range(DEVICES)]
FLIP_BOTH = [(d, d ^ 9) for d in range(DEVICES)]
FLIP_OUTER = [(d, d ^ 72) for d in range(DEVICES)]
X_UP = moved(1)
X_DOWN = moved(-1)
UP = [(d, d + 1) for d in range(DEVICES) if d % ROW != ROW - 1]
DOWN = [(d, d - 1) for d in range(DEVICES) if d % ROW != 0]
WRAP = [(d, d ^ 7) for d in range(DEVICES) if d % ROW in (0, ROW - 1)]
NEXT_ROW = [(d, d + ROW) for d in range(0, DEVICES - ROW, ROW)] + [
    (d, d - ROW) for d in range(2 * ROW - 1, DEVICES, ROW)
]


def permute(array, pairs):
    return lax.ppermute(array, AXES, pairs)


IN_VMEM = pl.BlockSpec(memory_space=pltpu.VMEM)
IN_HBM = pl.BlockSpec(memory_space=pltpu.HBM)
IN_SMEM = pl.BlockSpec(memory_space=pltpu.SMEM)
ANYWHERE = pl.BlockSpec(memory_space=pl.ANY)


def kept_in_hbm(array):
    return pltpu.with_memory_space_constraint(array, pltpu.HBM)


def kept_in_vmem(array):
    return pltpu.with_memory_space_constraint(array, pltpu.VMEM)


def limit(mib):
    return pltpu.CompilerParams(vmem_limit_bytes=mib << 20)


def stage_kernel(coef, charges, *refs):
    outs, buffers, sems = refs[:5], refs[5:10], refs[10]
    cone = lax.axis_index("cone")
    zl, core = cone // 8, cone % 2
    sources = (
        coef.at[1 - zl, :, core],
        coef.at[1 - zl, :, 1 - core],
        coef.at[zl, :, 1 - core],
        coef.at[zl, :, core],
        charges,
    )
    loads = [pltpu.make_async_copy(sources[i], buffers[i], sems.at[0, i]) for i in range(5)]
    stores = [pltpu.make_async_copy(buffers[i], outs[i], sems.at[1, i]) for i in range(5)]
    for load in loads:
        load.start()
    for load, store in zip(loads, stores):
        load.wait()
        store.start()
    for store in stores:
        store.wait()


def stage(coef, charges):
    part = jax.ShapeDtypeStruct(coef.shape[1:2] + coef.shape[3:], coef.dtype)
    outs = (part,) * 4 + (jax.ShapeDtypeStruct(charges.shape, charges.dtype),)
    return pl.pallas_call(
        stage_kernel,
        out_shape=outs,
        in_specs=[IN_HBM, IN_HBM],
        out_specs=(IN_HBM,) * 5,
        scratch_shapes=[pltpu.VMEM(out.shape, out.dtype) for out in outs] + [pltpu.SemaphoreType.DMA((2, 5))],
        compiler_params=limit(6),
        cost_estimate=SMALL,
        name="stage",
    )(kept_in_hbm(coef), kept_in_hbm(charges))


def tied(array, *others):
    def kernel(*refs):
        del refs

    return pl.pallas_call(
        kernel,
        out_shape=jax.ShapeDtypeStruct(array.shape, array.dtype),
        in_specs=[ANYWHERE] * (1 + len(others)),
        out_specs=ANYWHERE,
        input_output_aliases={0: 0},
        cost_estimate=SMALL,
        name="tied",
    )(array, *others)


def transfer_kernel(count, ties, targets, cosines, sines, *refs):
    coefs, moves = refs[:4], refs[4:8]
    outs = refs[8 + ties : 8 + ties + 2 * count]
    coef_in, move_in, coef_sems, move_sems = refs[8 + ties + 2 * count :]
    width = outs[0].shape[-1]
    half = outs[0].shape[-2] // 2

    def coef_load(t, source):
        return pltpu.make_async_copy(coefs[source].at[targets[t]], coef_in.at[t, source], coef_sems.at[t, source])

    def move_load(part, source):
        octants = pl.ds(0, 2) if part == 0 else pl.ds(2, 6)
        return pltpu.make_async_copy(
            moves[source].at[:, octants], move_in.at[source, :, octants], move_sems.at[part, source]
        )

    for part in range(2):
        for source in range(4):
            if part < count:
                coef_load(part, source).start()
            move_load(part, source).start()
    for t in range(2, count):
        for source in range(4):
            coef_load(t, source).start()

    for t in range(count):
        for source in range(4):
            coef_load(t, source).wait()
        for o in range(8):
            if t == 0 and o in (0, 2):
                for source in range(4):
                    move_load(o // 2, source).wait()
            total = None
            for source in range(4):
                columns = []
                for j in range(2):
                    rows = []
                    for cone in range(2):
                        at = ((targets[t] * 2 + j) * 8 + source * 2 + cone) * 8 + o
                        cosine, sine = cosines[at], sines[at]
                        real = coef_in[t, source, j, cone, :half, :].astype(F32)
                        imag = coef_in[t, source, j, cone, half:, :].astype(F32)
                        rows.append((cosine * real - sine * imag).astype(BF16))
                        rows.append((sine * real + cosine * imag).astype(BF16))
                    columns.append(jnp.concatenate(rows, axis=0))
                turned = jnp.concatenate(columns, axis=1)
                matrix = jnp.concatenate([move_in[source, 0, o], move_in[source, 1, o]], axis=1)
                term = jnp.dot(matrix, turned, preferred_element_type=F32)
                total = term if total is None else total + term
            for j in range(2):
                outs[t * 2 + j][o] = total[:, j * width : (j + 1) * width].astype(BF16)


def transfer_terms(targets, cosines, sines, coefs, moves, ties=()):
    count = targets.shape[0]
    out = pltpu.VMEM((8,) + coefs[0].shape[-2:], BF16)

    def kernel(*refs):
        transfer_kernel(count, len(ties), *refs)

    return pl.pallas_call(
        kernel,
        out_shape=(out,) * (2 * count),
        in_specs=[IN_SMEM] * 3 + [IN_HBM] * 8 + [ANYWHERE] * len(ties),
        out_specs=(IN_VMEM,) * (2 * count),
        scratch_shapes=[
            pltpu.VMEM((count, 4) + coefs[0].shape[1:], BF16),
            pltpu.VMEM((4,) + moves[0].shape, BF16),
            pltpu.SemaphoreType.DMA((count, 4)),
            pltpu.SemaphoreType.DMA((2, 4)),
        ],
        compiler_params=limit(8),
        cost_estimate=SMALL,
        name="transfer_terms",
    )(targets, cosines, sines, *[kept_in_hbm(a) for a in coefs], *[kept_in_hbm(a) for a in moves], *ties)


def add_kernel(left, right, arrived, out):
    for o in range(8):
        out[0, o] = left[o]
        out[1, o] = (right[o].astype(F32) + arrived[o].astype(F32)).astype(BF16)


def with_arrived(left, right, arrived):
    return pl.pallas_call(
        add_kernel,
        out_shape=pltpu.VMEM((2,) + left.shape, BF16),
        in_specs=[IN_VMEM] * 3,
        out_specs=IN_VMEM,
        compiler_params=limit(2),
        cost_estimate=SMALL,
        name="with_arrived",
    )(left, right, kept_in_vmem(arrived))


def pair_term(real, imag, charge):
    points, columns = charge.shape[0], charge.shape[1] // 2
    both = jnp.dot(jnp.concatenate([real, imag], axis=0), charge, preferred_element_type=F32)
    first, second = both[:points], both[points:]
    return jnp.concatenate(
        [first[:, :columns] - second[:, columns:], first[:, columns:] + second[:, :columns]], axis=1
    )


GROUP = 4
AHEAD = 3
PAIRS = 64


SLOTS = (AHEAD + 1) * GROUP


def pair_scratch(points, wide):
    block = pltpu.VMEM((SLOTS, points, wide), BF16)
    return [block, block, block, pltpu.SemaphoreType.DMA((3, SLOTS))]


def listed_pairs(listed, ids, near_real, near_imag, charges_of, sums, reals, imags, charges, sems):
    length = listed[0]
    groups = (length + GROUP - 1) // GROUP

    def blocks(place):
        pair = listed[1 + place]
        leaf, n = pair // 4, pair % 4
        slot = lax.rem(place, SLOTS)
        return (
            pltpu.make_async_copy(near_real.at[leaf, n], reals.at[slot], sems.at[0, slot]),
            pltpu.make_async_copy(near_imag.at[leaf, n], imags.at[slot], sems.at[1, slot]),
        )

    def charge_load(source, place):
        slot = lax.rem(place, SLOTS)
        return pltpu.make_async_copy(source, charges.at[slot], sems.at[2, slot])

    def start(place):
        @pl.when(place < length)
        def _():
            for copy in blocks(place):
                copy.start()
            for case, source in charges_of(ids[listed[1 + place]]):

                @pl.when(case)
                def _():
                    charge_load(source, place).start()

    def finish(place):
        @pl.when(place < length)
        def _():
            for copy in blocks(place):
                copy.wait()
            _, source = charges_of(ids[listed[1 + place]])[0]
            charge_load(source, place).wait()

    for place in range(AHEAD * GROUP):
        start(place)

    @pl.loop(0, groups)
    def _(group):
        for i in range(GROUP):
            start((group + AHEAD) * GROUP + i)
        for i in range(GROUP):
            finish(group * GROUP + i)
        terms = []
        for i in range(GROUP):
            place = group * GROUP + i
            inside = place < length
            place = jnp.where(inside, place, length - 1)
            slot = lax.rem(place, SLOTS)
            charge = charges[slot]
            charge = jnp.where(inside, charge, jnp.zeros_like(charge))
            terms.append((listed[1 + place] // 4, pair_term(reals[slot], imags[slot], charge)))
        for leaf, term in terms:
            sums[leaf] += term


def own_kernel(ids, near_real, near_imag, basis, own, bases, sums, beside, wrapping, inner, basis_sem, *scratch):
    count = own.shape[0]
    load_basis = pltpu.make_async_copy(basis, bases, basis_sem)
    load_basis.start()
    at_row = lax.rem(lax.axis_index("cone"), ROW)

    for listed in (inner, beside, wrapping):
        listed[0] = 0

    @pl.loop(0, count * 4)
    def _(pair):
        at = ids[pair]
        low, high = at < count, at >= 2 * count
        wraps = (low & (at_row == 0)) | (high & (at_row == ROW - 1))

        def put(listed):
            length = listed[0] + 1
            listed[0] = length
            listed[length] = pair

        @pl.when(jnp.logical_not(low | high))
        def _():
            put(inner)

        @pl.when(wraps)
        def _():
            put(wrapping)

        @pl.when((low | high) & jnp.logical_not(wraps))
        def _():
            put(beside)

    @pl.loop(0, count)
    def _(leaf):
        sums[leaf] = jnp.zeros(sums.shape[1:], F32)

    def charges_of(at):
        return [(True, own.at[at - count])]

    listed_pairs(inner, ids, near_real, near_imag, charges_of, sums, *scratch)
    load_basis.wait()


def own_sums(ids, near_real, near_imag, basis, own):
    pairs = jax.ShapeDtypeStruct((1 + PAIRS,), jnp.int32)
    return pl.pallas_call(
        own_kernel,
        out_shape=(pltpu.VMEM(basis.shape, BF16), pltpu.VMEM(own.shape, F32), pairs, pairs),
        in_specs=[IN_SMEM] + [IN_HBM] * 4,
        out_specs=(IN_VMEM,) * 2 + (IN_SMEM,) * 2,
        scratch_shapes=[pltpu.SMEM(pairs.shape, jnp.int32), pltpu.SemaphoreType.DMA]
        + pair_scratch(*own.shape[1:]),
        compiler_params=limit(9),
        cost_estimate=SMALL,
        name="own_sums",
    )(ids, kept_in_hbm(near_real), kept_in_hbm(near_imag), kept_in_hbm(basis), kept_in_hbm(own))


def beside_kernel(ids, listed, near_real, near_imag, below, above, before, sums, *scratch):
    count = below.shape[0]
    del before

    def charges_of(at):
        inside = lax.rem(at, count)
        return [(at < count, below.at[inside]), (at >= count, above.at[inside])]

    listed_pairs(listed, ids, near_real, near_imag, charges_of, sums, *scratch)


def beside_sums(ids, listed, near_real, near_imag, below, above, sums):
    return pl.pallas_call(
        beside_kernel,
        out_shape=pltpu.VMEM(sums.shape, F32),
        in_specs=[IN_SMEM] * 2 + [IN_HBM] * 4 + [IN_VMEM],
        out_specs=IN_VMEM,
        input_output_aliases={6: 0},
        scratch_shapes=pair_scratch(*sums.shape[1:]),
        compiler_params=limit(9),
        cost_estimate=SMALL,
        name="beside_sums",
    )(ids, listed, kept_in_hbm(near_real), kept_in_hbm(near_imag), kept_in_hbm(below), kept_in_hbm(above), sums)


def apply_kernel(
    ids, listed, near_real, near_imag, wrapped, before, basis, leaf00, leaf01, leaf1, leaf2, out, sums, totals, store_sems, *scratch
):
    count = wrapped.shape[0]
    del before

    def charges_of(at):
        return [(True, wrapped.at[lax.rem(at, count)])]

    def store(leaf):
        return pltpu.make_async_copy(totals.at[leaf], out.at[leaf], store_sems.at[leaf])

    listed_pairs(listed, ids, near_real, near_imag, charges_of, sums, *scratch)
    for j, own in enumerate((leaf00, leaf01)):

        @pl.loop(0, count // 4)
        def _(half):
            for i in range(2):
                o = 2 * half + i
                leaf = j * (count // 2) + o
                coef = own[o].astype(F32) + leaf1[1 - j, o].astype(F32) + leaf2[j, o].astype(F32)
                coef = coef.astype(BF16)
                far = [jnp.dot(basis[leaf, s], coef, preferred_element_type=F32) for s in range(2)]
                totals[leaf] = (sums[leaf] + jnp.concatenate(far, axis=1)).astype(BF16)
                store(leaf).start()

    for leaf in range(count):
        store(leaf).wait()


def apply_leaves(ids, listed, near_real, near_imag, wrapped, sums, basis, leaf_terms):
    count = sums.shape[0]
    leaf_terms = leaf_terms[:2] + [kept_in_vmem(a) for a in leaf_terms[2:]]
    return pl.pallas_call(
        apply_kernel,
        out_shape=(jax.ShapeDtypeStruct(sums.shape, BF16), pltpu.VMEM(sums.shape, F32)),
        in_specs=[IN_SMEM] * 2 + [IN_HBM] * 3 + [IN_VMEM] * 6,
        out_specs=(IN_HBM, IN_VMEM),
        input_output_aliases={5: 1},
        scratch_shapes=[pltpu.VMEM(sums.shape, BF16), pltpu.SemaphoreType.DMA((count,))]
        + pair_scratch(*sums.shape[1:]),
        compiler_params=limit(11),
        cost_estimate=SMALL,
        name="apply_leaves",
    )(ids, listed, kept_in_hbm(near_real), kept_in_hbm(near_imag), kept_in_hbm(wrapped), sums, basis, *leaf_terms)[0]


def per_device(
    upper_coef, phase, cone_used, transfer, leaf_basis, charges, neighbours, near_real, near_imag
):
    leaf_count = charges.shape[0]
    cluster, cone = lax.axis_index("cluster"), lax.axis_index("cone")
    zl, x, core = cone // 8, (cone // 2) % 4, cone % 2

    coef = upper_coef.reshape((2, 4, 2, 2) + upper_coef.shape[1:])
    to_z, to_both, to_core, kept, staged = stage(coef, charges)
    from_z = permute(to_z, FLIP_Z)
    from_both = permute(to_both, FLIP_BOTH)
    from_core = permute(to_core, FLIP_CORE)

    weight = cone_used.astype(F32)[..., None]
    turn = jnp.stack([jnp.cos(phase) * weight, jnp.sin(phase) * weight])
    turn = turn.reshape((2, 2, 4, 2, 2) + turn.shape[2:])

    def turn_of(z, c):
        return turn[:, z, :, c]

    turns = [
        turn_of(zl, core),
        permute(turn_of(zl, 1 - core), FLIP_CORE),
        permute(turn_of(1 - zl, core), FLIP_Z),
        permute(turn_of(1 - zl, 1 - core), FLIP_BOTH),
    ]
    staged = tied(staged, *turns[1:])
    turns = jnp.stack(turns, axis=3)
    cosines, sines = turns[0].reshape(-1), turns[1].reshape(-1)

    transfer_outer = permute(transfer, FLIP_OUTER)
    moves = [transfer, permute(transfer, FLIP_CORE), transfer_outer, permute(transfer_outer, FLIP_CORE)]
    coefs = [kept, from_core, from_z, from_both]

    first_leaf = (cluster * 16 + cone) * leaf_count
    ids = (neighbours - first_leaf + leaf_count).reshape(-1)
    basis, sums, beside, wrapping = own_sums(ids, near_real, near_imag, leaf_basis, staged)

    below = permute(staged, UP)
    above = permute(staged, DOWN)
    crossed = tied(permute(staged, WRAP), from_z, from_both, transfer_outer, beside)
    wrapped = permute(crossed, NEXT_ROW)

    def terms(offsets, ties=()):
        targets = jnp.stack([(x + offset) % 4 for offset in offsets]).astype(jnp.int32)
        return transfer_terms(targets, cosines, sines, coefs, moves, ties)

    far_first, far_second = terms([2], [beside])
    up = permute(far_first, X_UP)
    down = permute(far_second, X_DOWN)
    up_first, up_second, down_first, down_second, own_first, own_second = terms([1, 3, 0], [below, above])
    from_below = permute(with_arrived(up_second, up_first, up), X_UP)
    from_above = permute(with_arrived(down_first, down_second, down), X_DOWN)
    sums = beside_sums(ids, beside, near_real, near_imag, below, above, sums)
    leaf_terms = [own_first, own_second, from_below, from_above]
    return apply_leaves(ids, wrapping, near_real, near_imag, wrapped, sums, basis, leaf_terms)


def solution(mesh):
    in_specs = (
        P("cluster", "cone", None, None),
        P("cluster", "cone", None),
        P("cluster", "cone"),
        P("cone", None, None, None),
        P(("cluster", "cone"), None, None, None),
        P(("cluster", "cone"), None, None),
        P(("cluster", "cone"), None),
        P(("cluster", "cone"), None, None, None),
        P(("cluster", "cone"), None, None, None),
    )
    out_specs = P(("cluster", "cone"), None, None)
    return jax.shard_map(
        per_device, mesh=mesh, in_specs=in_specs, out_specs=out_specs, check_vma=False
    )
```

time: 198 us -> 96.7 us (0.49)
  the two profiles are of different devices: /device:TPU:63 before, /device:TPU:7 now
where the time goes in v2:
time: 96.7 us
  Pallas kernels  38.3 us (40%)
  starting transfers between devices  28.2 us (29%)
  waiting for transfers between devices  19.4 us (20%)
  local copies, waits for them, and re-layouts  9.44 us (10%)
  other arithmetic  0.99 us (1%)
    ppermute x17, starting transfers between devices, permute(): return lax.ppermute(array, AXES, pairs)  28.2 us
    ppermute x17, waiting for transfers between devices, permute(): return lax.ppermute(array, AXES, pairs)  19.4 us
    pallas_call x2, Pallas kernels, transfer_terms(): pl.pallas_call(kernel, out_shape=(out,) * (2 * count), in_specs=[IN_SMEM]...  12.3 us
    pallas_call x1, Pallas kernels, own_sums(): pl.pallas_call(own_kernel, out_shape=(pltpu.VMEM(basis.shape, BF16), pltp...  11.3 us
    unnamed x39, local copies, waits for them, and re-layouts  8.99 us
    pallas_call x1, Pallas kernels, apply_leaves(): pl.pallas_call(apply_kernel, out_shape=(jax.ShapeDtypeStruct(sums.shape,...  7.69 us
    pallas_call x1, Pallas kernels, beside_sums(): pl.pallas_call(beside_kernel, out_shape=pltpu.VMEM(sums.shape, F32), in_s...  4.23 us
    pallas_call x1, Pallas kernels, stage(): pl.pallas_call(stage_kernel, out_shape=outs, in_specs=[IN_HBM, IN_HBM], o...  2.68 us
  transfers between devices with their start and end apart: 17, of which 5 were waited for; matrix products, arithmetic and copies ran while one was open for 1% of the time, Pallas kernels for 32%

profile of v2, /device:TPU:7, one launch (start us, length us, event | category | flops | bytes accessed | tf_op | source)
XLA Modules:
  0.0 96.7 jit_solution(3148697984435058738)
XLA Ops:
  0.0 0.8 copy.18
  0.8 0.7 convert_element_type.3
  1.5 0.1 sine_multiply_fusion
  1.7 0.8 collective-permute-start
  2.5 1.7 %collective-permute-start.1 = (f32[2,4,2,2,8]{4,3,2,1,0:T(2,128)S(1)}, f32[2,4,2,2,8]{4,3,2,1,0:T(2,128)S(1)}, u32[]{:S(2)}, u32[]{:S(2)}) collective-permute-start(f32[2,4,2,2,8]{4,3,2,1,0:T(2,128)S(1)} %bitcast.30), channel_id=1, source_target_pairs={{0,8},{1,9},{2,10},{3,11},{4,12},{5,13},{6,14},{7,15},{8,0},{9,1},... | collective-permute-start | bytes 3080 | tf_op jit(solution)/shard_map/ppermute | solution.py:35
  4.2 0.1 collective-permute-start.2
  4.3 2.7 %stage.1 = (bf16[4,2,2,128,128]{4,3,2,1,0:T(8,128)(2,1)}, bf16[4,2,2,128,128]{4,3,2,1,0:T(8,128)(2,1)S(1)}, bf16[4,2,2,128,128]{4,3,2,1,0:T(8,128)(2,1)S(1)}, bf...) custom-call(bf16[2,4,2,2,2,128,128]{6,5,4,3,2,1,0:T(8,128)(2,1)} %bitcast.22, bf16[16,256,256]{2,1,0:T(8,128)(2,1)} %charges.1), custom_call_target="tpu_custom_call" | custom-call | bytes 1024 | tf_op jit(solution)/shard_map/stage/pallas_call | solution.py:81
  7.0 0.0 copy-start.2
  7.0 1.3 %copy-done.2 = bf16[16,256,256]{2,1,0:T(8,128)(2,1)} copy-done((bf16[16,256,256]{2,1,0:T(8,128)(2,1)}, bf16[16,256,256]{2,1,0:T(8,128)(2,1)S(1)}, u32[]{:S(2)}) %copy-start.2) | copy-done | bytes 2097176
  8.3 0.8 copy-done.6
  9.1 0.6 copy-done.12
  9.7 0.0 copy-done.14
  9.7 0.0 copy-done.16
  9.7 2.5 %collective-permute-start.3 = (bf16[16,256,256]{2,1,0:T(8,128)(2,1)}, bf16[16,256,256]{2,1,0:T(8,128)(2,1)}, u32[]{:S(2)}, u32[]{:S(2)}) collective-permute-start(bf16[16,256,256]{2,1,0:T(8,128)(2,1)} %tied.2.own), channel_id=1, source_target_pairs={{0,7},{7,0},{8,15},{15,8},{16,23},{23,16},{24,31},{31,24},{32,39},... | collective-permute-start | bytes 6291464 | tf_op jit(solution)/shard_map/ppermute | solution.py:35
  12.2 1.5 %collective-permute-start.4 = (bf16[4,2,2,128,128]{4,3,2,1,0:T(8,128)(2,1)}, bf16[4,2,2,128,128]{4,3,2,1,0:T(8,128)(2,1)}, u32[]{:S(2)}, u32[]{:S(2)}) collective-permute-start(bf16[4,2,2,128,128]{4,3,2,1,0:T(8,128)(2,1)} %get-tuple-element.25), channel_id=1, source_target_pairs={{0,8},{1,9},{2,10},{3,11},{4,12},{5,13},{6,14},{7,15},{8,0},{9,1},... | collective-permute-start | bytes 1572872 | tf_op jit(solution)/shard_map/ppermute | solution.py:35
  13.8 1.3 %collective-permute-start.8 = (bf16[16,256,256]{2,1,0:T(8,128)(2,1)}, bf16[16,256,256]{2,1,0:T(8,128)(2,1)S(1)}, u32[]{:S(2)}, u32[]{:S(2)}) collective-permute-start(bf16[16,256,256]{2,1,0:T(8,128)(2,1)} %tied.2.own), channel_id=1, source_target_pairs={{0,1},{1,2},{2,3},{3,4},{4,5},{5,6},{6,7},{8,9},{9,10},{10,11},{11... | collective-permute-start | bytes 6291464 | tf_op jit(solution)/shard_map/ppermute | solution.py:35
  15.0 4.4 %collective-permute-start.9 = (bf16[16,256,256]{2,1,0:T(8,128)(2,1)}, bf16[16,256,256]{2,1,0:T(8,128)(2,1)}, u32[]{:S(2)}, u32[]{:S(2)}) collective-permute-start(bf16[16,256,256]{2,1,0:T(8,128)(2,1)} %tied.2.own), channel_id=1, source_target_pairs={{1,0},{2,1},{3,2},{4,3},{5,4},{6,5},{7,6},{9,8},{10,9},{11,10},{12... | collective-permute-start | bytes 6291464 | tf_op jit(solution)/shard_map/ppermute | solution.py:35
  19.5 0.1 collective-permute-start.5
  19.6 6.6 %collective-permute-done.4.refs_1_.refs_5_ = bf16[4,2,2,128,128]{4,3,2,1,0:T(8,128)(2,1)} collective-permute-done((bf16[4,2,2,128,128]{4,3,2,1,0:T(8,128)(2,1)}, bf16[4,2,2,128,128]{4,3,2,1,0:T(8,128)(2,1)}, u32[]{:S(2)}, u32[]{:S(2)}) %collective-permute-start.4) | collective-permute-done | bytes 524320 | tf_op jit(solution)/shard_map/ppermute | solution.py:35
  26.2 3.6 %collective-permute-start.6 = (bf16[2,8,128,128]{3,2,1,0:T(8,128)(2,1)}, bf16[2,8,128,128]{3,2,1,0:T(8,128)(2,1)}, u32[]{:S(2)}, u32[]{:S(2)}) collective-permute-start(bf16[2,8,128,128]{3,2,1,0:T(8,128)(2,1)} %refs_7_.3), channel_id=1, source_target_pairs={{0,72},{1,73},{2,74},{3,75},{4,76},{5,77},{6,78},{7,79},{8,64},{9,... | collective-permute-start | bytes 1572872 | tf_op jit(solution)/shard_map/ppermute | solution.py:35
  29.8 0.1 copy.17
  29.9 0.1 reshape.12.ids
  30.0 11.3 %own_sums.1 = (bf16[16,2,256,128]{3,2,1,0:T(8,128)(2,1)S(1)}, f32[16,256,256]{2,1,0:T(8,128)S(1)}, s32[65]{0:T(128)S(1)}, s32[65]{0:T(128)S(1)}) custom-call(s32[64]{0:T(128)S(1)} %reshape.12.ids, bf16[16,4,256,256]{3,2,1,0:T(8,128)(2,1)} %near_real.5, bf16[16,4,256,256]{3,2,1,0:T(8,128)(2,1)} %near_imag.5, bf16[16,2,256,128]{3,2,1,0:T(8,128)(2,1)} %basis.1, ...), custom_call_target="tpu_custom_call" | custom-call | bytes 1024 | tf_op jit(solution)/shard_map/own_sums/pallas_call | solution.py:328
  41.3 2.0 %copy-done = f32[16,256,256]{2,1,0:T(8,128)} copy-done((f32[16,256,256]{2,1,0:T(8,128)}, f32[16,256,256]{2,1,0:T(8,128)S(1)}, u32[]{:S(2)}) %copy-start) | copy-done | bytes 4194328
  43.2 1.4 %copy-done.4 = bf16[16,2,256,128]{3,2,1,0:T(8,128)(2,1)} copy-done((bf16[16,2,256,128]{3,2,1,0:T(8,128)(2,1)}, bf16[16,2,256,128]{3,2,1,0:T(8,128)(2,1)S(1)}, u32[]{:S(2)}) %copy-start.4) | copy-done | bytes 2097176
  44.6 0.5 copy-done.7
  45.2 0.0 copy-start.9
  45.2 1.4 %collective-permute-start.7 = (bf16[16,256,256]{2,1,0:T(8,128)(2,1)}, bf16[16,256,256]{2,1,0:T(8,128)(2,1)}, u32[]{:S(2)}, u32[]{:S(2)}) collective-permute-start(bf16[16,256,256]{2,1,0:T(8,128)(2,1)} %tied.3), channel_id=1, source_target_pairs={{0,8},{8,16},{16,24},{24,32},{32,40},{40,48},{48,56},{56,64},{64,7... | collective-permute-start | bytes 6291464 | tf_op jit(solution)/shard_map/ppermute | solution.py:35
  46.7 2.3 %collective-permute-start.10 = (bf16[4,2,2,128,128]{4,3,2,1,0:T(8,128)(2,1)S(1)}, bf16[4,2,2,128,128]{4,3,2,1,0:T(8,128)(2,1)S(1)}, u32[]{:S(2)}, u32[]{:S(2)}) collective-permute-start(bf16[4,2,2,128,128]{4,3,2,1,0:T(8,128)(2,1)S(1)} %get-tuple-element.31), channel_id=1, source_target_pairs={{0,1},{1,0},{2,3},{3,2},{4,5},{5,4},{6,7},{7,6},{8,9},{9,8},{10,11... | collective-permute-start | bytes 1572872 | tf_op jit(solution)/shard_map/ppermute | solution.py:35
  49.0 2.2 %collective-permute-done.10.refs_4_ = bf16[4,2,2,128,128]{4,3,2,1,0:T(8,128)(2,1)S(1)} collective-permute-done((bf16[4,2,2,128,128]{4,3,2,1,0:T(8,128)(2,1)S(1)}, bf16[4,2,2,128,128]{4,3,2,1,0:T(8,128)(2,1)S(1)}, u32[]{:S(2)}, u32[]{:S(2)}) %collective-permute-start.10) | collective-permute-done | bytes 524320 | tf_op jit(solution)/shard_map/ppermute | solution.py:35
  51.2 0.8 copy-done.10
  52.0 0.4 collective-permute-start.12
  52.5 0.1 reshape_squeeze.6.refs_1_
  52.6 0.1 reshape_squeeze.7.refs_2_
  52.7 1.4 %collective-permute-done.12.refs_10_ = bf16[2,8,128,128]{3,2,1,0:T(8,128)(2,1)S(1)} collective-permute-done((bf16[2,8,128,128]{3,2,1,0:T(8,128)(2,1)}, bf16[2,8,128,128]{3,2,1,0:T(8,128)(2,1)S(1)}, u32[]{:S(2)}, u32[]{:S(2)}) %collective-permute-start.12) | collective-permute-done | bytes 524320 | tf_op jit(solution)/shard_map/ppermute | solution.py:35
  54.1 0.8 copy-done.11
  54.9 4.1 %transfer_terms.3 = (bf16[8,128,128]{2,1,0:T(8,128)(2,1)S(1)}, bf16[8,128,128]{2,1,0:T(8,128)(2,1)S(1)}) custom-call(s32[1]{0:T(128)} %bitcast.13.refs_0_, f32[512]{0:T(512)S(1)} %reshape_squeeze.6.refs_1_, f32[512]{0:T(512)S(1)} %reshape_squeeze.7.refs_2_, bf16[4,2,2,128,128]{4,3,2,1,0:T(8,128)(2,1)} %copy-done.6, bf16[4,2,2,128,128]{4,3,2,1,0:T(8,128)(2,1)} %copy-done.10, ...), custom_call_target="tpu_custom_call" | custom-call | bytes 1024 | tf_op jit(solution)/shard_map/transfer_terms/pallas_call | solution.py:168
  59.0 5.3 %collective-permute-start.13 = (bf16[8,128,128]{2,1,0:T(8,128)(2,1)S(1)}, bf16[8,128,128]{2,1,0:T(8,128)(2,1)S(1)}, u32[]{:S(2)}, u32[]{:S(2)}) collective-permute-start(bf16[8,128,128]{2,1,0:T(8,128)(2,1)S(1)} %get-tuple-element.36), channel_id=1, source_target_pairs={{0,2},{1,3},{2,4},{3,5},{4,6},{5,7},{6,0},{7,1},{8,10},{9,11},{10,... | collective-permute-start | bytes 786440 | tf_op jit(solution)/shard_map/ppermute | solution.py:35
  64.3 0.1 pad_add_fusion.refs_0_
  64.4 8.2 %transfer_terms.2 = (bf16[8,128,128]{2,1,0:T(8,128)(2,1)S(1)}, bf16[8,128,128]{2,1,0:T(8,128)(2,1)S(1)}, bf16[8,128,128]{2,1,0:T(8,128)(2,1)S(1)}, bf16[8,128,12...) custom-call(s32[3]{0:T(128)S(1)} %pad_add_fusion.refs_0_, ...), custom_call_target="tpu_custom_call" | custom-call | bytes 1024 | tf_op jit(solution)/shard_map/transfer_terms/pallas_call | solution.py:168
  72.6 0.1 with_arrived.2
  72.7 2.7 %collective-permute-start.14 = (bf16[2,8,128,128]{3,2,1,0:T(8,128)(2,1)S(1)}, bf16[2,8,128,128]{3,2,1,0:T(8,128)(2,1)S(1)}, u32[]{:S(2)}, u32[]{:S(2)}) collective-permute-start(bf16[2,8,128,128]{3,2,1,0:T(8,128)(2,1)S(1)} %with_arrived.2), channel_id=1, source_target_pairs={{0,2},{1,3},{2,4},{3,5},{4,6},{5,7},{6,0},{7,1},{8,10},{9,11},{10,... | collective-permute-start | bytes 1572872 | tf_op jit(solution)/shard_map/ppermute | solution.py:35
  75.4 0.1 with_arrived.3
  75.5 0.1 collective-permute-start.16
  75.6 4.2 %beside_sums.1.before = f32[16,256,256]{2,1,0:T(8,128)S(1)} custom-call(s32[64]{0:T(128)S(1)} %reshape.12.ids, s32[65]{0:T(128)S(1)} %copy-done.8, bf16[16,4,256,256]{3,2,1,0:T(8,128)(2,1)} %near_real.5, bf16[16,4,256,256]{3,2,1,0:T(8,128)(2,1)} %near_imag.5, bf16[16,256,256]{2,1,0:T(8,128)(2,1)} %copy-done.3, ...), custom_call_target="tpu_custom_call", output_to_operand_aliasing={{}: (6, {})} | custom-call | bytes 1024 | tf_op jit(solution)/shard_map/beside_sums/pallas_call | solution.py:353
  79.8 5.9 %collective-permute-done.14.leaf1 = bf16[2,8,128,128]{3,2,1,0:T(8,128)(2,1)S(1)} collective-permute-done((bf16[2,8,128,128]{3,2,1,0:T(8,128)(2,1)S(1)}, bf16[2,8,128,128]{3,2,1,0:T(8,128)(2,1)S(1)}, u32[]{:S(2)}, u32[]{:S(2)}) %collective-permute-start.14) | collective-permute-done | bytes 524320 | tf_op jit(solution)/shard_map/ppermute | solution.py:35
  85.7 3.3 %collective-permute-done.16.leaf2 = bf16[2,8,128,128]{3,2,1,0:T(8,128)(2,1)S(1)} collective-permute-done((bf16[2,8,128,128]{3,2,1,0:T(8,128)(2,1)S(1)}, bf16[2,8,128,128]{3,2,1,0:T(8,128)(2,1)S(1)}, u32[]{:S(2)}, u32[]{:S(2)}) %collective-permute-start.16) | collective-permute-done | bytes 524320 | tf_op jit(solution)/shard_map/ppermute | solution.py:35
  89.0 7.7 %apply_leaves.1 = (bf16[16,256,256]{2,1,0:T(8,128)(2,1)}, f32[16,256,256]{2,1,0:T(8,128)S(1)}) custom-call(s32[64]{0:T(128)S(1)} %reshape.12.ids, s32[65]{0:T(128)S(1)} %get-tuple-element.24.listed, bf16[16,4,256,256]{3,2,1,0:T(8,128)(2,1)} %near_real.5, bf16[16,4,256,256]{3,2,1,0:T(8,128)(2,1)} %near_imag.5, ...), custom_call_target="tpu_custom_call", output_to_operand_aliasing={{1}: (5, {})} | custom-call | bytes 1024 | tf_op jit(solution)/shard_map/apply_leaves/pallas_call | solution.py:399
  (52 shorter events, 0.2 us)
Async XLA Ops:
  1.7 7.4 %collective-permute-start = (f32[2,4,2,2,8]{4,3,2,1,0:T(2,128)S(1)}, f32[2,4,2,2,8]{4,3,2,1,0:T(2,128)S(1)}, u32[]{:S(2)}, u32[]{:S(2)}) collective-permute-start(f32[2,4,2,2,8]{4,3,2,1,0:T(2,128)S(1)} %bitcast.29), channel_id=1, source_target_pairs={{0,1},{1,0},{2,3},{3,2},{4,5},{5,4},{6,7},{7,6},{8,9},{9,8},{10,11... | collective-permute-start | bytes 3080 | tf_op jit(solution)/shard_map/ppermute | solution.py:35
  2.5 6.7 %collective-permute-start.1 = (f32[2,4,2,2,8]{4,3,2,1,0:T(2,128)S(1)}, f32[2,4,2,2,8]{4,3,2,1,0:T(2,128)S(1)}, u32[]{:S(2)}, u32[]{:S(2)}) collective-permute-start(f32[2,4,2,2,8]{4,3,2,1,0:T(2,128)S(1)} %bitcast.30), channel_id=1, source_target_pairs={{0,8},{1,9},{2,10},{3,11},{4,12},{5,13},{6,14},{7,15},{8,0},{9,1},... | collective-permute-start | bytes 3080 | tf_op jit(solution)/shard_map/ppermute | solution.py:35
  4.2 4.9 %collective-permute-start.2 = (f32[2,4,2,2,8]{4,3,2,1,0:T(2,128)S(1)}, f32[2,4,2,2,8]{4,3,2,1,0:T(2,128)S(1)}, u32[]{:S(2)}, u32[]{:S(2)}) collective-permute-start(f32[2,4,2,2,8]{4,3,2,1,0:T(2,128)S(1)} %bitcast.31), channel_id=1, source_target_pairs={{0,9},{1,8},{2,11},{3,10},{4,13},{5,12},{6,15},{7,14},{8,1},{9,0},... | collective-permute-start | bytes 3080 | tf_op jit(solution)/shard_map/ppermute | solution.py:35
  7.0 1.3 %copy-start.2 = (bf16[16,256,256]{2,1,0:T(8,128)(2,1)}, bf16[16,256,256]{2,1,0:T(8,128)(2,1)S(1)}, u32[]{:S(2)}) copy-start(bf16[16,256,256]{2,1,0:T(8,128)(2,1)S(1)} %get-tuple-element.23.refs_0_) | copy-start | bytes 6291460
  8.3 0.8 copy-start.6
  9.1 0.6 copy-start.12
  9.1 0.6 copy-start.14
  9.1 0.6 copy-start.16
  9.7 20.1 %copy-start.18 = (s32[16,4]{0,1:T(4,128)S(1)}, s32[16,4]{0,1:T(4,128)}, u32[]{:S(2)}) copy-start(s32[16,4]{0,1:T(4,128)} %param.15) | copy-start | bytes 772
  9.7 35.4 %collective-permute-start.3 = (bf16[16,256,256]{2,1,0:T(8,128)(2,1)}, bf16[16,256,256]{2,1,0:T(8,128)(2,1)}, u32[]{:S(2)}, u32[]{:S(2)}) collective-permute-start(bf16[16,256,256]{2,1,0:T(8,128)(2,1)} %tied.2.own), channel_id=1, source_target_pairs={{0,7},{7,0},{8,15},{15,8},{16,23},{23,16},{24,31},{31,24},{32,39},... | collective-permute-start | bytes 6291464 | tf_op jit(solution)/shard_map/ppermute | solution.py:35
  12.2 14.0 %collective-permute-start.4 = (bf16[4,2,2,128,128]{4,3,2,1,0:T(8,128)(2,1)}, bf16[4,2,2,128,128]{4,3,2,1,0:T(8,128)(2,1)}, u32[]{:S(2)}, u32[]{:S(2)}) collective-permute-start(bf16[4,2,2,128,128]{4,3,2,1,0:T(8,128)(2,1)} %get-tuple-element.25), channel_id=1, source_target_pairs={{0,8},{1,9},{2,10},{3,11},{4,12},{5,13},{6,14},{7,15},{8,0},{9,1},... | collective-permute-start | bytes 1572872 | tf_op jit(solution)/shard_map/ppermute | solution.py:35
  13.8 50.6 %collective-permute-start.8 = (bf16[16,256,256]{2,1,0:T(8,128)(2,1)}, bf16[16,256,256]{2,1,0:T(8,128)(2,1)S(1)}, u32[]{:S(2)}, u32[]{:S(2)}) collective-permute-start(bf16[16,256,256]{2,1,0:T(8,128)(2,1)} %tied.2.own), channel_id=1, source_target_pairs={{0,1},{1,2},{2,3},{3,4},{4,5},{5,6},{6,7},{8,9},{9,10},{10,11},{11... | collective-permute-start | bytes 6291464 | tf_op jit(solution)/shard_map/ppermute | solution.py:35
  15.0 49.3 %collective-permute-start.9 = (bf16[16,256,256]{2,1,0:T(8,128)(2,1)}, bf16[16,256,256]{2,1,0:T(8,128)(2,1)}, u32[]{:S(2)}, u32[]{:S(2)}) collective-permute-start(bf16[16,256,256]{2,1,0:T(8,128)(2,1)} %tied.2.own), channel_id=1, source_target_pairs={{1,0},{2,1},{3,2},{4,3},{5,4},{6,5},{7,6},{9,8},{10,9},{11,10},{12... | collective-permute-start | bytes 6291464 | tf_op jit(solution)/shard_map/ppermute | solution.py:35
  19.5 25.7 %collective-permute-start.5 = (bf16[4,2,2,128,128]{4,3,2,1,0:T(8,128)(2,1)S(1)}, bf16[4,2,2,128,128]{4,3,2,1,0:T(8,128)(2,1)}, u32[]{:S(2)}, u32[]{:S(2)}) collective-permute-start(bf16[4,2,2,128,128]{4,3,2,1,0:T(8,128)(2,1)S(1)} %get-tuple-element.26), channel_id=1, source_target_pairs={{0,9},{1,8},{2,11},{3,10},{4,13},{5,12},{6,15},{7,14},{8,1},{9,0},... | collective-permute-start | bytes 1572872 | tf_op jit(solution)/shard_map/ppermute | solution.py:35
  26.2 19.0 %collective-permute-start.6 = (bf16[2,8,128,128]{3,2,1,0:T(8,128)(2,1)}, bf16[2,8,128,128]{3,2,1,0:T(8,128)(2,1)}, u32[]{:S(2)}, u32[]{:S(2)}) collective-permute-start(bf16[2,8,128,128]{3,2,1,0:T(8,128)(2,1)} %refs_7_.3), channel_id=1, source_target_pairs={{0,72},{1,73},{2,74},{3,75},{4,76},{5,77},{6,78},{7,79},{8,64},{9,... | collective-permute-start | bytes 1572872 | tf_op jit(solution)/shard_map/ppermute | solution.py:35
  41.2 2.0 %copy-start = (f32[16,256,256]{2,1,0:T(8,128)}, f32[16,256,256]{2,1,0:T(8,128)S(1)}, u32[]{:S(2)}) copy-start(f32[16,256,256]{2,1,0:T(8,128)S(1)} %get-tuple-element.28.before) | copy-start | bytes 12582916
  43.2 1.4 %copy-start.4 = (bf16[16,2,256,128]{3,2,1,0:T(8,128)(2,1)}, bf16[16,2,256,128]{3,2,1,0:T(8,128)(2,1)S(1)}, u32[]{:S(2)}) copy-start(bf16[16,2,256,128]{3,2,1,0:T(8,128)(2,1)S(1)} %get-tuple-element.29.basis) | copy-start | bytes 6291460
  44.6 0.5 copy-start.7
  45.2 3.8 %copy-start.9 = (bf16[2,8,128,128]{3,2,1,0:T(8,128)(2,1)S(1)}, bf16[2,8,128,128]{3,2,1,0:T(8,128)(2,1)}, u32[]{:S(2)}) copy-start(bf16[2,8,128,128]{3,2,1,0:T(8,128)(2,1)} %refs_7_.3) | copy-start | bytes 1572868
  45.2 7.2 %copy-start.13 = (f32[2,4,2,2,8]{4,3,2,1,0:T(2,128)S(1)}, f32[2,4,2,2,8]{4,3,2,1,0:T(2,128)}, u32[]{:S(2)}) copy-start(f32[2,4,2,2,8]{4,3,2,1,0:T(2,128)} %copy-done.12) | copy-start | bytes 3076
  45.2 7.2 %copy-start.15 = (f32[2,4,2,2,8]{4,3,2,1,0:T(2,128)S(1)}, f32[2,4,2,2,8]{4,3,2,1,0:T(2,128)}, u32[]{:S(2)}) copy-start(f32[2,4,2,2,8]{4,3,2,1,0:T(2,128)} %copy-done.14) | copy-start | bytes 3076
  45.2 7.2 %copy-start.17 = (f32[2,4,2,2,8]{4,3,2,1,0:T(2,128)S(1)}, f32[2,4,2,2,8]{4,3,2,1,0:T(2,128)}, u32[]{:S(2)}) copy-start(f32[2,4,2,2,8]{4,3,2,1,0:T(2,128)} %copy-done.16) | copy-start | bytes 3076
  45.2 9.7 %copy-start.8 = (s32[65]{0:T(128)S(1)}, s32[65]{0:T(128)}, u32[]{:S(2)}) copy-start(s32[65]{0:T(128)} %copy-done.7) | copy-start | bytes 784
  45.2 43.7 %collective-permute-start.7 = (bf16[16,256,256]{2,1,0:T(8,128)(2,1)}, bf16[16,256,256]{2,1,0:T(8,128)(2,1)}, u32[]{:S(2)}, u32[]{:S(2)}) collective-permute-start(bf16[16,256,256]{2,1,0:T(8,128)(2,1)} %tied.3), channel_id=1, source_target_pairs={{0,8},{8,16},{16,24},{24,32},{32,40},{40,48},{48,56},{56,64},{64,7... | collective-permute-start | bytes 6291464 | tf_op jit(solution)/shard_map/ppermute | solution.py:35
  46.7 4.6 %collective-permute-start.10 = (bf16[4,2,2,128,128]{4,3,2,1,0:T(8,128)(2,1)S(1)}, bf16[4,2,2,128,128]{4,3,2,1,0:T(8,128)(2,1)S(1)}, u32[]{:S(2)}, u32[]{:S(2)}) collective-permute-start(bf16[4,2,2,128,128]{4,3,2,1,0:T(8,128)(2,1)S(1)} %get-tuple-element.31), channel_id=1, source_target_pairs={{0,1},{1,0},{2,3},{3,2},{4,5},{5,4},{6,7},{7,6},{8,9},{9,8},{10,11... | collective-permute-start | bytes 1572872 | tf_op jit(solution)/shard_map/ppermute | solution.py:35
  49.0 3.7 %collective-permute-start.11 = (bf16[2,8,128,128]{3,2,1,0:T(8,128)(2,1)S(1)}, bf16[2,8,128,128]{3,2,1,0:T(8,128)(2,1)}, u32[]{:S(2)}, u32[]{:S(2)}) collective-permute-start(bf16[2,8,128,128]{3,2,1,0:T(8,128)(2,1)S(1)} %copy-done.9), channel_id=1, source_target_pairs={{0,1},{1,0},{2,3},{3,2},{4,5},{5,4},{6,7},{7,6},{8,9},{9,8},{10,11... | collective-permute-start | bytes 1572872 | tf_op jit(solution)/shard_map/ppermute | solution.py:35
  51.2 0.8 copy-start.10
  52.0 2.1 %collective-permute-start.12 = (bf16[2,8,128,128]{3,2,1,0:T(8,128)(2,1)}, bf16[2,8,128,128]{3,2,1,0:T(8,128)(2,1)S(1)}, u32[]{:S(2)}, u32[]{:S(2)}) collective-permute-start(bf16[2,8,128,128]{3,2,1,0:T(8,128)(2,1)} %collective-permute-done.6.refs_3_.refs_9_), channel_id=1, source_target_pairs={{0,1},{1,0},{2,3},{3,2},{4,5},{5,4},{6,7},{7,6},{8,9},{9,8},{10,11... | collective-permute-start | bytes 1572872 | tf_op jit(solution)/shard_map/ppermute | solution.py:35
  54.1 0.8 copy-start.11
  59.0 13.6 %collective-permute-start.13 = (bf16[8,128,128]{2,1,0:T(8,128)(2,1)S(1)}, bf16[8,128,128]{2,1,0:T(8,128)(2,1)S(1)}, u32[]{:S(2)}, u32[]{:S(2)}) collective-permute-start(bf16[8,128,128]{2,1,0:T(8,128)(2,1)S(1)} %get-tuple-element.36), channel_id=1, source_target_pairs={{0,2},{1,3},{2,4},{3,5},{4,6},{5,7},{6,0},{7,1},{8,10},{9,11},{10,... | collective-permute-start | bytes 786440 | tf_op jit(solution)/shard_map/ppermute | solution.py:35
  64.3 11.2 %collective-permute-start.15 = (bf16[8,128,128]{2,1,0:T(8,128)(2,1)S(1)}, bf16[8,128,128]{2,1,0:T(8,128)(2,1)S(1)}, u32[]{:S(2)}, u32[]{:S(2)}) collective-permute-start(bf16[8,128,128]{2,1,0:T(8,128)(2,1)S(1)} %get-tuple-element.39), channel_id=1, source_target_pairs={{0,6},{1,7},{2,0},{3,1},{4,2},{5,3},{6,4},{7,5},{8,14},{9,15},{10,... | collective-permute-start | bytes 786440 | tf_op jit(solution)/shard_map/ppermute | solution.py:35
  64.3 8.2 %copy-start.3 = (bf16[16,256,256]{2,1,0:T(8,128)(2,1)}, bf16[16,256,256]{2,1,0:T(8,128)(2,1)S(1)}, u32[]{:S(2)}) copy-start(bf16[16,256,256]{2,1,0:T(8,128)(2,1)S(1)} %collective-permute-done.8.below.refs_11_) | copy-start | bytes 6291460
  64.4 11.2 %copy-start.1 = (f32[16,256,256]{2,1,0:T(8,128)S(1)}, f32[16,256,256]{2,1,0:T(8,128)}, u32[]{:S(2)}) copy-start(f32[16,256,256]{2,1,0:T(8,128)} %copy-done) | copy-start | bytes 12582916
  72.7 13.0 %collective-permute-start.14 = (bf16[2,8,128,128]{3,2,1,0:T(8,128)(2,1)S(1)}, bf16[2,8,128,128]{3,2,1,0:T(8,128)(2,1)S(1)}, u32[]{:S(2)}, u32[]{:S(2)}) collective-permute-start(bf16[2,8,128,128]{3,2,1,0:T(8,128)(2,1)S(1)} %with_arrived.2), channel_id=1, source_target_pairs={{0,2},{1,3},{2,4},{3,5},{4,6},{5,7},{6,0},{7,1},{8,10},{9,11},{10,... | collective-permute-start | bytes 1572872 | tf_op jit(solution)/shard_map/ppermute | solution.py:35
  75.5 13.5 %collective-permute-start.16 = (bf16[2,8,128,128]{3,2,1,0:T(8,128)(2,1)S(1)}, bf16[2,8,128,128]{3,2,1,0:T(8,128)(2,1)S(1)}, u32[]{:S(2)}, u32[]{:S(2)}) collective-permute-start(bf16[2,8,128,128]{3,2,1,0:T(8,128)(2,1)S(1)} %with_arrived.3), channel_id=1, source_target_pairs={{0,6},{1,7},{2,0},{3,1},{4,2},{5,3},{6,4},{7,5},{8,14},{9,15},{10,... | collective-permute-start | bytes 1572872 | tf_op jit(solution)/shard_map/ppermute | solution.py:35
  75.6 13.4 %copy-start.5 = (bf16[16,2,256,128]{3,2,1,0:T(8,128)(2,1)S(1)}, bf16[16,2,256,128]{3,2,1,0:T(8,128)(2,1)}, u32[]{:S(2)}) copy-start(bf16[16,2,256,128]{3,2,1,0:T(8,128)(2,1)} %copy-done.4) | copy-start | bytes 6291460

commit v3 on v0

v3 whole, which is shorter than its diff:
```python
import jax
import jax.numpy as jnp
from jax import lax
from jax.experimental import pallas as pl
from jax.experimental.pallas import tpu as pltpu
from jax.sharding import PartitionSpec as P

AXES = ("cluster", "cone")
DEVICES = 128
ROW = 8
F32 = jnp.float32
BF16 = jnp.bfloat16
SMALL = pl.CostEstimate(flops=0, bytes_accessed=1024, transcendentals=0)


def moved(dx):
    return [(d, (d & ~6) | ((((d >> 1) & 3) + dx) % 4) << 1) for d in range(DEVICES)]


FLIP_CORE = [(d, d ^ 1) for d in range(DEVICES)]
FLIP_Z = [(d, d ^ 8) for d in range(DEVICES)]
FLIP_BOTH = [(d, d ^ 9) for d in range(DEVICES)]
FLIP_OUTER = [(d, d ^ 72) for d in range(DEVICES)]
X_UP = moved(1)
X_DOWN = moved(-1)
UP = [(d, d - d % ROW + (d + 1) % ROW) for d in range(DEVICES)]
DOWN = [(d, d - d % ROW + (d - 1) % ROW) for d in range(DEVICES)]
NEXT_ROW = [(d, d + ROW) for d in range(0, DEVICES - ROW, ROW)] + [
    (d, d - ROW) for d in range(2 * ROW - 1, DEVICES, ROW)
]


def permute(array, pairs):
    return lax.ppermute(array, AXES, pairs)


IN_VMEM = pl.BlockSpec(memory_space=pltpu.VMEM)
IN_HBM = pl.BlockSpec(memory_space=pltpu.HBM)
IN_SMEM = pl.BlockSpec(memory_space=pltpu.SMEM)
ANYWHERE = pl.BlockSpec(memory_space=pl.ANY)


def kept_in_hbm(array):
    return pltpu.with_memory_space_constraint(array, pltpu.HBM)


def kept_in_vmem(array):
    return pltpu.with_memory_space_constraint(array, pltpu.VMEM)


def limit(mib):
    return pltpu.CompilerParams(vmem_limit_bytes=mib << 20)


ANGLES = 16
TAIL = 4 * ANGLES


def stage_kernel(angle, used, coef, transfer, *refs):
    outs, buffers, angles, weights, sems = refs[:5], refs[5:10], refs[10], refs[11], refs[12]
    small = [pltpu.make_async_copy(angle, angles, sems.at[1, 5]), pltpu.make_async_copy(used, weights, sems.at[1, 6])]
    for copy in small:
        copy.start()
    cone = lax.axis_index("cone")
    zl, core = cone // 8, cone % 2
    sources = ((1 - zl, core), (1 - zl, 1 - core), (zl, 1 - core), (zl, core))
    rows = coef.shape[-2]
    loads = [
        [
            pltpu.make_async_copy(coef.at[z, x, c], buffers[i].at[pl.ds(x * rows, rows)], sems.at[0, i * 4 + x])
            for x in range(4)
        ]
        for i, (z, c) in enumerate(sources)
    ] + [[pltpu.make_async_copy(transfer, buffers[4], sems.at[0, 16])]]
    stores = [pltpu.make_async_copy(buffers[i], outs[i], sems.at[1, i]) for i in range(5)]
    for part in loads:
        for load in part:
            load.start()

    for copy in small:
        copy.wait()
    high = angles[...].astype(BF16)
    left = angles[...] - high.astype(F32)
    middle = left.astype(BF16)
    low = (left - middle.astype(F32)).astype(BF16)
    weight = weights[...].astype(F32)
    each = (ANGLES // 2, weight.shape[1])
    weight = jnp.concatenate([jnp.broadcast_to(weight[i : i + 1], each) for i in range(2)], axis=0)
    for buffer in buffers[:4]:
        buffer[4 * rows :, :] = jnp.zeros((TAIL, buffer.shape[1]), BF16)
        for i, piece in enumerate((high, middle, low, weight.astype(BF16))):
            start = 4 * rows + i * ANGLES
            buffer[start : start + ANGLES, : piece.shape[1]] = piece

    for part, store in zip(loads, stores):
        for load in part:
            load.wait()
        store.start()
    for store in stores:
        store.wait()


def stage(angle, used, coef, transfer):
    part = jax.ShapeDtypeStruct((4 * coef.shape[-2] + TAIL, coef.shape[-1]), coef.dtype)
    outs = (part,) * 4 + (jax.ShapeDtypeStruct(transfer.shape, transfer.dtype),)
    return pl.pallas_call(
        stage_kernel,
        out_shape=outs,
        in_specs=[IN_HBM] * 4,
        out_specs=(IN_HBM,) * 5,
        scratch_shapes=[pltpu.VMEM(a.shape, a.dtype) for a in (*outs, angle, used)]
        + [pltpu.SemaphoreType.DMA((2, 17))],
        compiler_params=limit(5),
        cost_estimate=SMALL,
        name="stage",
    )(*[kept_in_hbm(a) for a in (angle, used, coef, transfer)])


def tied(array, *others):
    def kernel(*refs):
        del refs

    return pl.pallas_call(
        kernel,
        out_shape=jax.ShapeDtypeStruct(array.shape, array.dtype),
        in_specs=[ANYWHERE] * (1 + len(others)),
        out_specs=ANYWHERE,
        input_output_aliases={0: 0},
        compiler_params=limit(1),
        cost_estimate=SMALL,
        name="tied",
    )(array, *others)


def cross_kernel(ties, below, above, *refs):
    out, buffer, sem = refs[ties:]
    at_row = lax.rem(lax.axis_index("cone"), ROW)

    def carry(source):
        for copy in (pltpu.make_async_copy(source, buffer, sem), pltpu.make_async_copy(buffer, out, sem)):
            copy.start()
            copy.wait()

    @pl.when(at_row == 0)
    def _():
        carry(below)

    @pl.when(at_row == ROW - 1)
    def _():
        carry(above)


def crossing_charges(below, above, ties):
    def kernel(*refs):
        cross_kernel(len(ties), *refs)

    return pl.pallas_call(
        kernel,
        out_shape=jax.ShapeDtypeStruct(below.shape, below.dtype),
        in_specs=[ANYWHERE] * (2 + len(ties)),
        out_specs=ANYWHERE,
        scratch_shapes=[pltpu.VMEM(below.shape, below.dtype), pltpu.SemaphoreType.DMA],
        compiler_params=limit(3),
        cost_estimate=SMALL,
        name="crossing_charges",
    )(below, above, *ties)


def transfer_kernel(offsets, ties, *refs):
    coefs, moves, outs = refs[:4], refs[4:8], refs[8 + ties :]
    cone_index = lax.axis_index("cone")
    zl, x, core = cone_index // 8, (cone_index // 2) % 4, cone_index % 2
    size, width = outs[0].shape[1:]
    half = size // 2
    lanes = lax.broadcasted_iota(jnp.int32, (ANGLES, width), 1)
    turns = []
    for coef in coefs:
        tail = coef[coef.shape[0] - TAIL :, :].astype(F32)
        high, middle, low, weight = (tail[i * ANGLES : (i + 1) * ANGLES] for i in range(4))
        angle = high + middle + low
        turns.append((jnp.cos(angle) * weight, jnp.sin(angle) * weight))

    for t, offset in enumerate(offsets):
        target = (x + offset) % 4
        first = zl * 16 + target * 4 + core * 2
        columns_of = [
            [
                [
                    jnp.sum(jnp.where(lanes == first + j, part, 0.0), axis=1, keepdims=True)
                    for part in turns[source]
                ]
                for j in range(2)
            ]
            for source in range(4)
        ]
        for o in range(8):
            total = None
            for source in range(4):
                columns = []
                for j in range(2):
                    rows = []
                    for cone in range(2):
                        at = cone * 8 + o
                        cosine, sine = (column[at : at + 1] for column in columns_of[source][j])
                        start = pl.multiple_of(((target * 2 + j) * 2 + cone) * size, size)
                        real = coefs[source][pl.ds(start, half), :].astype(F32)
                        imag = coefs[source][pl.ds(start + half, half), :].astype(F32)
                        rows.append((cosine * real - sine * imag).astype(BF16))
                        rows.append((sine * real + cosine * imag).astype(BF16))
                    columns.append(jnp.concatenate(rows, axis=0))
                turned = jnp.concatenate(columns, axis=1)
                matrix = jnp.concatenate([moves[source][0, o], moves[source][1, o]], axis=1)
                term = jnp.dot(matrix, turned, preferred_element_type=F32)
                total = term if total is None else total + term
            for j in range(2):
                outs[t * 2 + j][o] = total[:, j * width : (j + 1) * width].astype(BF16)


def transfer_terms(offsets, coefs, moves, ties=()):
    out = pltpu.VMEM(moves[0].shape[1:], BF16)

    def kernel(*refs):
        transfer_kernel(offsets, len(ties), *refs)

    return pl.pallas_call(
        kernel,
        out_shape=(out,) * (2 * len(offsets)),
        in_specs=[IN_VMEM] * 8 + [ANYWHERE] * len(ties),
        out_specs=(IN_VMEM,) * (2 * len(offsets)),
        compiler_params=limit(8),
        cost_estimate=SMALL,
        name="transfer_terms",
    )(*[kept_in_vmem(a) for a in coefs], *[kept_in_vmem(a) for a in moves], *ties)


def add_kernel(left, right, arrived, *rest):
    out = rest[-1]
    for o in range(8):
        out[0, o] = left[o]
        out[1, o] = (right[o].astype(F32) + arrived[o].astype(F32)).astype(BF16)


def with_arrived(left, right, arrived, ties=()):
    return pl.pallas_call(
        add_kernel,
        out_shape=pltpu.VMEM((2,) + left.shape, BF16),
        in_specs=[IN_VMEM] * 3 + [ANYWHERE] * len(ties),
        out_specs=IN_VMEM,
        compiler_params=limit(2),
        cost_estimate=SMALL,
        name="with_arrived",
    )(left, right, kept_in_vmem(arrived), *ties)


def pair_term(real, imag, charge):
    points, columns = charge.shape[0], charge.shape[1] // 2
    both = jnp.dot(jnp.concatenate([real, imag], axis=0), charge, preferred_element_type=F32)
    first, second = both[:points], both[points:]
    return jnp.concatenate(
        [first[:, :columns] - second[:, columns:], first[:, columns:] + second[:, :columns]], axis=1
    )


GROUP = 4
PAIRS = 64


def place_of(neighbours, pair):
    count = neighbours.shape[1]
    device = lax.axis_index("cluster") * 16 + lax.axis_index("cone")
    return neighbours[pair % 4, pair // 4] - (device - 1) * count


def listed_pairs(listed, reals, imags, charge_of, sums, ready=None):
    length = listed[0]

    @pl.loop(0, (length + GROUP - 1) // GROUP)
    def _(group):
        places = [group * GROUP + i for i in range(GROUP)]
        pairs = [listed[1 + jnp.minimum(place, length - 1)] for place in places]
        if ready is not None:
            ready(pairs[-1] // 4)
        terms = []
        for place, pair in zip(places, pairs):
            charge = charge_of(pair)
            charge = jnp.where(place < length, charge, jnp.zeros_like(charge))
            leaf, n = pair // 4, pair % 4
            terms.append((leaf, pair_term(reals[leaf, n], imags[leaf, n], charge)))
        for leaf, term in terms:
            sums[leaf] += term


LEAVES_AHEAD = 5


def own_kernel(
    ties, neighbours, near_real, near_imag, basis, own, *refs
):
    reals, imags, bases, sums, beside, wrapping, inner, charges, loaded, sems, other_sems = refs[ties:]
    count = own.shape[0]
    load_charges = pltpu.make_async_copy(own, charges, other_sems.at[0])
    load_basis = pltpu.make_async_copy(basis, bases, other_sems.at[1])

    def loads(leaf):
        return (
            pltpu.make_async_copy(near_real.at[leaf], reals.at[leaf], sems.at[0, leaf]),
            pltpu.make_async_copy(near_imag.at[leaf], imags.at[leaf], sems.at[1, leaf]),
        )

    load_charges.start()
    for leaf in range(LEAVES_AHEAD):
        for copy in loads(leaf):
            copy.start()

    at_row = lax.rem(lax.axis_index("cone"), ROW)
    for listed in (inner, beside, wrapping):
        listed[0] = 0

    @pl.loop(0, count * 4)
    def _(pair):
        at = place_of(neighbours, pair)
        low, high = at < count, at >= 2 * count
        wraps = (low & (at_row == 0)) | (high & (at_row == ROW - 1))

        def put(listed):
            length = listed[0] + 1
            listed[0] = length
            listed[length] = pair

        @pl.when(jnp.logical_not(low | high))
        def _():
            put(inner)

        @pl.when(wraps)
        def _():
            put(wrapping)

        @pl.when((low | high) & jnp.logical_not(wraps))
        def _():
            put(beside)

    loaded[0] = 0

    @pl.loop(0, count)
    def _(leaf):
        sums[leaf] = jnp.zeros(sums.shape[1:], F32)

    load_charges.wait()

    def ready(leaf):
        @pl.loop(loaded[0], leaf + 1)
        def _(waited):
            for copy in loads(waited):
                copy.wait()

            @pl.when(waited + LEAVES_AHEAD < count)
            def _():
                for copy in loads(waited + LEAVES_AHEAD):
                    copy.start()

        loaded[0] = jnp.maximum(loaded[0], leaf + 1)

    def charge_of(pair):
        return charges[place_of(neighbours, pair) - count]

    listed_pairs(inner, reals, imags, charge_of, sums, ready)
    load_basis.start()
    ready(count - 1)
    load_basis.wait()


def own_sums(neighbours, near_real, near_imag, basis, own, ties):
    count = own.shape[0]
    pairs = jax.ShapeDtypeStruct((1 + PAIRS,), jnp.int32)

    def kernel(*refs):
        own_kernel(len(ties), *refs)

    return pl.pallas_call(
        kernel,
        out_shape=(
            pltpu.VMEM(near_real.shape, BF16),
            pltpu.VMEM(near_imag.shape, BF16),
            pltpu.VMEM(basis.shape, BF16),
            pltpu.VMEM(own.shape, F32),
            pairs,
            pairs,
        ),
        in_specs=[IN_SMEM] + [IN_HBM] * 4 + [ANYWHERE] * len(ties),
        out_specs=(IN_VMEM,) * 4 + (IN_SMEM,) * 2,
        scratch_shapes=[
            pltpu.SMEM(pairs.shape, jnp.int32),
            pltpu.VMEM(own.shape, BF16),
            pltpu.SMEM((1,), jnp.int32),
            pltpu.SemaphoreType.DMA((2, count)),
            pltpu.SemaphoreType.DMA((2,)),
        ],
        compiler_params=limit(6),
        cost_estimate=SMALL,
        name="own_sums",
    )(neighbours, *[kept_in_hbm(a) for a in (near_real, near_imag, basis, own)], *ties)


def more_kernel(parts, ties, neighbours, listed, reals, imags, *refs):
    sources = refs[:parts]
    token, sums, charges, sems = refs[parts + 1 + ties :]
    count = reals.shape[0]
    token[0] = 0

    @pl.when(listed[0] > 0)
    def _():
        copies = [
            pltpu.make_async_copy(source, charges.at[pl.ds(i * count, count)], sems.at[i])
            for i, source in enumerate(sources)
        ]
        for copy in copies:
            copy.start()
        for copy in copies:
            copy.wait()

    def charge_of(pair):
        at = place_of(neighbours, pair)
        inside = lax.rem(at, count)
        return charges[inside if parts == 1 else jnp.where(at < count, inside, inside + count)]

    listed_pairs(listed, reals, imags, charge_of, sums)


def more_sums(neighbours, listed, reals, imags, sources, sums, ties=()):
    parts = len(sources)

    def kernel(*refs):
        more_kernel(parts, len(ties), *refs)

    return pl.pallas_call(
        kernel,
        out_shape=(jax.ShapeDtypeStruct(listed.shape, jnp.int32), pltpu.VMEM(sums.shape, F32)),
        in_specs=[IN_SMEM] * 2 + [IN_VMEM] * 2 + [ANYWHERE] * parts + [IN_VMEM] + [ANYWHERE] * len(ties),
        out_specs=(IN_SMEM, IN_VMEM),
        input_output_aliases={4 + parts: 1},
        scratch_shapes=[
            pltpu.VMEM((parts * sums.shape[0],) + sums.shape[1:], BF16),
            pltpu.SemaphoreType.DMA((parts,)),
        ],
        compiler_params=limit(8),
        cost_estimate=SMALL,
        name="more_sums",
    )(neighbours, listed, reals, imags, *sources, sums, *ties)


def apply_kernel(sums, basis, leaf00, leaf01, leaf1, leaf2, out, totals, sems):
    count = sums.shape[0]

    def store(leaf):
        return pltpu.make_async_copy(totals.at[leaf], out.at[leaf], sems.at[leaf])

    for j, own in enumerate((leaf00, leaf01)):

        @pl.loop(0, count // 4)
        def _(half):
            for i in range(2):
                o = 2 * half + i
                leaf = j * (count // 2) + o
                coef = own[o].astype(F32) + leaf1[1 - j, o].astype(F32) + leaf2[j, o].astype(F32)
                coef = coef.astype(BF16)
                far = [jnp.dot(basis[leaf, s], coef, preferred_element_type=F32) for s in range(2)]
                totals[leaf] = (sums[leaf] + jnp.concatenate(far, axis=1)).astype(BF16)
                store(leaf).start()

    for leaf in range(count):
        store(leaf).wait()


def apply_leaves(sums, basis, leaf_terms):
    count = sums.shape[0]
    leaf_terms = leaf_terms[:2] + [kept_in_vmem(a) for a in leaf_terms[2:]]
    return pl.pallas_call(
        apply_kernel,
        out_shape=jax.ShapeDtypeStruct(sums.shape, BF16),
        in_specs=[IN_VMEM] * 6,
        out_specs=IN_HBM,
        scratch_shapes=[pltpu.VMEM(sums.shape, BF16), pltpu.SemaphoreType.DMA((count,))],
        compiler_params=limit(4),
        cost_estimate=SMALL,
        name="apply_leaves",
    )(sums, basis, *leaf_terms)


def per_device(
    upper_coef, phase, cone_used, transfer, leaf_basis, charges, neighbours, near_real, near_imag
):
    columns = upper_coef.shape[-1]
    coef = upper_coef.reshape(2, 4, 2, -1, columns)
    angle = phase.transpose(1, 2, 0).reshape(ANGLES, -1)
    to_z, to_both, to_core, kept, matrices = stage(angle, cone_used.T, coef, transfer)
    from_core = permute(to_core, FLIP_CORE)
    from_z = permute(to_z, FLIP_Z)
    from_both = permute(to_both, FLIP_BOTH)

    below = permute(charges, UP)
    above = permute(charges, DOWN)
    neighbours = neighbours.T
    transfer_outer = permute(tied(matrices, from_core), FLIP_OUTER)
    reals, imags, basis, sums, beside, wrapping = own_sums(
        neighbours, near_real, near_imag, leaf_basis, charges, [from_core]
    )
    token = beside
    kept_matrices = tied(matrices, token)
    transfer_core = permute(kept_matrices, FLIP_CORE)
    transfer_both = permute(tied(transfer_outer, token), FLIP_CORE)
    moves = [kept_matrices, transfer_core, transfer_outer, transfer_both]
    coefs = [kept, from_core, from_z, from_both]
    crossing = crossing_charges(below, above, [token])
    token, sums = more_sums(neighbours, beside, reals, imags, [below, above], sums)
    crossing = tied(crossing, from_z, from_both, transfer_core, transfer_both, token)
    wrapped = permute(crossing, NEXT_ROW)

    far_first, far_second = transfer_terms([2], coefs, moves, [crossing])
    up = permute(far_first, X_UP)
    down = permute(far_second, X_DOWN)
    up_first, up_second, down_first, down_second = transfer_terms([1, 3], coefs, moves)
    to_above = with_arrived(up_second, up_first, up)
    to_below = with_arrived(down_first, down_second, down)
    from_below = permute(to_above, X_UP)
    from_above = permute(to_below, X_DOWN)
    own_first, own_second = transfer_terms([0], coefs, moves, [to_above, to_below])
    _, sums = more_sums(neighbours, wrapping, reals, imags, [wrapped], sums, [own_first])
    return apply_leaves(sums, basis, [own_first, own_second, from_below, from_above])


def solution(mesh):
    in_specs = (
        P("cluster", "cone", None, None),
        P("cluster", "cone", None),
        P("cluster", "cone"),
        P("cone", None, None, None),
        P(("cluster", "cone"), None, None, None),
        P(("cluster", "cone"), None, None),
        P(("cluster", "cone"), None),
        P(("cluster", "cone"), None, None, None),
        P(("cluster", "cone"), None, None, None),
    )
    out_specs = P(("cluster", "cone"), None, None)
    return jax.shard_map(
        per_device, mesh=mesh, in_specs=in_specs, out_specs=out_specs, check_vma=False
    )
```

time: 198 us -> 70.8 us (0.36)
  the two profiles are of different devices: /device:TPU:63 before, /device:TPU:24 now
where the time goes in v3:
time: 70.8 us; the launch traced here: 70.6 us
  Pallas kernels  30.4 us (43%)
  waiting for transfers between devices  23.5 us (33%)
  starting transfers between devices  16.4 us (23%)
    ppermute x13, waiting for transfers between devices, permute(): return lax.ppermute(array, AXES, pairs)  23.5 us
    ppermute x13, starting transfers between devices, permute(): return lax.ppermute(array, AXES, pairs)  16.4 us
    pallas_call x1, Pallas kernels, own_sums(): pl.pallas_call(kernel, out_shape=(pltpu.VMEM(near_real.shape, BF16), pltp...  11.9 us
    pallas_call x3, Pallas kernels, transfer_terms(): pl.pallas_call(kernel, out_shape=(out,) * (2 * len(offsets)), in_specs=[I...  6.73 us
    pallas_call x2, Pallas kernels, more_sums(): pl.pallas_call(kernel, out_shape=(jax.ShapeDtypeStruct(listed.shape, jnp....  6.61 us
    pallas_call x1, Pallas kernels, apply_leaves(): pl.pallas_call(apply_kernel, out_shape=jax.ShapeDtypeStruct(sums.shape, B...  2.56 us
    pallas_call x1, Pallas kernels, stage(): pl.pallas_call(stage_kernel, out_shape=outs, in_specs=[IN_HBM] * 4, out_s...  2.15 us
  transfers between devices with their start and end apart: 13, of which 6 were waited for; matrix products, arithmetic and copies ran while one was open for 0% of the time, Pallas kernels for 39%

profile of v3, /device:TPU:24, one launch (start us, length us, event | category | flops | bytes accessed | tf_op | source)
XLA Modules:
  0.0 70.6 jit_solution(10144001833908902631)
XLA Ops:
  0.0 0.0 collective-permute-start.1
  0.0 3.0 %collective-permute-start.2 = (bf16[16,256,256]{2,1,0:T(8,128)(2,1)}, bf16[16,256,256]{2,1,0:T(8,128)(2,1)S(1)}, u32[]{:S(2)}, u32[]{:S(2)}) collective-permute-start(bf16[16,256,256]{2,1,0:T(8,128)(2,1)} %refs_4_.1), channel_id=1, source_target_pairs={{0,7},{1,0},{2,1},{3,2},{4,3},{5,4},{6,5},{7,6},{8,15},{9,8},{10,9... | collective-permute-start | bytes 6291464 | tf_op jit(solution)/shard_map/ppermute | solution.py:34
  3.0 0.0 copy-start
  3.0 2.2 %stage.1 = (bf16[2112,128]{1,0:T(8,128)(2,1)S(1)}, bf16[2112,128]{1,0:T(8,128)(2,1)S(1)}, bf16[2112,128]{1,0:T(8,128)(2,1)S(1)}, bf16[2112,128]{1,0:T(8,128)(2,1)S(1)}, bf16[2,8,128,128]{3,2,1,0:T(8,128)(2,1)S(1)}) custom-call(f32[16,32]{1,0:T(8,128)} %bitcast.10, s32[2,32]{1,0:T(2,128)} %bitcast.11, bf16[2,4,2,512,128]{4,3,2,1,0:T(8,128)(2,1)} %bitcast.9, ...), custom_call_target="tpu_custom_call" | custom-call | bytes 1024 | tf_op jit(solution)/shard_map/stage/pallas_call | solution.py:106
  5.1 0.1 collective-permute-start
  5.3 1.9 %collective-permute-done.refs_5_.refs_1_ = bf16[2112,128]{1,0:T(8,128)(2,1)S(1)} collective-permute-done((bf16[2112,128]{1,0:T(8,128)(2,1)S(1)}, bf16[2112,128]{1,0:T(8,128)(2,1)S(1)}, u32[]{:S(2)}, u32[]{:S(2)}) %collective-permute-start) | collective-permute-done | bytes 540704 | tf_op jit(solution)/shard_map/ppermute | solution.py:34
  7.1 4.0 %collective-permute-start.6 = (bf16[2,8,128,128]{3,2,1,0:T(8,128)(2,1)S(1)}, bf16[2,8,128,128]{3,2,1,0:T(8,128)(2,1)S(1)}, u32[]{:S(2)}, u32[]{:S(2)}) collective-permute-start(bf16[2,8,128,128]{3,2,1,0:T(8,128)(2,1)S(1)} %tied.5), channel_id=1, source_target_pairs={{0,72},{1,73},{2,74},{3,75},{4,76},{5,77},{6,78},{7,79},{8,64},{9,... | collective-permute-start | bytes 1572872 | tf_op jit(solution)/shard_map/ppermute | solution.py:34
  11.2 0.0 collective-permute-start.3
  11.2 1.2 %collective-permute-start.4 = (bf16[2112,128]{1,0:T(8,128)(2,1)S(1)}, bf16[2112,128]{1,0:T(8,128)(2,1)S(1)}, u32[]{:S(2)}, u32[]{:S(2)}) collective-permute-start(bf16[2112,128]{1,0:T(8,128)(2,1)S(1)} %get-tuple-element.33), channel_id=1, source_target_pairs={{0,9},{1,8},{2,11},{3,10},{4,13},{5,12},{6,15},{7,14},{8,1},{9,0},... | collective-permute-start | bytes 1622024 | tf_op jit(solution)/shard_map/ppermute | solution.py:34
  12.4 0.0 copy-done
  12.4 11.9 %own_sums.1 = (bf16[16,4,256,256]{3,2,1,0:T(8,128)(2,1)S(1)}, bf16[16,4,256,256]{3,2,1,0:T(8,128)(2,1)S(1)}, bf16[16,2,256,128]{3,2,1,0:T(8,128)(2,1)S(1)}, f32[...) custom-call(s32[4,16]{1,0:T(4,128)S(1)} %bitcast.6, bf16[16,4,256,256]{3,2,1,0:T(8,128)(2,1)} %refs_1_.1, ...), custom_call_target="tpu_custom_call" | custom-call | bytes 1024 | tf_op jit(solution)/shard_map/own_sums/pallas_call | solution.py:379
  24.3 0.0 collective-permute-done.6.refs_6_
  24.3 1.0 %collective-permute-start.5 = (bf16[2,8,128,128]{3,2,1,0:T(8,128)(2,1)S(1)}, bf16[2,8,128,128]{3,2,1,0:T(8,128)(2,1)S(1)}, u32[]{:S(2)}, u32[]{:S(2)}) collective-permute-start(bf16[2,8,128,128]{3,2,1,0:T(8,128)(2,1)S(1)} %tied.4.refs_4_), channel_id=1, source_target_pairs={{0,1},{1,0},{2,3},{3,2},{4,5},{5,4},{6,7},{7,6},{8,9},{9,8},{10,11... | collective-permute-start | bytes 1572872 | tf_op jit(solution)/shard_map/ppermute | solution.py:34
  25.3 1.5 %collective-permute-done.1.refs_0_.refs_4_ = bf16[16,256,256]{2,1,0:T(8,128)(2,1)S(1)} collective-permute-done((bf16[16,256,256]{2,1,0:T(8,128)(2,1)}, bf16[16,256,256]{2,1,0:T(8,128)(2,1)S(1)}, u32[]{:S(2)}, u32[]{:S(2)}) %collective-permute-start.1) | collective-permute-done | bytes 2097184 | tf_op jit(solution)/shard_map/ppermute | solution.py:34
  26.9 0.0 collective-permute-start.7
  26.9 0.0 collective-permute-done.2.refs_1_.refs_5_
  26.9 0.3 crossing_charges.1.refs_0_
  27.2 3.1 %more_sums.2 = (s32[65]{0:T(128)S(1)}, f32[16,256,256]{2,1,0:T(8,128)S(1)}) custom-call(s32[4,16]{1,0:T(4,128)S(1)} %bitcast.7, s32[65]{0:T(128)S(1)} %get-tuple-element.31.refs_2_.refs_1_, bf16[16,4,256,256]{3,2,1,0:T(8,128)(2,1)S(1)} %get-tuple-element.29.refs_2_, ...), custom_call_target="tpu_custom_call", output_to_operand_aliasing={{1}: (6, {})} | custom-call | bytes 1024 | tf_op jit(solution)/shard_map/more_sums/pallas_call | solution.py:435
  30.3 0.0 collective-permute-done.3.refs_1_.refs_2_
  30.3 5.3 %collective-permute-done.4.refs_2_.refs_3_ = bf16[2112,128]{1,0:T(8,128)(2,1)S(1)} collective-permute-done((bf16[2112,128]{1,0:T(8,128)(2,1)S(1)}, bf16[2112,128]{1,0:T(8,128)(2,1)S(1)}, u32[]{:S(2)}, u32[]{:S(2)}) %collective-permute-start.4) | collective-permute-done | bytes 540704 | tf_op jit(solution)/shard_map/ppermute | solution.py:34
  35.7 0.0 collective-permute-done.5.refs_3_.refs_5_
  35.7 0.0 collective-permute-done.7.refs_4_.refs_7_
  35.7 2.6 %collective-permute-start.8 = (bf16[16,256,256]{2,1,0:T(8,128)(2,1)S(1)}, bf16[16,256,256]{2,1,0:T(8,128)(2,1)S(1)}, u32[]{:S(2)}, u32[]{:S(2)}) collective-permute-start(bf16[16,256,256]{2,1,0:T(8,128)(2,1)S(1)} %tied.7.refs_8_), channel_id=1, source_target_pairs={{0,8},{8,16},{16,24},{24,32},{32,40},{40,48},{48,56},{56,64},{64,7... | collective-permute-start | bytes 6291464 | tf_op jit(solution)/shard_map/ppermute | solution.py:34
  38.3 1.8 %transfer_terms.4 = (bf16[8,128,128]{2,1,0:T(8,128)(2,1)S(1)}, bf16[8,128,128]{2,1,0:T(8,128)(2,1)S(1)}) custom-call(bf16[2112,128]{1,0:T(8,128)(2,1)S(1)} %get-tuple-element.38.refs_0_, bf16[2112,128]{1,0:T(8,128)(2,1)S(1)} %collective-permute-done.refs_5_.refs_1_, bf16[2112,128]{1,0:T(8,128)(2,1)S(1)} %collective-permute-done.3.refs_1_.refs_2_, ...), custom_call_target="tpu_custom_call" | custom-call | bytes 1024 | tf_op jit(solution)/shard_map/transfer_terms/pallas_call | solution.py:225
  40.0 0.1 collective-permute-start.10
  40.1 2.0 %collective-permute-start.9 = (bf16[8,128,128]{2,1,0:T(8,128)(2,1)S(1)}, bf16[8,128,128]{2,1,0:T(8,128)(2,1)S(1)}, u32[]{:S(2)}, u32[]{:S(2)}) collective-permute-start(bf16[8,128,128]{2,1,0:T(8,128)(2,1)S(1)} %get-tuple-element.41), channel_id=1, source_target_pairs={{0,2},{1,3},{2,4},{3,5},{4,6},{5,7},{6,0},{7,1},{8,10},{9,11},{10,... | collective-permute-start | bytes 786440 | tf_op jit(solution)/shard_map/ppermute | solution.py:34
  42.1 3.2 %transfer_terms.3 = (bf16[8,128,128]{2,1,0:T(8,128)(2,1)S(1)}, bf16[8,128,128]{2,1,0:T(8,128)(2,1)S(1)}, bf16[8,128,128]{2,1,0:T(8,128)(2,1)S(1)}, bf16[8,128,128]{2,1,0:T(8,128)(2,1)S(1)}) custom-call(bf16[2112,128]{1,0:T(8,128)(2,1)S(1)} %get-tuple-element.38.refs_0_, bf16[2112,128]{1,0:T(8,128)(2,1)S(1)} %collective-permute-done.refs_5_.refs_1_, ...), custom_call_target="tpu_custom_call" | custom-call | bytes 1024 | tf_op jit(solution)/shard_map/transfer_terms/pallas_call | solution.py:225
  45.3 2.1 %collective-permute-done.10.arrived = bf16[8,128,128]{2,1,0:T(8,128)(2,1)S(1)} collective-permute-done((bf16[8,128,128]{2,1,0:T(8,128)(2,1)S(1)}, bf16[8,128,128]{2,1,0:T(8,128)(2,1)S(1)}, u32[]{:S(2)}, u32[]{:S(2)}) %collective-permute-start.10) | collective-permute-done | bytes 262176 | tf_op jit(solution)/shard_map/ppermute | solution.py:34
  47.5 0.1 with_arrived.3.refs_9_
  47.5 2.1 %collective-permute-start.12 = (bf16[2,8,128,128]{3,2,1,0:T(8,128)(2,1)S(1)}, bf16[2,8,128,128]{3,2,1,0:T(8,128)(2,1)S(1)}, u32[]{:S(2)}, u32[]{:S(2)}) collective-permute-start(bf16[2,8,128,128]{3,2,1,0:T(8,128)(2,1)S(1)} %with_arrived.3.refs_9_), channel_id=1, source_target_pairs={{0,6},{1,7},{2,0},{3,1},{4,2},{5,3},{6,4},{7,5},{8,14},{9,15},{10,... | collective-permute-start | bytes 1572872 | tf_op jit(solution)/shard_map/ppermute | solution.py:34
  49.6 0.3 collective-permute-done.9.arrived
  49.9 0.1 with_arrived.2.refs_8_
  50.0 0.4 collective-permute-start.11
  50.5 1.7 %transfer_terms.5 = (bf16[8,128,128]{2,1,0:T(8,128)(2,1)S(1)}, bf16[8,128,128]{2,1,0:T(8,128)(2,1)S(1)}) custom-call(bf16[2112,128]{1,0:T(8,128)(2,1)S(1)} %get-tuple-element.38.refs_0_, bf16[2112,128]{1,0:T(8,128)(2,1)S(1)} %collective-permute-done.refs_5_.refs_1_, bf16[2112,128]{1,0:T(8,128)(2,1)S(1)} %collective-permute-done.3.refs_1_.refs_2_, ...), custom_call_target="tpu_custom_call" | custom-call | bytes 1024 | tf_op jit(solution)/shard_map/transfer_terms/pallas_call | solution.py:225
  52.2 12.3 %collective-permute-done.8.refs_4_ = bf16[16,256,256]{2,1,0:T(8,128)(2,1)S(1)} collective-permute-done((bf16[16,256,256]{2,1,0:T(8,128)(2,1)S(1)}, bf16[16,256,256]{2,1,0:T(8,128)(2,1)S(1)}, u32[]{:S(2)}, u32[]{:S(2)}) %collective-permute-start.8) | collective-permute-done | bytes 2097184 | tf_op jit(solution)/shard_map/ppermute | solution.py:34
  64.5 3.5 %more_sums.3 = (s32[65]{0:T(128)}, f32[16,256,256]{2,1,0:T(8,128)S(1)}) custom-call(s32[4,16]{1,0:T(4,128)S(1)} %bitcast.8, s32[65]{0:T(128)S(1)} %get-tuple-element.28.refs_1_, bf16[16,4,256,256]{3,2,1,0:T(8,128)(2,1)S(1)} %get-tuple-element.29.refs_2_, bf16[16,4,256,256]{3,2,1,0:T(8,128)(2,1)S(1)} %get-tuple-element.30.refs_3_, ...), custom_call_target="tpu_custom_call", output_to_operand_aliasing={{1}: (5, {})} | custom-call | bytes 1024 | tf_op jit(solution)/shard_map/more_sums/pallas_call | solution.py:435
  68.0 0.0 collective-permute-done.12.leaf2
  68.0 0.0 collective-permute-done.11.leaf1
  68.0 2.6 %apply_leaves.1 = bf16[16,256,256]{2,1,0:T(8,128)(2,1)} custom-call(f32[16,256,256]{2,1,0:T(8,128)S(1)} %get-tuple-element.46.sums, bf16[16,2,256,128]{3,2,1,0:T(8,128)(2,1)S(1)} %get-tuple-element.47.basis, bf16[8,128,128]{2,1,0:T(8,128)(2,1)S(1)} %get-tuple-element.45.refs_6_.leaf00, bf16[8,128,128]{2,1,0:T(8,128)(2,1)S(1)} %get-tuple-element.48.leaf01, ...), custom_call_target="tpu_custom_call" | custom-call | bytes 1024 | tf_op jit(solution)/shard_map/apply_leaves/pallas_call | solution.py:477
  (6 shorter events, 0.1 us)
Async XLA Ops:
  0.0 26.9 %collective-permute-start.1 = (bf16[16,256,256]{2,1,0:T(8,128)(2,1)}, bf16[16,256,256]{2,1,0:T(8,128)(2,1)S(1)}, u32[]{:S(2)}, u32[]{:S(2)}) collective-permute-start(bf16[16,256,256]{2,1,0:T(8,128)(2,1)} %refs_4_.1), channel_id=1, source_target_pairs={{0,1},{1,2},{2,3},{3,4},{4,5},{5,6},{6,7},{7,0},{8,9},{9,10},{10,1... | collective-permute-start | bytes 6291464 | tf_op jit(solution)/shard_map/ppermute | solution.py:34
  0.0 26.9 %collective-permute-start.2 = (bf16[16,256,256]{2,1,0:T(8,128)(2,1)}, bf16[16,256,256]{2,1,0:T(8,128)(2,1)S(1)}, u32[]{:S(2)}, u32[]{:S(2)}) collective-permute-start(bf16[16,256,256]{2,1,0:T(8,128)(2,1)} %refs_4_.1), channel_id=1, source_target_pairs={{0,7},{1,0},{2,1},{3,2},{4,3},{5,4},{6,5},{7,6},{8,15},{9,8},{10,9... | collective-permute-start | bytes 6291464 | tf_op jit(solution)/shard_map/ppermute | solution.py:34
  3.0 9.4 %copy-start = (s32[16,4]{0,1:T(4,128)S(1)}, s32[16,4]{0,1:T(4,128)}, u32[]{:S(2)}) copy-start(s32[16,4]{0,1:T(4,128)} %param.15) | copy-start | bytes 772
  5.1 2.0 %collective-permute-start = (bf16[2112,128]{1,0:T(8,128)(2,1)S(1)}, bf16[2112,128]{1,0:T(8,128)(2,1)S(1)}, u32[]{:S(2)}, u32[]{:S(2)}) collective-permute-start(bf16[2112,128]{1,0:T(8,128)(2,1)S(1)} %get-tuple-element.27), channel_id=1, source_target_pairs={{0,1},{1,0},{2,3},{3,2},{4,5},{5,4},{6,7},{7,6},{8,9},{9,8},{10,11... | collective-permute-start | bytes 1622024 | tf_op jit(solution)/shard_map/ppermute | solution.py:34
  7.1 17.2 %collective-permute-start.6 = (bf16[2,8,128,128]{3,2,1,0:T(8,128)(2,1)S(1)}, bf16[2,8,128,128]{3,2,1,0:T(8,128)(2,1)S(1)}, u32[]{:S(2)}, u32[]{:S(2)}) collective-permute-start(bf16[2,8,128,128]{3,2,1,0:T(8,128)(2,1)S(1)} %tied.5), channel_id=1, source_target_pairs={{0,72},{1,73},{2,74},{3,75},{4,76},{5,77},{6,78},{7,79},{8,64},{9,... | collective-permute-start | bytes 1572872 | tf_op jit(solution)/shard_map/ppermute | solution.py:34
  11.2 19.2 %collective-permute-start.3 = (bf16[2112,128]{1,0:T(8,128)(2,1)S(1)}, bf16[2112,128]{1,0:T(8,128)(2,1)S(1)}, u32[]{:S(2)}, u32[]{:S(2)}) collective-permute-start(bf16[2112,128]{1,0:T(8,128)(2,1)S(1)} %get-tuple-element.32), channel_id=1, source_target_pairs={{0,8},{1,9},{2,10},{3,11},{4,12},{5,13},{6,14},{7,15},{8,0},{9,1},... | collective-permute-start | bytes 1622024 | tf_op jit(solution)/shard_map/ppermute | solution.py:34
  11.2 24.5 %collective-permute-start.4 = (bf16[2112,128]{1,0:T(8,128)(2,1)S(1)}, bf16[2112,128]{1,0:T(8,128)(2,1)S(1)}, u32[]{:S(2)}, u32[]{:S(2)}) collective-permute-start(bf16[2112,128]{1,0:T(8,128)(2,1)S(1)} %get-tuple-element.33), channel_id=1, source_target_pairs={{0,9},{1,8},{2,11},{3,10},{4,13},{5,12},{6,15},{7,14},{8,1},{9,0},... | collective-permute-start | bytes 1622024 | tf_op jit(solution)/shard_map/ppermute | solution.py:34
  24.3 11.4 %collective-permute-start.5 = (bf16[2,8,128,128]{3,2,1,0:T(8,128)(2,1)S(1)}, bf16[2,8,128,128]{3,2,1,0:T(8,128)(2,1)S(1)}, u32[]{:S(2)}, u32[]{:S(2)}) collective-permute-start(bf16[2,8,128,128]{3,2,1,0:T(8,128)(2,1)S(1)} %tied.4.refs_4_), channel_id=1, source_target_pairs={{0,1},{1,0},{2,3},{3,2},{4,5},{5,4},{6,7},{7,6},{8,9},{9,8},{10,11... | collective-permute-start | bytes 1572872 | tf_op jit(solution)/shard_map/ppermute | solution.py:34
  26.9 8.8 %collective-permute-start.7 = (bf16[2,8,128,128]{3,2,1,0:T(8,128)(2,1)S(1)}, bf16[2,8,128,128]{3,2,1,0:T(8,128)(2,1)S(1)}, u32[]{:S(2)}, u32[]{:S(2)}) collective-permute-start(bf16[2,8,128,128]{3,2,1,0:T(8,128)(2,1)S(1)} %tied.6), channel_id=1, source_target_pairs={{0,1},{1,0},{2,3},{3,2},{4,5},{5,4},{6,7},{7,6},{8,9},{9,8},{10,11... | collective-permute-start | bytes 1572872 | tf_op jit(solution)/shard_map/ppermute | solution.py:34
  35.7 28.8 %collective-permute-start.8 = (bf16[16,256,256]{2,1,0:T(8,128)(2,1)S(1)}, bf16[16,256,256]{2,1,0:T(8,128)(2,1)S(1)}, u32[]{:S(2)}, u32[]{:S(2)}) collective-permute-start(bf16[16,256,256]{2,1,0:T(8,128)(2,1)S(1)} %tied.7.refs_8_), channel_id=1, source_target_pairs={{0,8},{8,16},{16,24},{24,32},{32,40},{40,48},{48,56},{56,64},{64,7... | collective-permute-start | bytes 6291464 | tf_op jit(solution)/shard_map/ppermute | solution.py:34
  40.0 7.4 %collective-permute-start.10 = (bf16[8,128,128]{2,1,0:T(8,128)(2,1)S(1)}, bf16[8,128,128]{2,1,0:T(8,128)(2,1)S(1)}, u32[]{:S(2)}, u32[]{:S(2)}) collective-permute-start(bf16[8,128,128]{2,1,0:T(8,128)(2,1)S(1)} %get-tuple-element.44), channel_id=1, source_target_pairs={{0,6},{1,7},{2,0},{3,1},{4,2},{5,3},{6,4},{7,5},{8,14},{9,15},{10,... | collective-permute-start | bytes 786440 | tf_op jit(solution)/shard_map/ppermute | solution.py:34
  40.1 9.8 %collective-permute-start.9 = (bf16[8,128,128]{2,1,0:T(8,128)(2,1)S(1)}, bf16[8,128,128]{2,1,0:T(8,128)(2,1)S(1)}, u32[]{:S(2)}, u32[]{:S(2)}) collective-permute-start(bf16[8,128,128]{2,1,0:T(8,128)(2,1)S(1)} %get-tuple-element.41), channel_id=1, source_target_pairs={{0,2},{1,3},{2,4},{3,5},{4,6},{5,7},{6,0},{7,1},{8,10},{9,11},{10,... | collective-permute-start | bytes 786440 | tf_op jit(solution)/shard_map/ppermute | solution.py:34
  47.5 20.5 %collective-permute-start.12 = (bf16[2,8,128,128]{3,2,1,0:T(8,128)(2,1)S(1)}, bf16[2,8,128,128]{3,2,1,0:T(8,128)(2,1)S(1)}, u32[]{:S(2)}, u32[]{:S(2)}) collective-permute-start(bf16[2,8,128,128]{3,2,1,0:T(8,128)(2,1)S(1)} %with_arrived.3.refs_9_), channel_id=1, source_target_pairs={{0,6},{1,7},{2,0},{3,1},{4,2},{5,3},{6,4},{7,5},{8,14},{9,15},{10,... | collective-permute-start | bytes 1572872 | tf_op jit(solution)/shard_map/ppermute | solution.py:34
  50.0 18.0 %collective-permute-start.11 = (bf16[2,8,128,128]{3,2,1,0:T(8,128)(2,1)S(1)}, bf16[2,8,128,128]{3,2,1,0:T(8,128)(2,1)S(1)}, u32[]{:S(2)}, u32[]{:S(2)}) collective-permute-start(bf16[2,8,128,128]{3,2,1,0:T(8,128)(2,1)S(1)} %with_arrived.2.refs_8_), channel_id=1, source_target_pairs={{0,2},{1,3},{2,4},{3,5},{4,6},{5,7},{6,0},{7,1},{8,10},{9,11},{10,... | collective-permute-start | bytes 1572872 | tf_op jit(solution)/shard_map/ppermute | solution.py:34

commit v4 on v3

--- a/solution.py
+++ b/solution.py
@@ -53,7 +53,7 @@
 
 
 ANGLES = 16
-TAIL = 4 * ANGLES
+TAIL = ANGLES
 
 
 def stage_kernel(angle, used, coef, transfer, *refs):
@@ -86,11 +86,10 @@
     weight = weights[...].astype(F32)
     each = (ANGLES // 2, weight.shape[1])
     weight = jnp.concatenate([jnp.broadcast_to(weight[i : i + 1], each) for i in range(2)], axis=0)
+    pieces = [piece.astype(F32) for piece in (high, middle, low)] + [weight]
+    tail = jnp.concatenate(pieces, axis=1).astype(BF16)
     for buffer in buffers[:4]:
-        buffer[4 * rows :, :] = jnp.zeros((TAIL, buffer.shape[1]), BF16)
-        for i, piece in enumerate((high, middle, low, weight.astype(BF16))):
-            start = 4 * rows + i * ANGLES
-            buffer[start : start + ANGLES, : piece.shape[1]] = piece
+        buffer[4 * rows :, :] = tail
 
     for part, store in zip(loads, stores):
         for load in part:
@@ -172,11 +171,12 @@
     zl, x, core = cone_index // 8, (cone_index // 2) % 4, cone_index % 2
     size, width = outs[0].shape[1:]
     half = size // 2
-    lanes = lax.broadcasted_iota(jnp.int32, (ANGLES, width), 1)
+    clusters = width // 4
+    lanes = lax.broadcasted_iota(jnp.int32, (ANGLES, clusters), 1)
     turns = []
     for coef in coefs:
         tail = coef[coef.shape[0] - TAIL :, :].astype(F32)
-        high, middle, low, weight = (tail[i * ANGLES : (i + 1) * ANGLES] for i in range(4))
+        high, middle, low, weight = (tail[:, i * clusters : (i + 1) * clusters] for i in range(4))
         angle = high + middle + low
         turns.append((jnp.cos(angle) * weight, jnp.sin(angle) * weight))
 
@@ -263,6 +263,7 @@
 
 GROUP = 4
 PAIRS = 64
+PLACES = 32
 
 
 def place_of(neighbours, pair):
@@ -271,20 +272,20 @@
     return neighbours[pair % 4, pair // 4] - (device - 1) * count
 
 
-def listed_pairs(listed, reals, imags, charge_of, sums, ready=None):
+def listed_pairs(listed, reals, imags, charges, sums, ready=None):
     length = listed[0]
 
     @pl.loop(0, (length + GROUP - 1) // GROUP)
     def _(group):
         places = [group * GROUP + i for i in range(GROUP)]
-        pairs = [listed[1 + jnp.minimum(place, length - 1)] for place in places]
+        entries = [listed[1 + jnp.minimum(place, length - 1)] for place in places]
         if ready is not None:
-            ready(pairs[-1] // 4)
+            ready(entries[-1] // (4 * PLACES))
         terms = []
-        for place, pair in zip(places, pairs):
-            charge = charge_of(pair)
+        for place, entry in zip(places, entries):
+            charge = charges[entry % PLACES]
             charge = jnp.where(place < length, charge, jnp.zeros_like(charge))
-            leaf, n = pair // 4, pair % 4
+            leaf, n = entry // (4 * PLACES), (entry // PLACES) % 4
             terms.append((leaf, pair_term(reals[leaf, n], imags[leaf, n], charge)))
         for leaf, term in terms:
             sums[leaf] += term
@@ -322,22 +323,24 @@
         low, high = at < count, at >= 2 * count
         wraps = (low & (at_row == 0)) | (high & (at_row == ROW - 1))
 
-        def put(listed):
+        inside = lax.rem(at, count)
+
+        def put(listed, charges_at):
             length = listed[0] + 1
             listed[0] = length
-            listed[length] = pair
+            listed[length] = pair * PLACES + charges_at
 
         @pl.when(jnp.logical_not(low | high))
         def _():
-            put(inner)
+            put(inner, inside)
 
         @pl.when(wraps)
         def _():
-            put(wrapping)
+            put(wrapping, inside)
 
         @pl.when((low | high) & jnp.logical_not(wraps))
         def _():
-            put(beside)
+            put(beside, jnp.where(low, inside, inside + count))
 
     loaded[0] = 0
 
@@ -360,10 +363,7 @@
 
         loaded[0] = jnp.maximum(loaded[0], leaf + 1)
 
-    def charge_of(pair):
-        return charges[place_of(neighbours, pair) - count]
-
-    listed_pairs(inner, reals, imags, charge_of, sums, ready)
+    listed_pairs(inner, reals, imags, charges, sums, ready)
     load_basis.start()
     ready(count - 1)
     load_basis.wait()
@@ -401,7 +401,7 @@
     )(neighbours, *[kept_in_hbm(a) for a in (near_real, near_imag, basis, own)], *ties)
 
 
-def more_kernel(parts, ties, neighbours, listed, reals, imags, *refs):
+def more_kernel(parts, ties, listed, reals, imags, *refs):
     sources = refs[:parts]
     token, sums, charges, sems = refs[parts + 1 + ties :]
     count = reals.shape[0]
@@ -418,15 +418,10 @@
         for copy in copies:
             copy.wait()
 
-    def charge_of(pair):
-        at = place_of(neighbours, pair)
-        inside = lax.rem(at, count)
-        return charges[inside if parts == 1 else jnp.where(at < count, inside, inside + count)]
-
-    listed_pairs(listed, reals, imags, charge_of, sums)
-
-
-def more_sums(neighbours, listed, reals, imags, sources, sums, ties=()):
+    listed_pairs(listed, reals, imags, charges, sums)
+
+
+def more_sums(listed, reals, imags, sources, sums, ties=()):
     parts = len(sources)
 
     def kernel(*refs):
@@ -435,9 +430,9 @@
     return pl.pallas_call(
         kernel,
         out_shape=(jax.ShapeDtypeStruct(listed.shape, jnp.int32), pltpu.VMEM(sums.shape, F32)),
-        in_specs=[IN_SMEM] * 2 + [IN_VMEM] * 2 + [ANYWHERE] * parts + [IN_VMEM] + [ANYWHERE] * len(ties),
+        in_specs=[IN_SMEM] + [IN_VMEM] * 2 + [ANYWHERE] * parts + [IN_VMEM] + [ANYWHERE] * len(ties),
         out_specs=(IN_SMEM, IN_VMEM),
-        input_output_aliases={4 + parts: 1},
+        input_output_aliases={3 + parts: 1},
         scratch_shapes=[
             pltpu.VMEM((parts * sums.shape[0],) + sums.shape[1:], BF16),
             pltpu.SemaphoreType.DMA((parts,)),
@@ -445,7 +440,7 @@
         compiler_params=limit(8),
         cost_estimate=SMALL,
         name="more_sums",
-    )(neighbours, listed, reals, imags, *sources, sums, *ties)
+    )(listed, reals, imags, *sources, sums, *ties)
 
 
 def apply_kernel(sums, basis, leaf00, leaf01, leaf1, leaf2, out, totals, sems):
@@ -456,10 +451,10 @@
 
     for j, own in enumerate((leaf00, leaf01)):
 
-        @pl.loop(0, count // 4)
-        def _(half):
-            for i in range(2):
-                o = 2 * half + i
+        @pl.loop(0, count // 8)
+        def _(part):
+            for i in range(4):
+                o = 4 * part + i
                 leaf = j * (count // 2) + o
                 coef = own[o].astype(F32) + leaf1[1 - j, o].astype(F32) + leaf2[j, o].astype(F32)
                 coef = coef.astype(BF16)
@@ -511,7 +506,7 @@
     moves = [kept_matrices, transfer_core, transfer_outer, transfer_both]
     coefs = [kept, from_core, from_z, from_both]
     crossing = crossing_charges(below, above, [token])
-    token, sums = more_sums(neighbours, beside, reals, imags, [below, above], sums)
+    token, sums = more_sums(beside, reals, imags, [below, above], sums)
     crossing = tied(crossing, from_z, from_both, transfer_core, transfer_both, token)
     wrapped = permute(crossing, NEXT_ROW)
 
@@ -524,7 +519,7 @@
     from_below = permute(to_above, X_UP)
     from_above = permute(to_below, X_DOWN)
     own_first, own_second = transfer_terms([0], coefs, moves, [to_above, to_below])
-    _, sums = more_sums(neighbours, wrapping, reals, imags, [wrapped], sums, [own_first])
+    _, sums = more_sums(wrapping, reals, imags, [wrapped], sums, [own_first])
     return apply_leaves(sums, basis, [own_first, own_second, from_below, from_above])
 
 

time: 70.8 us -> 69.9 us (0.987)
  transfers between devices with their start and end apart: 13 -> 13, of which waited for: 6 -> 6; matrix products, arithmetic and copies ran while one was open for 0% -> 0% of each run, Pallas kernels for 39% -> 41%
where the time goes in v4:
time: 69.9 us; the launch traced here: 69.4 us
  Pallas kernels  30.1 us (43%)
  waiting for transfers between devices  22.8 us (33%)
  starting transfers between devices  16.2 us (23%)
    ppermute x13, waiting for transfers between devices, permute(): return lax.ppermute(array, AXES, pairs)  22.8 us
    ppermute x13, starting transfers between devices, permute(): return lax.ppermute(array, AXES, pairs)  16.2 us
    pallas_call x1, Pallas kernels, own_sums(): pl.pallas_call(kernel, out_shape=(pltpu.VMEM(near_real.shape, BF16), pltp...  12 us
    pallas_call x3, Pallas kernels, transfer_terms(): pl.pallas_call(kernel, out_shape=(out,) * (2 * len(offsets)), in_specs=[I...  7 us
    pallas_call x2, Pallas kernels, more_sums(): pl.pallas_call(kernel, out_shape=(jax.ShapeDtypeStruct(listed.shape, jnp....  6.52 us
    pallas_call x1, Pallas kernels, stage(): pl.pallas_call(stage_kernel, out_shape=outs, in_specs=[IN_HBM] * 4, out_s...  2.15 us
    pallas_call x1, Pallas kernels, apply_leaves(): pl.pallas_call(apply_kernel, out_shape=jax.ShapeDtypeStruct(sums.shape, B...  2 us
  transfers between devices with their start and end apart: 13, of which 6 were waited for; matrix products, arithmetic and copies ran while one was open for 0% of the time, Pallas kernels for 41%

profile of v4, /device:TPU:24, one launch (start us, length us, event | category | flops | bytes accessed | tf_op | source)
XLA Modules:
  0.0 69.4 jit_solution(13510443535182310645)
XLA Ops:
  0.0 0.0 collective-permute-start.1
  0.0 3.0 %collective-permute-start.2 = (bf16[16,256,256]{2,1,0:T(8,128)(2,1)}, bf16[16,256,256]{2,1,0:T(8,128)(2,1)S(1)}, u32[]{:S(2)}, u32[]{:S(2)}) collective-permute-start(bf16[16,256,256]{2,1,0:T(8,128)(2,1)} %refs_4_.1), channel_id=1, source_target_pairs={{0,7},{1,0},{2,1},{3,2},{4,3},{5,4},{6,5},{7,6},{8,15},{9,8},{10,9... | collective-permute-start | bytes 6291464 | tf_op jit(solution)/shard_map/ppermute | solution.py:34
  3.0 0.0 copy-start
  3.0 2.2 %stage.1 = (bf16[2064,128]{1,0:T(8,128)(2,1)S(1)}, bf16[2064,128]{1,0:T(8,128)(2,1)S(1)}, bf16[2064,128]{1,0:T(8,128)(2,1)S(1)}, bf16[2064,128]{1,0:T(8,128)(2,1)S(1)}, bf16[2,8,128,128]{3,2,1,0:T(8,128)(2,1)S(1)}) custom-call(f32[16,32]{1,0:T(8,128)} %bitcast.8, s32[2,32]{1,0:T(2,128)} %bitcast.9, bf16[2,4,2,512,128]{4,3,2,1,0:T(8,128)(2,1)} %bitcast.7, ...), custom_call_target="tpu_custom_call" | custom-call | bytes 1024 | tf_op jit(solution)/shard_map/stage/pallas_call | solution.py:105
  5.1 0.1 collective-permute-start
  5.3 1.9 %collective-permute-done.refs_5_.refs_1_ = bf16[2064,128]{1,0:T(8,128)(2,1)S(1)} collective-permute-done((bf16[2064,128]{1,0:T(8,128)(2,1)S(1)}, bf16[2064,128]{1,0:T(8,128)(2,1)S(1)}, u32[]{:S(2)}, u32[]{:S(2)}) %collective-permute-start) | collective-permute-done | bytes 528416 | tf_op jit(solution)/shard_map/ppermute | solution.py:34
  7.1 4.0 %collective-permute-start.6 = (bf16[2,8,128,128]{3,2,1,0:T(8,128)(2,1)S(1)}, bf16[2,8,128,128]{3,2,1,0:T(8,128)(2,1)S(1)}, u32[]{:S(2)}, u32[]{:S(2)}) collective-permute-start(bf16[2,8,128,128]{3,2,1,0:T(8,128)(2,1)S(1)} %tied.5), channel_id=1, source_target_pairs={{0,72},{1,73},{2,74},{3,75},{4,76},{5,77},{6,78},{7,79},{8,64},{9,... | collective-permute-start | bytes 1572872 | tf_op jit(solution)/shard_map/ppermute | solution.py:34
  11.2 0.0 collective-permute-start.3
  11.2 1.2 %collective-permute-start.4 = (bf16[2064,128]{1,0:T(8,128)(2,1)S(1)}, bf16[2064,128]{1,0:T(8,128)(2,1)S(1)}, u32[]{:S(2)}, u32[]{:S(2)}) collective-permute-start(bf16[2064,128]{1,0:T(8,128)(2,1)S(1)} %get-tuple-element.33), channel_id=1, source_target_pairs={{0,9},{1,8},{2,11},{3,10},{4,13},{5,12},{6,15},{7,14},{8,1},{9,0},... | collective-permute-start | bytes 1585160 | tf_op jit(solution)/shard_map/ppermute | solution.py:34
  12.4 0.0 copy-done
  12.4 12.0 %own_sums.1 = (bf16[16,4,256,256]{3,2,1,0:T(8,128)(2,1)S(1)}, bf16[16,4,256,256]{3,2,1,0:T(8,128)(2,1)S(1)}, bf16[16,2,256,128]{3,2,1,0:T(8,128)(2,1)S(1)}, f32[...) custom-call(s32[4,16]{1,0:T(4,128)S(1)} %bitcast.6, bf16[16,4,256,256]{3,2,1,0:T(8,128)(2,1)} %refs_1_.1, ...), custom_call_target="tpu_custom_call" | custom-call | bytes 1024 | tf_op jit(solution)/shard_map/own_sums/pallas_call | solution.py:379
  24.4 0.0 collective-permute-done.6.refs_6_
  24.4 0.8 %collective-permute-start.5 = (bf16[2,8,128,128]{3,2,1,0:T(8,128)(2,1)S(1)}, bf16[2,8,128,128]{3,2,1,0:T(8,128)(2,1)S(1)}, u32[]{:S(2)}, u32[]{:S(2)}) collective-permute-start(bf16[2,8,128,128]{3,2,1,0:T(8,128)(2,1)S(1)} %tied.4.refs_4_), channel_id=1, source_target_pairs={{0,1},{1,0},{2,3},{3,2},{4,5},{5,4},{6,7},{7,6},{8,9},{9,8},{10,11... | collective-permute-start | bytes 1572872 | tf_op jit(solution)/shard_map/ppermute | solution.py:34
  25.3 1.6 %collective-permute-done.1.refs_0_.refs_3_ = bf16[16,256,256]{2,1,0:T(8,128)(2,1)S(1)} collective-permute-done((bf16[16,256,256]{2,1,0:T(8,128)(2,1)}, bf16[16,256,256]{2,1,0:T(8,128)(2,1)S(1)}, u32[]{:S(2)}, u32[]{:S(2)}) %collective-permute-start.1) | collective-permute-done | bytes 2097184 | tf_op jit(solution)/shard_map/ppermute | solution.py:34
  26.9 0.0 collective-permute-start.7
  26.9 0.0 collective-permute-done.2.refs_1_.refs_4_
  26.9 0.3 crossing_charges.1.refs_0_
  27.2 3.1 %more_sums.2 = (s32[65]{0:T(128)S(1)}, f32[16,256,256]{2,1,0:T(8,128)S(1)}) custom-call(s32[65]{0:T(128)S(1)} %get-tuple-element.31.refs_2_.refs_1_.refs_0_, bf16[16,4,256,256]{3,2,1,0:T(8,128)(2,1)S(1)} %get-tuple-element.29.refs_1_, bf16[16,4,256,256]{3,2,1,0:T(8,128)(2,1)S(1)} %get-tuple-element.30.refs_2_, ...), custom_call_target="tpu_custom_call", output_to_operand_aliasing={{1}: (5, {})} | custom-call | bytes 1024 | tf_op jit(solution)/shard_map/more_sums/pallas_call | solution.py:430
  30.3 0.0 collective-permute-done.3.refs_1_.refs_2_
  30.3 4.8 %collective-permute-done.4.refs_2_.refs_3_ = bf16[2064,128]{1,0:T(8,128)(2,1)S(1)} collective-permute-done((bf16[2064,128]{1,0:T(8,128)(2,1)S(1)}, bf16[2064,128]{1,0:T(8,128)(2,1)S(1)}, u32[]{:S(2)}, u32[]{:S(2)}) %collective-permute-start.4) | collective-permute-done | bytes 528416 | tf_op jit(solution)/shard_map/ppermute | solution.py:34
  35.1 0.0 collective-permute-done.5.refs_3_.refs_5_
  35.1 0.0 collective-permute-done.7.refs_4_.refs_7_
  35.1 2.6 %collective-permute-start.8 = (bf16[16,256,256]{2,1,0:T(8,128)(2,1)S(1)}, bf16[16,256,256]{2,1,0:T(8,128)(2,1)S(1)}, u32[]{:S(2)}, u32[]{:S(2)}) collective-permute-start(bf16[16,256,256]{2,1,0:T(8,128)(2,1)S(1)} %tied.7.refs_8_), channel_id=1, source_target_pairs={{0,8},{8,16},{16,24},{24,32},{32,40},{40,48},{48,56},{56,64},{64,7... | collective-permute-start | bytes 6291464 | tf_op jit(solution)/shard_map/ppermute | solution.py:34
  37.7 1.8 %transfer_terms.4 = (bf16[8,128,128]{2,1,0:T(8,128)(2,1)S(1)}, bf16[8,128,128]{2,1,0:T(8,128)(2,1)S(1)}) custom-call(bf16[2064,128]{1,0:T(8,128)(2,1)S(1)} %get-tuple-element.38.refs_0_, bf16[2064,128]{1,0:T(8,128)(2,1)S(1)} %collective-permute-done.refs_5_.refs_1_, bf16[2064,128]{1,0:T(8,128)(2,1)S(1)} %collective-permute-done.3.refs_1_.refs_2_, ...), custom_call_target="tpu_custom_call" | custom-call | bytes 1024 | tf_op jit(solution)/shard_map/transfer_terms/pallas_call | solution.py:225
  39.6 0.1 collective-permute-start.10
  39.6 2.0 %collective-permute-start.9 = (bf16[8,128,128]{2,1,0:T(8,128)(2,1)S(1)}, bf16[8,128,128]{2,1,0:T(8,128)(2,1)S(1)}, u32[]{:S(2)}, u32[]{:S(2)}) collective-permute-start(bf16[8,128,128]{2,1,0:T(8,128)(2,1)S(1)} %get-tuple-element.41), channel_id=1, source_target_pairs={{0,2},{1,3},{2,4},{3,5},{4,6},{5,7},{6,0},{7,1},{8,10},{9,11},{10,... | collective-permute-start | bytes 786440 | tf_op jit(solution)/shard_map/ppermute | solution.py:34
  41.7 3.3 %transfer_terms.3 = (bf16[8,128,128]{2,1,0:T(8,128)(2,1)S(1)}, bf16[8,128,128]{2,1,0:T(8,128)(2,1)S(1)}, bf16[8,128,128]{2,1,0:T(8,128)(2,1)S(1)}, bf16[8,128,128]{2,1,0:T(8,128)(2,1)S(1)}) custom-call(bf16[2064,128]{1,0:T(8,128)(2,1)S(1)} %get-tuple-element.38.refs_0_, bf16[2064,128]{1,0:T(8,128)(2,1)S(1)} %collective-permute-done.refs_5_.refs_1_, ...), custom_call_target="tpu_custom_call" | custom-call | bytes 1024 | tf_op jit(solution)/shard_map/transfer_terms/pallas_call | solution.py:225
  45.0 2.0 %collective-permute-done.10.arrived = bf16[8,128,128]{2,1,0:T(8,128)(2,1)S(1)} collective-permute-done((bf16[8,128,128]{2,1,0:T(8,128)(2,1)S(1)}, bf16[8,128,128]{2,1,0:T(8,128)(2,1)S(1)}, u32[]{:S(2)}, u32[]{:S(2)}) %collective-permute-start.10) | collective-permute-done | bytes 262176 | tf_op jit(solution)/shard_map/ppermute | solution.py:34
  47.0 0.1 with_arrived.3.refs_9_
  47.1 2.1 %collective-permute-start.12 = (bf16[2,8,128,128]{3,2,1,0:T(8,128)(2,1)S(1)}, bf16[2,8,128,128]{3,2,1,0:T(8,128)(2,1)S(1)}, u32[]{:S(2)}, u32[]{:S(2)}) collective-permute-start(bf16[2,8,128,128]{3,2,1,0:T(8,128)(2,1)S(1)} %with_arrived.3.refs_9_), channel_id=1, source_target_pairs={{0,6},{1,7},{2,0},{3,1},{4,2},{5,3},{6,4},{7,5},{8,14},{9,15},{10,... | collective-permute-start | bytes 1572872 | tf_op jit(solution)/shard_map/ppermute | solution.py:34
  49.1 0.3 collective-permute-done.9.arrived
  49.5 0.1 with_arrived.2.refs_8_
  49.5 0.4 collective-permute-start.11
  50.0 1.8 %transfer_terms.5 = (bf16[8,128,128]{2,1,0:T(8,128)(2,1)S(1)}, bf16[8,128,128]{2,1,0:T(8,128)(2,1)S(1)}) custom-call(bf16[2064,128]{1,0:T(8,128)(2,1)S(1)} %get-tuple-element.38.refs_0_, bf16[2064,128]{1,0:T(8,128)(2,1)S(1)} %collective-permute-done.refs_5_.refs_1_, bf16[2064,128]{1,0:T(8,128)(2,1)S(1)} %collective-permute-done.3.refs_1_.refs_2_, ...), custom_call_target="tpu_custom_call" | custom-call | bytes 1024 | tf_op jit(solution)/shard_map/transfer_terms/pallas_call | solution.py:225
  51.8 12.1 %collective-permute-done.8.refs_3_ = bf16[16,256,256]{2,1,0:T(8,128)(2,1)S(1)} collective-permute-done((bf16[16,256,256]{2,1,0:T(8,128)(2,1)S(1)}, bf16[16,256,256]{2,1,0:T(8,128)(2,1)S(1)}, u32[]{:S(2)}, u32[]{:S(2)}) %collective-permute-start.8) | collective-permute-done | bytes 2097184 | tf_op jit(solution)/shard_map/ppermute | solution.py:34
  64.0 3.4 %more_sums.3 = (s32[65]{0:T(128)}, f32[16,256,256]{2,1,0:T(8,128)S(1)}) custom-call(s32[65]{0:T(128)S(1)} %get-tuple-element.28.refs_0_, bf16[16,4,256,256]{3,2,1,0:T(8,128)(2,1)S(1)} %get-tuple-element.29.refs_1_, bf16[16,4,256,256]{3,2,1,0:T(8,128)(2,1)S(1)} %get-tuple-element.30.refs_2_, ...), custom_call_target="tpu_custom_call", output_to_operand_aliasing={{1}: (4, {})} | custom-call | bytes 1024 | tf_op jit(solution)/shard_map/more_sums/pallas_call | solution.py:430
  67.4 0.0 collective-permute-done.12.leaf2
  67.4 0.0 collective-permute-done.11.leaf1
  67.4 2.0 %apply_leaves.1 = bf16[16,256,256]{2,1,0:T(8,128)(2,1)} custom-call(f32[16,256,256]{2,1,0:T(8,128)S(1)} %get-tuple-element.46.sums, bf16[16,2,256,128]{3,2,1,0:T(8,128)(2,1)S(1)} %get-tuple-element.47.basis, bf16[8,128,128]{2,1,0:T(8,128)(2,1)S(1)} %get-tuple-element.45.refs_5_.leaf00, bf16[8,128,128]{2,1,0:T(8,128)(2,1)S(1)} %get-tuple-element.48.leaf01, ...), custom_call_target="tpu_custom_call" | custom-call | bytes 1024 | tf_op jit(solution)/shard_map/apply_leaves/pallas_call | solution.py:472
  (6 shorter events, 0.1 us)
Async XLA Ops:
  0.0 26.9 %collective-permute-start.1 = (bf16[16,256,256]{2,1,0:T(8,128)(2,1)}, bf16[16,256,256]{2,1,0:T(8,128)(2,1)S(1)}, u32[]{:S(2)}, u32[]{:S(2)}) collective-permute-start(bf16[16,256,256]{2,1,0:T(8,128)(2,1)} %refs_4_.1), channel_id=1, source_target_pairs={{0,1},{1,2},{2,3},{3,4},{4,5},{5,6},{6,7},{7,0},{8,9},{9,10},{10,1... | collective-permute-start | bytes 6291464 | tf_op jit(solution)/shard_map/ppermute | solution.py:34
  0.0 26.9 %collective-permute-start.2 = (bf16[16,256,256]{2,1,0:T(8,128)(2,1)}, bf16[16,256,256]{2,1,0:T(8,128)(2,1)S(1)}, u32[]{:S(2)}, u32[]{:S(2)}) collective-permute-start(bf16[16,256,256]{2,1,0:T(8,128)(2,1)} %refs_4_.1), channel_id=1, source_target_pairs={{0,7},{1,0},{2,1},{3,2},{4,3},{5,4},{6,5},{7,6},{8,15},{9,8},{10,9... | collective-permute-start | bytes 6291464 | tf_op jit(solution)/shard_map/ppermute | solution.py:34
  3.0 9.4 %copy-start = (s32[16,4]{0,1:T(4,128)S(1)}, s32[16,4]{0,1:T(4,128)}, u32[]{:S(2)}) copy-start(s32[16,4]{0,1:T(4,128)} %param.15) | copy-start | bytes 772
  5.1 2.0 %collective-permute-start = (bf16[2064,128]{1,0:T(8,128)(2,1)S(1)}, bf16[2064,128]{1,0:T(8,128)(2,1)S(1)}, u32[]{:S(2)}, u32[]{:S(2)}) collective-permute-start(bf16[2064,128]{1,0:T(8,128)(2,1)S(1)} %get-tuple-element.27), channel_id=1, source_target_pairs={{0,1},{1,0},{2,3},{3,2},{4,5},{5,4},{6,7},{7,6},{8,9},{9,8},{10,11... | collective-permute-start | bytes 1585160 | tf_op jit(solution)/shard_map/ppermute | solution.py:34
  7.1 17.3 %collective-permute-start.6 = (bf16[2,8,128,128]{3,2,1,0:T(8,128)(2,1)S(1)}, bf16[2,8,128,128]{3,2,1,0:T(8,128)(2,1)S(1)}, u32[]{:S(2)}, u32[]{:S(2)}) collective-permute-start(bf16[2,8,128,128]{3,2,1,0:T(8,128)(2,1)S(1)} %tied.5), channel_id=1, source_target_pairs={{0,72},{1,73},{2,74},{3,75},{4,76},{5,77},{6,78},{7,79},{8,64},{9,... | collective-permute-start | bytes 1572872 | tf_op jit(solution)/shard_map/ppermute | solution.py:34
  11.2 19.1 %collective-permute-start.3 = (bf16[2064,128]{1,0:T(8,128)(2,1)S(1)}, bf16[2064,128]{1,0:T(8,128)(2,1)S(1)}, u32[]{:S(2)}, u32[]{:S(2)}) collective-permute-start(bf16[2064,128]{1,0:T(8,128)(2,1)S(1)} %get-tuple-element.32), channel_id=1, source_target_pairs={{0,8},{1,9},{2,10},{3,11},{4,12},{5,13},{6,14},{7,15},{8,0},{9,1},... | collective-permute-start | bytes 1585160 | tf_op jit(solution)/shard_map/ppermute | solution.py:34
  11.2 24.0 %collective-permute-start.4 = (bf16[2064,128]{1,0:T(8,128)(2,1)S(1)}, bf16[2064,128]{1,0:T(8,128)(2,1)S(1)}, u32[]{:S(2)}, u32[]{:S(2)}) collective-permute-start(bf16[2064,128]{1,0:T(8,128)(2,1)S(1)} %get-tuple-element.33), channel_id=1, source_target_pairs={{0,9},{1,8},{2,11},{3,10},{4,13},{5,12},{6,15},{7,14},{8,1},{9,0},... | collective-permute-start | bytes 1585160 | tf_op jit(solution)/shard_map/ppermute | solution.py:34
  24.4 10.7 %collective-permute-start.5 = (bf16[2,8,128,128]{3,2,1,0:T(8,128)(2,1)S(1)}, bf16[2,8,128,128]{3,2,1,0:T(8,128)(2,1)S(1)}, u32[]{:S(2)}, u32[]{:S(2)}) collective-permute-start(bf16[2,8,128,128]{3,2,1,0:T(8,128)(2,1)S(1)} %tied.4.refs_4_), channel_id=1, source_target_pairs={{0,1},{1,0},{2,3},{3,2},{4,5},{5,4},{6,7},{7,6},{8,9},{9,8},{10,11... | collective-permute-start | bytes 1572872 | tf_op jit(solution)/shard_map/ppermute | solution.py:34
  26.9 8.3 %collective-permute-start.7 = (bf16[2,8,128,128]{3,2,1,0:T(8,128)(2,1)S(1)}, bf16[2,8,128,128]{3,2,1,0:T(8,128)(2,1)S(1)}, u32[]{:S(2)}, u32[]{:S(2)}) collective-permute-start(bf16[2,8,128,128]{3,2,1,0:T(8,128)(2,1)S(1)} %tied.6), channel_id=1, source_target_pairs={{0,1},{1,0},{2,3},{3,2},{4,5},{5,4},{6,7},{7,6},{8,9},{9,8},{10,11... | collective-permute-start | bytes 1572872 | tf_op jit(solution)/shard_map/ppermute | solution.py:34
  35.1 28.8 %collective-permute-start.8 = (bf16[16,256,256]{2,1,0:T(8,128)(2,1)S(1)}, bf16[16,256,256]{2,1,0:T(8,128)(2,1)S(1)}, u32[]{:S(2)}, u32[]{:S(2)}) collective-permute-start(bf16[16,256,256]{2,1,0:T(8,128)(2,1)S(1)} %tied.7.refs_8_), channel_id=1, source_target_pairs={{0,8},{8,16},{16,24},{24,32},{32,40},{40,48},{48,56},{56,64},{64,7... | collective-permute-start | bytes 6291464 | tf_op jit(solution)/shard_map/ppermute | solution.py:34
  39.6 7.4 %collective-permute-start.10 = (bf16[8,128,128]{2,1,0:T(8,128)(2,1)S(1)}, bf16[8,128,128]{2,1,0:T(8,128)(2,1)S(1)}, u32[]{:S(2)}, u32[]{:S(2)}) collective-permute-start(bf16[8,128,128]{2,1,0:T(8,128)(2,1)S(1)} %get-tuple-element.44), channel_id=1, source_target_pairs={{0,6},{1,7},{2,0},{3,1},{4,2},{5,3},{6,4},{7,5},{8,14},{9,15},{10,... | collective-permute-start | bytes 786440 | tf_op jit(solution)/shard_map/ppermute | solution.py:34
  39.6 9.8 %collective-permute-start.9 = (bf16[8,128,128]{2,1,0:T(8,128)(2,1)S(1)}, bf16[8,128,128]{2,1,0:T(8,128)(2,1)S(1)}, u32[]{:S(2)}, u32[]{:S(2)}) collective-permute-start(bf16[8,128,128]{2,1,0:T(8,128)(2,1)S(1)} %get-tuple-element.41), channel_id=1, source_target_pairs={{0,2},{1,3},{2,4},{3,5},{4,6},{5,7},{6,0},{7,1},{8,10},{9,11},{10,... | collective-permute-start | bytes 786440 | tf_op jit(solution)/shard_map/ppermute | solution.py:34
  47.1 20.3 %collective-permute-start.12 = (bf16[2,8,128,128]{3,2,1,0:T(8,128)(2,1)S(1)}, bf16[2,8,128,128]{3,2,1,0:T(8,128)(2,1)S(1)}, u32[]{:S(2)}, u32[]{:S(2)}) collective-permute-start(bf16[2,8,128,128]{3,2,1,0:T(8,128)(2,1)S(1)} %with_arrived.3.refs_9_), channel_id=1, source_target_pairs={{0,6},{1,7},{2,0},{3,1},{4,2},{5,3},{6,4},{7,5},{8,14},{9,15},{10,... | collective-permute-start | bytes 1572872 | tf_op jit(solution)/shard_map/ppermute | solution.py:34
  49.5 17.9 %collective-permute-start.11 = (bf16[2,8,128,128]{3,2,1,0:T(8,128)(2,1)S(1)}, bf16[2,8,128,128]{3,2,1,0:T(8,128)(2,1)S(1)}, u32[]{:S(2)}, u32[]{:S(2)}) collective-permute-start(bf16[2,8,128,128]{3,2,1,0:T(8,128)(2,1)S(1)} %with_arrived.2.refs_8_), channel_id=1, source_target_pairs={{0,2},{1,3},{2,4},{3,5},{4,6},{5,7},{6,0},{7,1},{8,10},{9,11},{10,... | collective-permute-start | bytes 1572872 | tf_op jit(solution)/shard_map/ppermute | solution.py:34

commit v5 on v4

--- a/solution.py
+++ b/solution.py
@@ -261,7 +261,7 @@
     )
 
 
-GROUP = 4
+GROUP = 8
 PAIRS = 64
 PLACES = 32
 
@@ -488,26 +488,26 @@
     coef = upper_coef.reshape(2, 4, 2, -1, columns)
     angle = phase.transpose(1, 2, 0).reshape(ANGLES, -1)
     to_z, to_both, to_core, kept, matrices = stage(angle, cone_used.T, coef, transfer)
-    from_core = permute(to_core, FLIP_CORE)
+    transfer_core = permute(transfer, FLIP_CORE)
     from_z = permute(to_z, FLIP_Z)
     from_both = permute(to_both, FLIP_BOTH)
 
     below = permute(charges, UP)
     above = permute(charges, DOWN)
     neighbours = neighbours.T
-    transfer_outer = permute(tied(matrices, from_core), FLIP_OUTER)
+    transfer_outer = permute(tied(matrices, transfer_core), FLIP_OUTER)
     reals, imags, basis, sums, beside, wrapping = own_sums(
-        neighbours, near_real, near_imag, leaf_basis, charges, [from_core]
+        neighbours, near_real, near_imag, leaf_basis, charges, [transfer_core, to_z]
     )
     token = beside
     kept_matrices = tied(matrices, token)
-    transfer_core = permute(kept_matrices, FLIP_CORE)
+    from_core = permute(tied(to_core, token), FLIP_CORE)
     transfer_both = permute(tied(transfer_outer, token), FLIP_CORE)
+    coefs = [kept, from_core, from_z, from_both]
     moves = [kept_matrices, transfer_core, transfer_outer, transfer_both]
-    coefs = [kept, from_core, from_z, from_both]
     crossing = crossing_charges(below, above, [token])
     token, sums = more_sums(beside, reals, imags, [below, above], sums)
-    crossing = tied(crossing, from_z, from_both, transfer_core, transfer_both, token)
+    crossing = tied(crossing, from_z, from_both, from_core, transfer_both, token)
     wrapped = permute(crossing, NEXT_ROW)
 
     far_first, far_second = transfer_terms([2], coefs, moves, [crossing])

time: 69.9 us -> 68.4 us (0.979)
  waiting for transfers between devices: 22.8 us -> 21.2 us
    ppermute x13, waiting for transfers between devices: 22.8 us -> 21.2 us  [permute(): return lax.ppermute(array, AXES, pairs)]
where the time goes in v5:
time: 68.4 us; the launch traced here: 68.2 us
  Pallas kernels  30.1 us (44%)
  waiting for transfers between devices  21.2 us (31%)
  starting transfers between devices  16.6 us (24%)
    ppermute x13, waiting for transfers between devices, permute(): return lax.ppermute(array, AXES, pairs)  21.2 us
    ppermute x13, starting transfers between devices, permute(): return lax.ppermute(array, AXES, pairs)  16.6 us
    pallas_call x1, Pallas kernels, own_sums(): pl.pallas_call(kernel, out_shape=(pltpu.VMEM(near_real.shape, BF16), pltp...  12.2 us
    pallas_call x3, Pallas kernels, transfer_terms(): pl.pallas_call(kernel, out_shape=(out,) * (2 * len(offsets)), in_specs=[I...  6.98 us
    pallas_call x2, Pallas kernels, more_sums(): pl.pallas_call(kernel, out_shape=(jax.ShapeDtypeStruct(listed.shape, jnp....  6.35 us
    pallas_call x1, Pallas kernels, stage(): pl.pallas_call(stage_kernel, out_shape=outs, in_specs=[IN_HBM] * 4, out_s...  2.15 us
    pallas_call x1, Pallas kernels, apply_leaves(): pl.pallas_call(apply_kernel, out_shape=jax.ShapeDtypeStruct(sums.shape, B...  2 us
  transfers between devices with their start and end apart: 13, of which 6 were waited for; matrix products, arithmetic and copies ran while one was open for 0% of the time, Pallas kernels for 41%

profile of v5, /device:TPU:24, one launch (start us, length us, event | category | flops | bytes accessed | tf_op | source)
XLA Modules:
  0.0 68.2 jit_solution(17209274808086754551)
XLA Ops:
  0.0 0.0 collective-permute-start.1
  0.0 3.0 %collective-permute-start.2 = (bf16[16,256,256]{2,1,0:T(8,128)(2,1)}, bf16[16,256,256]{2,1,0:T(8,128)(2,1)S(1)}, u32[]{:S(2)}, u32[]{:S(2)}) collective-permute-start(bf16[16,256,256]{2,1,0:T(8,128)(2,1)} %refs_4_.1), channel_id=1, source_target_pairs={{0,7},{1,0},{2,1},{3,2},{4,3},{5,4},{6,5},{7,6},{8,15},{9,8},{10,9... | collective-permute-start | bytes 6291464 | tf_op jit(solution)/shard_map/ppermute | solution.py:34
  3.0 0.0 collective-permute-start
  3.0 0.0 copy-start
  3.0 2.2 %stage.1 = (bf16[2064,128]{1,0:T(8,128)(2,1)S(1)}, bf16[2064,128]{1,0:T(8,128)(2,1)S(1)}, bf16[2064,128]{1,0:T(8,128)(2,1)S(1)}, bf16[2064,128]{1,0:T(8,128)(2,1)S(1)}, bf16[2,8,128,128]{3,2,1,0:T(8,128)(2,1)S(1)}) custom-call(f32[16,32]{1,0:T(8,128)} %bitcast.8, s32[2,32]{1,0:T(2,128)} %bitcast.9, bf16[2,4,2,512,128]{4,3,2,1,0:T(8,128)(2,1)} %bitcast.7, ...), custom_call_target="tpu_custom_call" | custom-call | bytes 1024 | tf_op jit(solution)/shard_map/stage/pallas_call | solution.py:105
  5.2 1.0 %collective-permute-done.refs_5_.refs_1_ = bf16[2,8,128,128]{3,2,1,0:T(8,128)(2,1)S(1)} collective-permute-done((bf16[2,8,128,128]{3,2,1,0:T(8,128)(2,1)}, bf16[2,8,128,128]{3,2,1,0:T(8,128)(2,1)S(1)}, u32[]{:S(2)}, u32[]{:S(2)}) %collective-permute-start) | collective-permute-done | bytes 524320 | tf_op jit(solution)/shard_map/ppermute | solution.py:34
  6.2 4.0 %collective-permute-start.6 = (bf16[2,8,128,128]{3,2,1,0:T(8,128)(2,1)S(1)}, bf16[2,8,128,128]{3,2,1,0:T(8,128)(2,1)S(1)}, u32[]{:S(2)}, u32[]{:S(2)}) collective-permute-start(bf16[2,8,128,128]{3,2,1,0:T(8,128)(2,1)S(1)} %tied.6), channel_id=1, source_target_pairs={{0,72},{1,73},{2,74},{3,75},{4,76},{5,77},{6,78},{7,79},{8,64},{9,... | collective-permute-start | bytes 1572872 | tf_op jit(solution)/shard_map/ppermute | solution.py:34
  10.3 0.0 collective-permute-start.3
  10.3 1.2 %collective-permute-start.4 = (bf16[2064,128]{1,0:T(8,128)(2,1)S(1)}, bf16[2064,128]{1,0:T(8,128)(2,1)S(1)}, u32[]{:S(2)}, u32[]{:S(2)}) collective-permute-start(bf16[2064,128]{1,0:T(8,128)(2,1)S(1)} %get-tuple-element.32), channel_id=1, source_target_pairs={{0,9},{1,8},{2,11},{3,10},{4,13},{5,12},{6,15},{7,14},{8,1},{9,0},... | collective-permute-start | bytes 1585160 | tf_op jit(solution)/shard_map/ppermute | solution.py:34
  11.5 0.0 copy-done
  11.5 12.2 %own_sums.1 = (bf16[16,4,256,256]{3,2,1,0:T(8,128)(2,1)S(1)}, bf16[16,4,256,256]{3,2,1,0:T(8,128)(2,1)S(1)}, bf16[16,2,256,128]{3,2,1,0:T(8,128)(2,1)S(1)}, f32[...) custom-call(s32[4,16]{1,0:T(4,128)S(1)} %bitcast.6, bf16[16,4,256,256]{3,2,1,0:T(8,128)(2,1)} %refs_1_.1, ...), custom_call_target="tpu_custom_call" | custom-call | bytes 1024 | tf_op jit(solution)/shard_map/own_sums/pallas_call | solution.py:379
  23.7 0.0 collective-permute-done.6.refs_6_
  23.7 1.0 %collective-permute-start.5 = (bf16[2064,128]{1,0:T(8,128)(2,1)S(1)}, bf16[2064,128]{1,0:T(8,128)(2,1)S(1)}, u32[]{:S(2)}, u32[]{:S(2)}) collective-permute-start(bf16[2064,128]{1,0:T(8,128)(2,1)S(1)} %tied.5), channel_id=1, source_target_pairs={{0,1},{1,0},{2,3},{3,2},{4,5},{5,4},{6,7},{7,6},{8,9},{9,8},{10,11... | collective-permute-start | bytes 1585160 | tf_op jit(solution)/shard_map/ppermute | solution.py:34
  24.8 2.1 %collective-permute-done.1.refs_0_.refs_3_ = bf16[16,256,256]{2,1,0:T(8,128)(2,1)S(1)} collective-permute-done((bf16[16,256,256]{2,1,0:T(8,128)(2,1)}, bf16[16,256,256]{2,1,0:T(8,128)(2,1)S(1)}, u32[]{:S(2)}, u32[]{:S(2)}) %collective-permute-start.1) | collective-permute-done | bytes 2097184 | tf_op jit(solution)/shard_map/ppermute | solution.py:34
  26.9 0.0 collective-permute-start.7
  26.9 0.0 collective-permute-done.2.refs_1_.refs_4_
  26.9 0.3 crossing_charges.1.refs_0_
  27.2 3.3 %more_sums.2 = (s32[65]{0:T(128)S(1)}, f32[16,256,256]{2,1,0:T(8,128)S(1)}) custom-call(s32[65]{0:T(128)S(1)} %get-tuple-element.31.refs_2_.refs_1_.refs_0_, bf16[16,4,256,256]{3,2,1,0:T(8,128)(2,1)S(1)} %get-tuple-element.29.refs_1_, bf16[16,4,256,256]{3,2,1,0:T(8,128)(2,1)S(1)} %get-tuple-element.30.refs_2_, ...), custom_call_target="tpu_custom_call", output_to_operand_aliasing={{1}: (5, {})} | custom-call | bytes 1024 | tf_op jit(solution)/shard_map/more_sums/pallas_call | solution.py:430
  30.5 0.0 collective-permute-done.3.refs_1_.refs_2_
  30.5 3.7 %collective-permute-done.4.refs_2_.refs_3_ = bf16[2064,128]{1,0:T(8,128)(2,1)S(1)} collective-permute-done((bf16[2064,128]{1,0:T(8,128)(2,1)S(1)}, bf16[2064,128]{1,0:T(8,128)(2,1)S(1)}, u32[]{:S(2)}, u32[]{:S(2)}) %collective-permute-start.4) | collective-permute-done | bytes 528416 | tf_op jit(solution)/shard_map/ppermute | solution.py:34
  34.2 0.0 collective-permute-done.5.refs_3_.refs_1_
  34.2 0.0 collective-permute-done.7.refs_4_.refs_7_
  34.2 2.6 %collective-permute-start.8 = (bf16[16,256,256]{2,1,0:T(8,128)(2,1)S(1)}, bf16[16,256,256]{2,1,0:T(8,128)(2,1)S(1)}, u32[]{:S(2)}, u32[]{:S(2)}) collective-permute-start(bf16[16,256,256]{2,1,0:T(8,128)(2,1)S(1)} %tied.8.refs_8_), channel_id=1, source_target_pairs={{0,8},{8,16},{16,24},{24,32},{32,40},{40,48},{48,56},{56,64},{64,7... | collective-permute-start | bytes 6291464 | tf_op jit(solution)/shard_map/ppermute | solution.py:34
  36.8 1.8 %transfer_terms.4 = (bf16[8,128,128]{2,1,0:T(8,128)(2,1)S(1)}, bf16[8,128,128]{2,1,0:T(8,128)(2,1)S(1)}) custom-call(bf16[2064,128]{1,0:T(8,128)(2,1)S(1)} %get-tuple-element.38.refs_0_, bf16[2064,128]{1,0:T(8,128)(2,1)S(1)} %collective-permute-done.5.refs_3_.refs_1_, bf16[2064,128]{1,0:T(8,128)(2,1)S(1)} %collective-permute-done.3.refs_1_.refs_2_, ...), custom_call_target="tpu_custom_call" | custom-call | bytes 1024 | tf_op jit(solution)/shard_map/transfer_terms/pallas_call | solution.py:225
  38.7 0.1 collective-permute-start.10
  38.8 2.0 %collective-permute-start.9 = (bf16[8,128,128]{2,1,0:T(8,128)(2,1)S(1)}, bf16[8,128,128]{2,1,0:T(8,128)(2,1)S(1)}, u32[]{:S(2)}, u32[]{:S(2)}) collective-permute-start(bf16[8,128,128]{2,1,0:T(8,128)(2,1)S(1)} %get-tuple-element.41), channel_id=1, source_target_pairs={{0,2},{1,3},{2,4},{3,5},{4,6},{5,7},{6,0},{7,1},{8,10},{9,11},{10,... | collective-permute-start | bytes 786440 | tf_op jit(solution)/shard_map/ppermute | solution.py:34
  40.8 3.3 %transfer_terms.3 = (bf16[8,128,128]{2,1,0:T(8,128)(2,1)S(1)}, bf16[8,128,128]{2,1,0:T(8,128)(2,1)S(1)}, bf16[8,128,128]{2,1,0:T(8,128)(2,1)S(1)}, bf16[8,128,128]{2,1,0:T(8,128)(2,1)S(1)}) custom-call(bf16[2064,128]{1,0:T(8,128)(2,1)S(1)} %get-tuple-element.38.refs_0_, bf16[2064,128]{1,0:T(8,128)(2,1)S(1)} %collective-permute-done.5.refs_3_.refs_1_, ...), custom_call_target="tpu_custom_call" | custom-call | bytes 1024 | tf_op jit(solution)/shard_map/transfer_terms/pallas_call | solution.py:225
  44.1 2.0 %collective-permute-done.10.arrived = bf16[8,128,128]{2,1,0:T(8,128)(2,1)S(1)} collective-permute-done((bf16[8,128,128]{2,1,0:T(8,128)(2,1)S(1)}, bf16[8,128,128]{2,1,0:T(8,128)(2,1)S(1)}, u32[]{:S(2)}, u32[]{:S(2)}) %collective-permute-start.10) | collective-permute-done | bytes 262176 | tf_op jit(solution)/shard_map/ppermute | solution.py:34
  46.1 0.1 with_arrived.3.refs_9_
  46.2 1.8 %collective-permute-start.12 = (bf16[2,8,128,128]{3,2,1,0:T(8,128)(2,1)S(1)}, bf16[2,8,128,128]{3,2,1,0:T(8,128)(2,1)S(1)}, u32[]{:S(2)}, u32[]{:S(2)}) collective-permute-start(bf16[2,8,128,128]{3,2,1,0:T(8,128)(2,1)S(1)} %with_arrived.3.refs_9_), channel_id=1, source_target_pairs={{0,6},{1,7},{2,0},{3,1},{4,2},{5,3},{6,4},{7,5},{8,14},{9,15},{10,... | collective-permute-start | bytes 1572872 | tf_op jit(solution)/shard_map/ppermute | solution.py:34
  48.0 0.4 collective-permute-done.9.arrived
  48.4 0.1 with_arrived.2.refs_8_
  48.4 0.9 %collective-permute-start.11 = (bf16[2,8,128,128]{3,2,1,0:T(8,128)(2,1)S(1)}, bf16[2,8,128,128]{3,2,1,0:T(8,128)(2,1)S(1)}, u32[]{:S(2)}, u32[]{:S(2)}) collective-permute-start(bf16[2,8,128,128]{3,2,1,0:T(8,128)(2,1)S(1)} %with_arrived.2.refs_8_), channel_id=1, source_target_pairs={{0,2},{1,3},{2,4},{3,5},{4,6},{5,7},{6,0},{7,1},{8,10},{9,11},{10,... | collective-permute-start | bytes 1572872 | tf_op jit(solution)/shard_map/ppermute | solution.py:34
  49.3 1.8 %transfer_terms.5 = (bf16[8,128,128]{2,1,0:T(8,128)(2,1)S(1)}, bf16[8,128,128]{2,1,0:T(8,128)(2,1)S(1)}) custom-call(bf16[2064,128]{1,0:T(8,128)(2,1)S(1)} %get-tuple-element.38.refs_0_, bf16[2064,128]{1,0:T(8,128)(2,1)S(1)} %collective-permute-done.5.refs_3_.refs_1_, bf16[2064,128]{1,0:T(8,128)(2,1)S(1)} %collective-permute-done.3.refs_1_.refs_2_, ...), custom_call_target="tpu_custom_call" | custom-call | bytes 1024 | tf_op jit(solution)/shard_map/transfer_terms/pallas_call | solution.py:225
  51.1 11.9 %collective-permute-done.8.refs_3_ = bf16[16,256,256]{2,1,0:T(8,128)(2,1)S(1)} collective-permute-done((bf16[16,256,256]{2,1,0:T(8,128)(2,1)S(1)}, bf16[16,256,256]{2,1,0:T(8,128)(2,1)S(1)}, u32[]{:S(2)}, u32[]{:S(2)}) %collective-permute-start.8) | collective-permute-done | bytes 2097184 | tf_op jit(solution)/shard_map/ppermute | solution.py:34
  63.1 3.1 %more_sums.3 = (s32[65]{0:T(128)}, f32[16,256,256]{2,1,0:T(8,128)S(1)}) custom-call(s32[65]{0:T(128)S(1)} %get-tuple-element.28.refs_0_, bf16[16,4,256,256]{3,2,1,0:T(8,128)(2,1)S(1)} %get-tuple-element.29.refs_1_, bf16[16,4,256,256]{3,2,1,0:T(8,128)(2,1)S(1)} %get-tuple-element.30.refs_2_, ...), custom_call_target="tpu_custom_call", output_to_operand_aliasing={{1}: (4, {})} | custom-call | bytes 1024 | tf_op jit(solution)/shard_map/more_sums/pallas_call | solution.py:430
  66.1 0.0 collective-permute-done.12.leaf2
  66.1 0.0 collective-permute-done.11.leaf1
  66.2 2.0 %apply_leaves.1 = bf16[16,256,256]{2,1,0:T(8,128)(2,1)} custom-call(f32[16,256,256]{2,1,0:T(8,128)S(1)} %get-tuple-element.46.sums, bf16[16,2,256,128]{3,2,1,0:T(8,128)(2,1)S(1)} %get-tuple-element.47.basis, bf16[8,128,128]{2,1,0:T(8,128)(2,1)S(1)} %get-tuple-element.45.refs_5_.leaf00, bf16[8,128,128]{2,1,0:T(8,128)(2,1)S(1)} %get-tuple-element.48.leaf01, ...), custom_call_target="tpu_custom_call" | custom-call | bytes 1024 | tf_op jit(solution)/shard_map/apply_leaves/pallas_call | solution.py:472
  (7 shorter events, 0.1 us)
Async XLA Ops:
  0.0 26.9 %collective-permute-start.1 = (bf16[16,256,256]{2,1,0:T(8,128)(2,1)}, bf16[16,256,256]{2,1,0:T(8,128)(2,1)S(1)}, u32[]{:S(2)}, u32[]{:S(2)}) collective-permute-start(bf16[16,256,256]{2,1,0:T(8,128)(2,1)} %refs_4_.1), channel_id=1, source_target_pairs={{0,1},{1,2},{2,3},{3,4},{4,5},{5,6},{6,7},{7,0},{8,9},{9,10},{10,1... | collective-permute-start | bytes 6291464 | tf_op jit(solution)/shard_map/ppermute | solution.py:34
  0.0 26.9 %collective-permute-start.2 = (bf16[16,256,256]{2,1,0:T(8,128)(2,1)}, bf16[16,256,256]{2,1,0:T(8,128)(2,1)S(1)}, u32[]{:S(2)}, u32[]{:S(2)}) collective-permute-start(bf16[16,256,256]{2,1,0:T(8,128)(2,1)} %refs_4_.1), channel_id=1, source_target_pairs={{0,7},{1,0},{2,1},{3,2},{4,3},{5,4},{6,5},{7,6},{8,15},{9,8},{10,9... | collective-permute-start | bytes 6291464 | tf_op jit(solution)/shard_map/ppermute | solution.py:34
  3.0 3.3 %collective-permute-start = (bf16[2,8,128,128]{3,2,1,0:T(8,128)(2,1)}, bf16[2,8,128,128]{3,2,1,0:T(8,128)(2,1)S(1)}, u32[]{:S(2)}, u32[]{:S(2)}) collective-permute-start(bf16[2,8,128,128]{3,2,1,0:T(8,128)(2,1)} %transfer.1), channel_id=1, source_target_pairs={{0,1},{1,0},{2,3},{3,2},{4,5},{5,4},{6,7},{7,6},{8,9},{9,8},{10,11... | collective-permute-start | bytes 1572872 | tf_op jit(solution)/shard_map/ppermute | solution.py:34
  3.0 8.5 %copy-start = (s32[16,4]{0,1:T(4,128)S(1)}, s32[16,4]{0,1:T(4,128)}, u32[]{:S(2)}) copy-start(s32[16,4]{0,1:T(4,128)} %param.15) | copy-start | bytes 772
  6.2 17.5 %collective-permute-start.6 = (bf16[2,8,128,128]{3,2,1,0:T(8,128)(2,1)S(1)}, bf16[2,8,128,128]{3,2,1,0:T(8,128)(2,1)S(1)}, u32[]{:S(2)}, u32[]{:S(2)}) collective-permute-start(bf16[2,8,128,128]{3,2,1,0:T(8,128)(2,1)S(1)} %tied.6), channel_id=1, source_target_pairs={{0,72},{1,73},{2,74},{3,75},{4,76},{5,77},{6,78},{7,79},{8,64},{9,... | collective-permute-start | bytes 1572872 | tf_op jit(solution)/shard_map/ppermute | solution.py:34
  10.3 20.2 %collective-permute-start.3 = (bf16[2064,128]{1,0:T(8,128)(2,1)S(1)}, bf16[2064,128]{1,0:T(8,128)(2,1)S(1)}, u32[]{:S(2)}, u32[]{:S(2)}) collective-permute-start(bf16[2064,128]{1,0:T(8,128)(2,1)S(1)} %get-tuple-element.27.refs_6_), channel_id=1, source_target_pairs={{0,8},{1,9},{2,10},{3,11},{4,12},{5,13},{6,14},{7,15},{8,0},{9,1},... | collective-permute-start | bytes 1585160 | tf_op jit(solution)/shard_map/ppermute | solution.py:34
  10.3 24.0 %collective-permute-start.4 = (bf16[2064,128]{1,0:T(8,128)(2,1)S(1)}, bf16[2064,128]{1,0:T(8,128)(2,1)S(1)}, u32[]{:S(2)}, u32[]{:S(2)}) collective-permute-start(bf16[2064,128]{1,0:T(8,128)(2,1)S(1)} %get-tuple-element.32), channel_id=1, source_target_pairs={{0,9},{1,8},{2,11},{3,10},{4,13},{5,12},{6,15},{7,14},{8,1},{9,0},... | collective-permute-start | bytes 1585160 | tf_op jit(solution)/shard_map/ppermute | solution.py:34
  23.7 10.5 %collective-permute-start.5 = (bf16[2064,128]{1,0:T(8,128)(2,1)S(1)}, bf16[2064,128]{1,0:T(8,128)(2,1)S(1)}, u32[]{:S(2)}, u32[]{:S(2)}) collective-permute-start(bf16[2064,128]{1,0:T(8,128)(2,1)S(1)} %tied.5), channel_id=1, source_target_pairs={{0,1},{1,0},{2,3},{3,2},{4,5},{5,4},{6,7},{7,6},{8,9},{9,8},{10,11... | collective-permute-start | bytes 1585160 | tf_op jit(solution)/shard_map/ppermute | solution.py:34
  26.9 7.4 %collective-permute-start.7 = (bf16[2,8,128,128]{3,2,1,0:T(8,128)(2,1)S(1)}, bf16[2,8,128,128]{3,2,1,0:T(8,128)(2,1)S(1)}, u32[]{:S(2)}, u32[]{:S(2)}) collective-permute-start(bf16[2,8,128,128]{3,2,1,0:T(8,128)(2,1)S(1)} %tied.7), channel_id=1, source_target_pairs={{0,1},{1,0},{2,3},{3,2},{4,5},{5,4},{6,7},{7,6},{8,9},{9,8},{10,11... | collective-permute-start | bytes 1572872 | tf_op jit(solution)/shard_map/ppermute | solution.py:34
  34.2 28.8 %collective-permute-start.8 = (bf16[16,256,256]{2,1,0:T(8,128)(2,1)S(1)}, bf16[16,256,256]{2,1,0:T(8,128)(2,1)S(1)}, u32[]{:S(2)}, u32[]{:S(2)}) collective-permute-start(bf16[16,256,256]{2,1,0:T(8,128)(2,1)S(1)} %tied.8.refs_8_), channel_id=1, source_target_pairs={{0,8},{8,16},{16,24},{24,32},{32,40},{40,48},{48,56},{56,64},{64,7... | collective-permute-start | bytes 6291464 | tf_op jit(solution)/shard_map/ppermute | solution.py:34
  38.7 7.4 %collective-permute-start.10 = (bf16[8,128,128]{2,1,0:T(8,128)(2,1)S(1)}, bf16[8,128,128]{2,1,0:T(8,128)(2,1)S(1)}, u32[]{:S(2)}, u32[]{:S(2)}) collective-permute-start(bf16[8,128,128]{2,1,0:T(8,128)(2,1)S(1)} %get-tuple-element.44), channel_id=1, source_target_pairs={{0,6},{1,7},{2,0},{3,1},{4,2},{5,3},{6,4},{7,5},{8,14},{9,15},{10,... | collective-permute-start | bytes 786440 | tf_op jit(solution)/shard_map/ppermute | solution.py:34
  38.8 9.6 %collective-permute-start.9 = (bf16[8,128,128]{2,1,0:T(8,128)(2,1)S(1)}, bf16[8,128,128]{2,1,0:T(8,128)(2,1)S(1)}, u32[]{:S(2)}, u32[]{:S(2)}) collective-permute-start(bf16[8,128,128]{2,1,0:T(8,128)(2,1)S(1)} %get-tuple-element.41), channel_id=1, source_target_pairs={{0,2},{1,3},{2,4},{3,5},{4,6},{5,7},{6,0},{7,1},{8,10},{9,11},{10,... | collective-permute-start | bytes 786440 | tf_op jit(solution)/shard_map/ppermute | solution.py:34
  46.2 20.0 %collective-permute-start.12 = (bf16[2,8,128,128]{3,2,1,0:T(8,128)(2,1)S(1)}, bf16[2,8,128,128]{3,2,1,0:T(8,128)(2,1)S(1)}, u32[]{:S(2)}, u32[]{:S(2)}) collective-permute-start(bf16[2,8,128,128]{3,2,1,0:T(8,128)(2,1)S(1)} %with_arrived.3.refs_9_), channel_id=1, source_target_pairs={{0,6},{1,7},{2,0},{3,1},{4,2},{5,3},{6,4},{7,5},{8,14},{9,15},{10,... | collective-permute-start | bytes 1572872 | tf_op jit(solution)/shard_map/ppermute | solution.py:34
  48.4 17.7 %collective-permute-start.11 = (bf16[2,8,128,128]{3,2,1,0:T(8,128)(2,1)S(1)}, bf16[2,8,128,128]{3,2,1,0:T(8,128)(2,1)S(1)}, u32[]{:S(2)}, u32[]{:S(2)}) collective-permute-start(bf16[2,8,128,128]{3,2,1,0:T(8,128)(2,1)S(1)} %with_arrived.2.refs_8_), channel_id=1, source_target_pairs={{0,2},{1,3},{2,4},{3,5},{4,6},{5,7},{6,0},{7,1},{8,10},{9,11},{10,... | collective-permute-start | bytes 1572872 | tf_op jit(solution)/shard_map/ppermute | solution.py:34

commit v6 on v5

--- a/solution.py
+++ b/solution.py
@@ -451,16 +451,13 @@
 
     for j, own in enumerate((leaf00, leaf01)):
 
-        @pl.loop(0, count // 8)
-        def _(part):
-            for i in range(4):
-                o = 4 * part + i
-                leaf = j * (count // 2) + o
-                coef = own[o].astype(F32) + leaf1[1 - j, o].astype(F32) + leaf2[j, o].astype(F32)
-                coef = coef.astype(BF16)
-                far = [jnp.dot(basis[leaf, s], coef, preferred_element_type=F32) for s in range(2)]
-                totals[leaf] = (sums[leaf] + jnp.concatenate(far, axis=1)).astype(BF16)
-                store(leaf).start()
+        for o in range(count // 2):
+            leaf = j * (count // 2) + o
+            coef = own[o].astype(F32) + leaf1[1 - j, o].astype(F32) + leaf2[j, o].astype(F32)
+            coef = coef.astype(BF16)
+            far = [jnp.dot(basis[leaf, s], coef, preferred_element_type=F32) for s in range(2)]
+            totals[leaf] = (sums[leaf] + jnp.concatenate(far, axis=1)).astype(BF16)
+            store(leaf).start()
 
     for leaf in range(count):
         store(leaf).wait()

time: 68.4 us -> 68.4 us (level)
  starting transfers between devices: 16.6 us -> 15.7 us
    pallas_call x1, Pallas kernels: 12.2 us -> 13.1 us  [own_sums(): pl.pallas_call(kernel, out_shape=(pltpu.VMEM(near_real.shape, BF16), pltp...]
    ppermute x13, starting transfers between devices: 16.6 us -> 15.7 us  [permute(): return lax.ppermute(array, AXES, pairs)]
  transfers between devices with their start and end apart: 13 -> 13, of which waited for: 6 -> 6; matrix products, arithmetic and copies ran while one was open for 0% -> 0% of each run, Pallas kernels for 41% -> 43%
where the time goes in v6:
time: 68.4 us; the launch traced here: 67.8 us
  Pallas kernels  30.6 us (45%)
  waiting for transfers between devices  21.2 us (31%)
  starting transfers between devices  15.7 us (23%)
    ppermute x13, waiting for transfers between devices, permute(): return lax.ppermute(array, AXES, pairs)  21.2 us
    ppermute x13, starting transfers between devices, permute(): return lax.ppermute(array, AXES, pairs)  15.7 us
    pallas_call x1, Pallas kernels, own_sums(): pl.pallas_call(kernel, out_shape=(pltpu.VMEM(near_real.shape, BF16), pltp...  13.1 us
    pallas_call x3, Pallas kernels, transfer_terms(): pl.pallas_call(kernel, out_shape=(out,) * (2 * len(offsets)), in_specs=[I...  6.98 us
    pallas_call x2, Pallas kernels, more_sums(): pl.pallas_call(kernel, out_shape=(jax.ShapeDtypeStruct(listed.shape, jnp....  6.34 us
    pallas_call x1, Pallas kernels, stage(): pl.pallas_call(stage_kernel, out_shape=outs, in_specs=[IN_HBM] * 4, out_s...  2.15 us
    pallas_call x1, Pallas kernels, apply_leaves(): pl.pallas_call(apply_kernel, out_shape=jax.ShapeDtypeStruct(sums.shape, B...  1.64 us
  transfers between devices with their start and end apart: 13, of which 6 were waited for; matrix products, arithmetic and copies ran while one was open for 0% of the time, Pallas kernels for 43%

profile of v6, /device:TPU:24, one launch (start us, length us, event | category | flops | bytes accessed | tf_op | source)
XLA Modules:
  0.0 67.8 jit_solution(2525047495455246089)
XLA Ops:
  0.0 0.0 collective-permute-start.1
  0.0 3.0 %collective-permute-start.2 = (bf16[16,256,256]{2,1,0:T(8,128)(2,1)}, bf16[16,256,256]{2,1,0:T(8,128)(2,1)S(1)}, u32[]{:S(2)}, u32[]{:S(2)}) collective-permute-start(bf16[16,256,256]{2,1,0:T(8,128)(2,1)} %refs_4_.1), channel_id=1, source_target_pairs={{0,7},{1,0},{2,1},{3,2},{4,3},{5,4},{6,5},{7,6},{8,15},{9,8},{10,9... | collective-permute-start | bytes 6291464 | tf_op jit(solution)/shard_map/ppermute | solution.py:34
  3.0 0.0 collective-permute-start
  3.0 0.0 copy-start
  3.0 2.2 %stage.1 = (bf16[2064,128]{1,0:T(8,128)(2,1)S(1)}, bf16[2064,128]{1,0:T(8,128)(2,1)S(1)}, bf16[2064,128]{1,0:T(8,128)(2,1)S(1)}, bf16[2064,128]{1,0:T(8,128)(2,1)S(1)}, bf16[2,8,128,128]{3,2,1,0:T(8,128)(2,1)S(1)}) custom-call(f32[16,32]{1,0:T(8,128)} %bitcast.8, s32[2,32]{1,0:T(2,128)} %bitcast.9, bf16[2,4,2,512,128]{4,3,2,1,0:T(8,128)(2,1)} %bitcast.7, ...), custom_call_target="tpu_custom_call" | custom-call | bytes 1024 | tf_op jit(solution)/shard_map/stage/pallas_call | solution.py:105
  5.2 1.0 %collective-permute-done.refs_5_.refs_1_ = bf16[2,8,128,128]{3,2,1,0:T(8,128)(2,1)S(1)} collective-permute-done((bf16[2,8,128,128]{3,2,1,0:T(8,128)(2,1)}, bf16[2,8,128,128]{3,2,1,0:T(8,128)(2,1)S(1)}, u32[]{:S(2)}, u32[]{:S(2)}) %collective-permute-start) | collective-permute-done | bytes 524320 | tf_op jit(solution)/shard_map/ppermute | solution.py:34
  6.2 4.0 %collective-permute-start.6 = (bf16[2,8,128,128]{3,2,1,0:T(8,128)(2,1)S(1)}, bf16[2,8,128,128]{3,2,1,0:T(8,128)(2,1)S(1)}, u32[]{:S(2)}, u32[]{:S(2)}) collective-permute-start(bf16[2,8,128,128]{3,2,1,0:T(8,128)(2,1)S(1)} %tied.6), channel_id=1, source_target_pairs={{0,72},{1,73},{2,74},{3,75},{4,76},{5,77},{6,78},{7,79},{8,64},{9,... | collective-permute-start | bytes 1572872 | tf_op jit(solution)/shard_map/ppermute | solution.py:34
  10.3 0.0 collective-permute-start.3
  10.3 1.2 %collective-permute-start.4 = (bf16[2064,128]{1,0:T(8,128)(2,1)S(1)}, bf16[2064,128]{1,0:T(8,128)(2,1)S(1)}, u32[]{:S(2)}, u32[]{:S(2)}) collective-permute-start(bf16[2064,128]{1,0:T(8,128)(2,1)S(1)} %get-tuple-element.32), channel_id=1, source_target_pairs={{0,9},{1,8},{2,11},{3,10},{4,13},{5,12},{6,15},{7,14},{8,1},{9,0},... | collective-permute-start | bytes 1585160 | tf_op jit(solution)/shard_map/ppermute | solution.py:34
  11.5 0.0 copy-done
  11.5 13.1 %own_sums.1 = (bf16[16,4,256,256]{3,2,1,0:T(8,128)(2,1)S(1)}, bf16[16,4,256,256]{3,2,1,0:T(8,128)(2,1)S(1)}, bf16[16,2,256,128]{3,2,1,0:T(8,128)(2,1)S(1)}, f32[...) custom-call(s32[4,16]{1,0:T(4,128)S(1)} %bitcast.6, bf16[16,4,256,256]{3,2,1,0:T(8,128)(2,1)} %refs_1_.1, ...), custom_call_target="tpu_custom_call" | custom-call | bytes 1024 | tf_op jit(solution)/shard_map/own_sums/pallas_call | solution.py:379
  24.5 0.0 collective-permute-done.6.refs_6_
  24.6 0.2 collective-permute-start.5
  24.8 2.1 %collective-permute-done.1.refs_0_.refs_3_ = bf16[16,256,256]{2,1,0:T(8,128)(2,1)S(1)} collective-permute-done((bf16[16,256,256]{2,1,0:T(8,128)(2,1)}, bf16[16,256,256]{2,1,0:T(8,128)(2,1)S(1)}, u32[]{:S(2)}, u32[]{:S(2)}) %collective-permute-start.1) | collective-permute-done | bytes 2097184 | tf_op jit(solution)/shard_map/ppermute | solution.py:34
  26.9 0.0 collective-permute-start.7
  26.9 0.0 collective-permute-done.2.refs_1_.refs_4_
  26.9 0.3 crossing_charges.1.refs_0_
  27.2 3.3 %more_sums.2 = (s32[65]{0:T(128)S(1)}, f32[16,256,256]{2,1,0:T(8,128)S(1)}) custom-call(s32[65]{0:T(128)S(1)} %get-tuple-element.31.refs_2_.refs_1_.refs_0_, bf16[16,4,256,256]{3,2,1,0:T(8,128)(2,1)S(1)} %get-tuple-element.29.refs_1_, bf16[16,4,256,256]{3,2,1,0:T(8,128)(2,1)S(1)} %get-tuple-element.30.refs_2_, ...), custom_call_target="tpu_custom_call", output_to_operand_aliasing={{1}: (5, {})} | custom-call | bytes 1024 | tf_op jit(solution)/shard_map/more_sums/pallas_call | solution.py:430
  30.5 0.0 collective-permute-done.3.refs_1_.refs_2_
  30.5 3.7 %collective-permute-done.4.refs_2_.refs_3_ = bf16[2064,128]{1,0:T(8,128)(2,1)S(1)} collective-permute-done((bf16[2064,128]{1,0:T(8,128)(2,1)S(1)}, bf16[2064,128]{1,0:T(8,128)(2,1)S(1)}, u32[]{:S(2)}, u32[]{:S(2)}) %collective-permute-start.4) | collective-permute-done | bytes 528416 | tf_op jit(solution)/shard_map/ppermute | solution.py:34
  34.2 0.0 collective-permute-done.5.refs_3_.refs_1_
  34.2 0.0 collective-permute-done.7.refs_4_.refs_7_
  34.2 2.6 %collective-permute-start.8 = (bf16[16,256,256]{2,1,0:T(8,128)(2,1)S(1)}, bf16[16,256,256]{2,1,0:T(8,128)(2,1)S(1)}, u32[]{:S(2)}, u32[]{:S(2)}) collective-permute-start(bf16[16,256,256]{2,1,0:T(8,128)(2,1)S(1)} %tied.8.refs_8_), channel_id=1, source_target_pairs={{0,8},{8,16},{16,24},{24,32},{32,40},{40,48},{48,56},{56,64},{64,7... | collective-permute-start | bytes 6291464 | tf_op jit(solution)/shard_map/ppermute | solution.py:34
  36.8 1.8 %transfer_terms.4 = (bf16[8,128,128]{2,1,0:T(8,128)(2,1)S(1)}, bf16[8,128,128]{2,1,0:T(8,128)(2,1)S(1)}) custom-call(bf16[2064,128]{1,0:T(8,128)(2,1)S(1)} %get-tuple-element.38.refs_0_, bf16[2064,128]{1,0:T(8,128)(2,1)S(1)} %collective-permute-done.5.refs_3_.refs_1_, bf16[2064,128]{1,0:T(8,128)(2,1)S(1)} %collective-permute-done.3.refs_1_.refs_2_, ...), custom_call_target="tpu_custom_call" | custom-call | bytes 1024 | tf_op jit(solution)/shard_map/transfer_terms/pallas_call | solution.py:225
  38.7 0.1 collective-permute-start.10
  38.8 2.0 %collective-permute-start.9 = (bf16[8,128,128]{2,1,0:T(8,128)(2,1)S(1)}, bf16[8,128,128]{2,1,0:T(8,128)(2,1)S(1)}, u32[]{:S(2)}, u32[]{:S(2)}) collective-permute-start(bf16[8,128,128]{2,1,0:T(8,128)(2,1)S(1)} %get-tuple-element.41), channel_id=1, source_target_pairs={{0,2},{1,3},{2,4},{3,5},{4,6},{5,7},{6,0},{7,1},{8,10},{9,11},{10,... | collective-permute-start | bytes 786440 | tf_op jit(solution)/shard_map/ppermute | solution.py:34
  40.8 3.3 %transfer_terms.3 = (bf16[8,128,128]{2,1,0:T(8,128)(2,1)S(1)}, bf16[8,128,128]{2,1,0:T(8,128)(2,1)S(1)}, bf16[8,128,128]{2,1,0:T(8,128)(2,1)S(1)}, bf16[8,128,128]{2,1,0:T(8,128)(2,1)S(1)}) custom-call(bf16[2064,128]{1,0:T(8,128)(2,1)S(1)} %get-tuple-element.38.refs_0_, bf16[2064,128]{1,0:T(8,128)(2,1)S(1)} %collective-permute-done.5.refs_3_.refs_1_, ...), custom_call_target="tpu_custom_call" | custom-call | bytes 1024 | tf_op jit(solution)/shard_map/transfer_terms/pallas_call | solution.py:225
  44.1 2.0 %collective-permute-done.10.arrived = bf16[8,128,128]{2,1,0:T(8,128)(2,1)S(1)} collective-permute-done((bf16[8,128,128]{2,1,0:T(8,128)(2,1)S(1)}, bf16[8,128,128]{2,1,0:T(8,128)(2,1)S(1)}, u32[]{:S(2)}, u32[]{:S(2)}) %collective-permute-start.10) | collective-permute-done | bytes 262176 | tf_op jit(solution)/shard_map/ppermute | solution.py:34
  46.1 0.1 with_arrived.3.refs_9_
  46.2 1.8 %collective-permute-start.12 = (bf16[2,8,128,128]{3,2,1,0:T(8,128)(2,1)S(1)}, bf16[2,8,128,128]{3,2,1,0:T(8,128)(2,1)S(1)}, u32[]{:S(2)}, u32[]{:S(2)}) collective-permute-start(bf16[2,8,128,128]{3,2,1,0:T(8,128)(2,1)S(1)} %with_arrived.3.refs_9_), channel_id=1, source_target_pairs={{0,6},{1,7},{2,0},{3,1},{4,2},{5,3},{6,4},{7,5},{8,14},{9,15},{10,... | collective-permute-start | bytes 1572872 | tf_op jit(solution)/shard_map/ppermute | solution.py:34
  48.0 0.4 collective-permute-done.9.arrived
  48.4 0.1 with_arrived.2.refs_8_
  48.4 0.9 %collective-permute-start.11 = (bf16[2,8,128,128]{3,2,1,0:T(8,128)(2,1)S(1)}, bf16[2,8,128,128]{3,2,1,0:T(8,128)(2,1)S(1)}, u32[]{:S(2)}, u32[]{:S(2)}) collective-permute-start(bf16[2,8,128,128]{3,2,1,0:T(8,128)(2,1)S(1)} %with_arrived.2.refs_8_), channel_id=1, source_target_pairs={{0,2},{1,3},{2,4},{3,5},{4,6},{5,7},{6,0},{7,1},{8,10},{9,11},{10,... | collective-permute-start | bytes 1572872 | tf_op jit(solution)/shard_map/ppermute | solution.py:34
  49.3 1.8 %transfer_terms.5 = (bf16[8,128,128]{2,1,0:T(8,128)(2,1)S(1)}, bf16[8,128,128]{2,1,0:T(8,128)(2,1)S(1)}) custom-call(bf16[2064,128]{1,0:T(8,128)(2,1)S(1)} %get-tuple-element.38.refs_0_, bf16[2064,128]{1,0:T(8,128)(2,1)S(1)} %collective-permute-done.5.refs_3_.refs_1_, bf16[2064,128]{1,0:T(8,128)(2,1)S(1)} %collective-permute-done.3.refs_1_.refs_2_, ...), custom_call_target="tpu_custom_call" | custom-call | bytes 1024 | tf_op jit(solution)/shard_map/transfer_terms/pallas_call | solution.py:225
  51.1 11.9 %collective-permute-done.8.refs_3_ = bf16[16,256,256]{2,1,0:T(8,128)(2,1)S(1)} collective-permute-done((bf16[16,256,256]{2,1,0:T(8,128)(2,1)S(1)}, bf16[16,256,256]{2,1,0:T(8,128)(2,1)S(1)}, u32[]{:S(2)}, u32[]{:S(2)}) %collective-permute-start.8) | collective-permute-done | bytes 2097184 | tf_op jit(solution)/shard_map/ppermute | solution.py:34
  63.1 3.1 %more_sums.3 = (s32[65]{0:T(128)}, f32[16,256,256]{2,1,0:T(8,128)S(1)}) custom-call(s32[65]{0:T(128)S(1)} %get-tuple-element.28.refs_0_, bf16[16,4,256,256]{3,2,1,0:T(8,128)(2,1)S(1)} %get-tuple-element.29.refs_1_, bf16[16,4,256,256]{3,2,1,0:T(8,128)(2,1)S(1)} %get-tuple-element.30.refs_2_, ...), custom_call_target="tpu_custom_call", output_to_operand_aliasing={{1}: (4, {})} | custom-call | bytes 1024 | tf_op jit(solution)/shard_map/more_sums/pallas_call | solution.py:430
  66.1 0.0 collective-permute-done.12.leaf2
  66.1 0.0 collective-permute-done.11.leaf1
  66.1 1.6 %apply_leaves.1 = bf16[16,256,256]{2,1,0:T(8,128)(2,1)} custom-call(f32[16,256,256]{2,1,0:T(8,128)S(1)} %get-tuple-element.46.sums, bf16[16,2,256,128]{3,2,1,0:T(8,128)(2,1)S(1)} %get-tuple-element.47.basis, bf16[8,128,128]{2,1,0:T(8,128)(2,1)S(1)} %get-tuple-element.45.refs_5_.leaf00, bf16[8,128,128]{2,1,0:T(8,128)(2,1)S(1)} %get-tuple-element.48.leaf01, ...), custom_call_target="tpu_custom_call" | custom-call | bytes 1024 | tf_op jit(solution)/shard_map/apply_leaves/pallas_call | solution.py:469
  (7 shorter events, 0.1 us)
Async XLA Ops:
  0.0 26.9 %collective-permute-start.1 = (bf16[16,256,256]{2,1,0:T(8,128)(2,1)}, bf16[16,256,256]{2,1,0:T(8,128)(2,1)S(1)}, u32[]{:S(2)}, u32[]{:S(2)}) collective-permute-start(bf16[16,256,256]{2,1,0:T(8,128)(2,1)} %refs_4_.1), channel_id=1, source_target_pairs={{0,1},{1,2},{2,3},{3,4},{4,5},{5,6},{6,7},{7,0},{8,9},{9,10},{10,1... | collective-permute-start | bytes 6291464 | tf_op jit(solution)/shard_map/ppermute | solution.py:34
  0.0 26.9 %collective-permute-start.2 = (bf16[16,256,256]{2,1,0:T(8,128)(2,1)}, bf16[16,256,256]{2,1,0:T(8,128)(2,1)S(1)}, u32[]{:S(2)}, u32[]{:S(2)}) collective-permute-start(bf16[16,256,256]{2,1,0:T(8,128)(2,1)} %refs_4_.1), channel_id=1, source_target_pairs={{0,7},{1,0},{2,1},{3,2},{4,3},{5,4},{6,5},{7,6},{8,15},{9,8},{10,9... | collective-permute-start | bytes 6291464 | tf_op jit(solution)/shard_map/ppermute | solution.py:34
  3.0 3.3 %collective-permute-start = (bf16[2,8,128,128]{3,2,1,0:T(8,128)(2,1)}, bf16[2,8,128,128]{3,2,1,0:T(8,128)(2,1)S(1)}, u32[]{:S(2)}, u32[]{:S(2)}) collective-permute-start(bf16[2,8,128,128]{3,2,1,0:T(8,128)(2,1)} %transfer.1), channel_id=1, source_target_pairs={{0,1},{1,0},{2,3},{3,2},{4,5},{5,4},{6,7},{7,6},{8,9},{9,8},{10,11... | collective-permute-start | bytes 1572872 | tf_op jit(solution)/shard_map/ppermute | solution.py:34
  3.0 8.5 %copy-start = (s32[16,4]{0,1:T(4,128)S(1)}, s32[16,4]{0,1:T(4,128)}, u32[]{:S(2)}) copy-start(s32[16,4]{0,1:T(4,128)} %param.15) | copy-start | bytes 772
  6.2 18.3 %collective-permute-start.6 = (bf16[2,8,128,128]{3,2,1,0:T(8,128)(2,1)S(1)}, bf16[2,8,128,128]{3,2,1,0:T(8,128)(2,1)S(1)}, u32[]{:S(2)}, u32[]{:S(2)}) collective-permute-start(bf16[2,8,128,128]{3,2,1,0:T(8,128)(2,1)S(1)} %tied.6), channel_id=1, source_target_pairs={{0,72},{1,73},{2,74},{3,75},{4,76},{5,77},{6,78},{7,79},{8,64},{9,... | collective-permute-start | bytes 1572872 | tf_op jit(solution)/shard_map/ppermute | solution.py:34
  10.3 20.2 %collective-permute-start.3 = (bf16[2064,128]{1,0:T(8,128)(2,1)S(1)}, bf16[2064,128]{1,0:T(8,128)(2,1)S(1)}, u32[]{:S(2)}, u32[]{:S(2)}) collective-permute-start(bf16[2064,128]{1,0:T(8,128)(2,1)S(1)} %get-tuple-element.27.refs_6_), channel_id=1, source_target_pairs={{0,8},{1,9},{2,10},{3,11},{4,12},{5,13},{6,14},{7,15},{8,0},{9,1},... | collective-permute-start | bytes 1585160 | tf_op jit(solution)/shard_map/ppermute | solution.py:34
  10.3 24.0 %collective-permute-start.4 = (bf16[2064,128]{1,0:T(8,128)(2,1)S(1)}, bf16[2064,128]{1,0:T(8,128)(2,1)S(1)}, u32[]{:S(2)}, u32[]{:S(2)}) collective-permute-start(bf16[2064,128]{1,0:T(8,128)(2,1)S(1)} %get-tuple-element.32), channel_id=1, source_target_pairs={{0,9},{1,8},{2,11},{3,10},{4,13},{5,12},{6,15},{7,14},{8,1},{9,0},... | collective-permute-start | bytes 1585160 | tf_op jit(solution)/shard_map/ppermute | solution.py:34
  24.6 9.7 %collective-permute-start.5 = (bf16[2064,128]{1,0:T(8,128)(2,1)S(1)}, bf16[2064,128]{1,0:T(8,128)(2,1)S(1)}, u32[]{:S(2)}, u32[]{:S(2)}) collective-permute-start(bf16[2064,128]{1,0:T(8,128)(2,1)S(1)} %tied.5), channel_id=1, source_target_pairs={{0,1},{1,0},{2,3},{3,2},{4,5},{5,4},{6,7},{7,6},{8,9},{9,8},{10,11... | collective-permute-start | bytes 1585160 | tf_op jit(solution)/shard_map/ppermute | solution.py:34
  26.9 7.4 %collective-permute-start.7 = (bf16[2,8,128,128]{3,2,1,0:T(8,128)(2,1)S(1)}, bf16[2,8,128,128]{3,2,1,0:T(8,128)(2,1)S(1)}, u32[]{:S(2)}, u32[]{:S(2)}) collective-permute-start(bf16[2,8,128,128]{3,2,1,0:T(8,128)(2,1)S(1)} %tied.7), channel_id=1, source_target_pairs={{0,1},{1,0},{2,3},{3,2},{4,5},{5,4},{6,7},{7,6},{8,9},{9,8},{10,11... | collective-permute-start | bytes 1572872 | tf_op jit(solution)/shard_map/ppermute | solution.py:34
  34.2 28.8 %collective-permute-start.8 = (bf16[16,256,256]{2,1,0:T(8,128)(2,1)S(1)}, bf16[16,256,256]{2,1,0:T(8,128)(2,1)S(1)}, u32[]{:S(2)}, u32[]{:S(2)}) collective-permute-start(bf16[16,256,256]{2,1,0:T(8,128)(2,1)S(1)} %tied.8.refs_8_), channel_id=1, source_target_pairs={{0,8},{8,16},{16,24},{24,32},{32,40},{40,48},{48,56},{56,64},{64,7... | collective-permute-start | bytes 6291464 | tf_op jit(solution)/shard_map/ppermute | solution.py:34
  38.7 7.4 %collective-permute-start.10 = (bf16[8,128,128]{2,1,0:T(8,128)(2,1)S(1)}, bf16[8,128,128]{2,1,0:T(8,128)(2,1)S(1)}, u32[]{:S(2)}, u32[]{:S(2)}) collective-permute-start(bf16[8,128,128]{2,1,0:T(8,128)(2,1)S(1)} %get-tuple-element.44), channel_id=1, source_target_pairs={{0,6},{1,7},{2,0},{3,1},{4,2},{5,3},{6,4},{7,5},{8,14},{9,15},{10,... | collective-permute-start | bytes 786440 | tf_op jit(solution)/shard_map/ppermute | solution.py:34
  38.8 9.6 %collective-permute-start.9 = (bf16[8,128,128]{2,1,0:T(8,128)(2,1)S(1)}, bf16[8,128,128]{2,1,0:T(8,128)(2,1)S(1)}, u32[]{:S(2)}, u32[]{:S(2)}) collective-permute-start(bf16[8,128,128]{2,1,0:T(8,128)(2,1)S(1)} %get-tuple-element.41), channel_id=1, source_target_pairs={{0,2},{1,3},{2,4},{3,5},{4,6},{5,7},{6,0},{7,1},{8,10},{9,11},{10,... | collective-permute-start | bytes 786440 | tf_op jit(solution)/shard_map/ppermute | solution.py:34
  46.2 19.9 %collective-permute-start.12 = (bf16[2,8,128,128]{3,2,1,0:T(8,128)(2,1)S(1)}, bf16[2,8,128,128]{3,2,1,0:T(8,128)(2,1)S(1)}, u32[]{:S(2)}, u32[]{:S(2)}) collective-permute-start(bf16[2,8,128,128]{3,2,1,0:T(8,128)(2,1)S(1)} %with_arrived.3.refs_9_), channel_id=1, source_target_pairs={{0,6},{1,7},{2,0},{3,1},{4,2},{5,3},{6,4},{7,5},{8,14},{9,15},{10,... | collective-permute-start | bytes 1572872 | tf_op jit(solution)/shard_map/ppermute | solution.py:34
  48.4 17.7 %collective-permute-start.11 = (bf16[2,8,128,128]{3,2,1,0:T(8,128)(2,1)S(1)}, bf16[2,8,128,128]{3,2,1,0:T(8,128)(2,1)S(1)}, u32[]{:S(2)}, u32[]{:S(2)}) collective-permute-start(bf16[2,8,128,128]{3,2,1,0:T(8,128)(2,1)S(1)} %with_arrived.2.refs_8_), channel_id=1, source_target_pairs={{0,2},{1,3},{2,4},{3,5},{4,6},{5,7},{6,0},{7,1},{8,10},{9,11},{10,... | collective-permute-start | bytes 1572872 | tf_op jit(solution)/shard_map/ppermute | solution.py:34
